TPU v7x, 32 devices: a whole 2x2x4 slice. The times are simulated.
32 devices in a mesh: dp: 8 (over z, core), fsdp: 4 (over y, x).
Axes of the slice: x: 2, y: 2, z: 4, core: 2. Of those that a mesh axis runs over, the one named last changes fastest.
Arguments:
- activations: bfloat16 [6144, 4096], P(('dp', 'fsdp')), may hold values from -12 to 12
- cotangent: bfloat16 [6144, 512], P(('dp', 'fsdp')), may hold values from -6 to 6
- weight: bfloat16 [4096, 512], P('fsdp'), may hold values from -0.09375 to 0.09375
- momentum: float32 [8, 4096, 512], P('dp', 'fsdp'), may hold values from -256 to 256
- positions: int32 [16, 32, 512], P('fsdp'), may hold values from 0 to 255, as said below
Outputs:
- grad_input: bfloat16 [6144, 4096], P(('dp', 'fsdp'))
- new_momentum: float32 [8, 4096, 512], P('dp', 'fsdp')
- update: bfloat16 [4096, 512], P('fsdp')
Inputs may be any that keep to these rules, and one draw needn't show every extreme that they name: For each block b and column c the 32 values positions[b, :, c] are distinct.
All inputs are finite; a program needn't handle non-finite values.
Results may differ from a plain program's by a relative error of at most 0.023.
Values may be sent and summed in bfloat16 or wider, within the bound.
No kernel may reach another device: no remote copies, remote signals or barrier semaphores. Data moves between devices by JAX's collectives and lax.ppermute only.
A program may use at most 64 MiB of HBM per device.

v0:
```python
import math

import jax
import jax.numpy as jnp
from jax import lax
from jax.sharding import PartitionSpec as P

SPAN = 256


MOMENTUM_DECAY = 0.999


def transform_table(length):
    freq = jnp.arange(length, dtype=jnp.float32)[:, None]
    place = jnp.arange(length, dtype=jnp.float32)[None, :]
    angles = jnp.pi * (2.0 * place + 1.0) * freq / (2.0 * length)
    scales = jnp.where(freq == 0.0, jnp.sqrt(1.0 / length), jnp.sqrt(2.0 / length))
    return scales * jnp.cos(angles)


def forward_blocks(table, blocks):
    return jnp.einsum("kn,bnc->bkc", table, blocks, precision=lax.Precision.HIGHEST)


def inverse_blocks(table, coeffs):
    return jnp.einsum("kn,bkc->bnc", table, coeffs, precision=lax.Precision.HIGHEST)


def grouped_positions(positions):
    blocks, picks, columns = positions.shape
    group = math.gcd(picks, 8)
    stacked = positions.reshape(blocks, picks // group, group, columns)
    return (jnp.transpose(stacked, (1, 0, 2, 3)), group)


def pick_band(coeffs, positions):
    blocks, length, columns = coeffs.shape
    picks = positions.shape[1]
    stacked, group = grouped_positions(positions)
    levels = jnp.arange(length, dtype=jnp.int32)[None, None, :, None]

    def one_group(where):
        onehot = where[:, :, None, :] == levels
        return jnp.sum(jnp.where(onehot, coeffs[:, None, :, :], 0.0), axis=2)

    found = lax.map(one_group, stacked)
    return jnp.transpose(found, (1, 0, 2, 3)).reshape(blocks, picks, columns)


def place_band(values, positions, length):
    blocks, picks, columns = values.shape
    stacked, group = grouped_positions(positions)
    stacked_values = jnp.transpose(
        values.reshape(blocks, picks // group, group, columns), (1, 0, 2, 3)
    )
    levels = jnp.arange(length, dtype=jnp.int32)[None, None, :, None]

    def add_group(dense, packed):
        where, amounts = packed
        onehot = where[:, :, None, :] == levels
        return (dense + jnp.sum(jnp.where(onehot, amounts[:, :, None, :], 0.0), axis=1), None)

    start = jnp.zeros((blocks, length, columns), jnp.float32)
    dense, unused = lax.scan(add_group, start, (stacked, stacked_values))
    return dense


def contract_last(left, right):
    return lax.dot_general(
        left, right, (((1,), (1,)), ((), ())), preferred_element_type=jnp.float32
    )


def on_device(activations, cotangent, weight, momentum, positions):
    table = transform_table(SPAN)
    grad_input = contract_last(
        cotangent, lax.all_gather(weight, "fsdp", axis=0, tiled=True)
    ).astype(jnp.bfloat16)
    gradient = lax.psum_scatter(
        lax.dot_general(
            activations, cotangent, (((0,), (0,)), ((), ())), preferred_element_type=jnp.float32
        ).astype(jnp.bfloat16),
        "fsdp",
        scatter_dimension=0,
        tiled=True,
    ).astype(jnp.float32)
    moment = MOMENTUM_DECAY * momentum[0] + gradient
    blocks = moment.reshape(positions.shape[0], SPAN, moment.shape[1])
    coeffs = forward_blocks(table, blocks)
    picked = pick_band(coeffs, positions)
    kept = blocks - inverse_blocks(table, place_band(picked, positions, SPAN))
    new_momentum = kept.reshape(moment.shape)[None]
    bands = picked.astype(jnp.bfloat16)
    replicas = lax.axis_size("dp")
    summed = jnp.sum(
        lax.all_gather(bands[None], "dp", axis=0, tiled=True).astype(jnp.float32), axis=0
    )
    mean_band = summed / replicas
    update = (
        inverse_blocks(table, place_band(mean_band, positions, SPAN))
        .reshape(moment.shape)
        .astype(jnp.bfloat16)
    )
    return (grad_input, new_momentum, update)


def solution(mesh):
    placed = (
        P(("dp", "fsdp"), None),
        P(("dp", "fsdp"), None),
        P("fsdp", None),
        P("dp", "fsdp", None),
        P("fsdp", None, None),
    )
    return jax.shard_map(
        on_device,
        mesh=mesh,
        in_specs=placed,
        out_specs=(P(("dp", "fsdp"), None), P("dp", "fsdp", None), P("fsdp", None)),
        check_vma=False,
    )
```

profile of v0, /device:TPU:0, one launch (start us, length us, event | category | flops | bytes accessed | tf_op | source)
XLA Modules:
  0.0 235.0 jit_solution(12260437047894337918)
XLA Ops:
  7.2 0.0 copy-start
  7.2 0.0 all-gather.3.cloned.1.call-start
  7.2 0.7 all-gather.3.cloned.1.call-update
  7.9 0.0 reduce-scatter.2.cloned.1.call-start
  8.0 0.6 copy-done
  8.6 4.2 %convolution_convert_fusion = bf16[4096,512]{1,0:T(8,128)(2,1)} fusion(bf16[192,4096]{1,0:T(8,128)(2,1)S(1)} %copy-done, bf16[192,512]{1,0:T(8,128)(2,1)} %param.12), kind=kOutput, calls=%fused_computation.17 | convolution fusion | flops 807403520 | bytes 5963776 | tf_op jit(solution)/shard_map/dot_general | solution.py:81
  12.8 0.0 copy-start.3
  12.8 0.0 copy-start.2
  12.8 0.0 reduce-scatter.2.cloned.1.call-update
  12.8 0.0 all-gather.5.cloned.1.call-start
  12.9 0.8 copy-done.3
  13.8 51.5 %all-gather.3.cloned.1.call-done = bf16[4096,512]{1,0:T(8,128)(2,1)} async-done(((bf16[1024,512]{1,0:T(8,128)(2,1)}), bf16[4096,512]{1,0:T(8,128)(2,1)}) %all-gather.3.cloned.1.call-update) | async-done | bytes 4194320 | tf_op jit(solution)/shard_map/all_gather | solution.py:78
  65.3 0.0 copy-done.2
  65.3 4.8 %convolution_convert_fusion.1 = bf16[192,4096]{1,0:T(8,128)(2,1)} fusion(bf16[192,512]{1,0:T(8,128)(2,1)S(1)} %copy-done.2, bf16[4096,512]{1,0:T(8,128)(2,1)} %all-gather.3.cloned.1.call-done), kind=kOutput, calls=%fused_computation.18 | convolution fusion | flops 806092800 | bytes 5963776 | tf_op jit(solution)/shard_map/dot_general | solution.py:70
  70.1 50.9 %reduce-scatter.2.cloned.1.call-done = bf16[1024,512]{1,0:T(8,128)(2,1)} async-done(((bf16[4096,512]{1,0:T(8,128)(2,1)}), bf16[1024,512]{1,0:T(8,128)(2,1)}) %reduce-scatter.2.cloned.1.call-update) | async-done | bytes 1048592 | tf_op jit(solution)/shard_map/reduce_scatter | solution.py:80
  121.0 2.2 bitcast_add_fusion
  123.3 0.0 copy-start.1
  123.3 1.3 copy-done.1
  124.6 5.7 %convolution_bitcast_fusion = f32[4,256,512]{1,2,0:T(8,128)} fusion(f32[4,256,512]{2,1,0:T(8,128)S(1)} %bitcast.64, f32[256]{0:T(256)S(1)} %get-tuple-element.196, f32[256]{0:T(256)S(1)} %get-tuple-element.195), kind=kOutput, calls=%fused_computation.22 | convolution fusion | flops 1610809344 | bytes 4196352 | tf_op jit(solution)/shard_map/kn,bnc->bkc/dot_general | solution.py:23
  130.3 2.9 %copy.30 = f32[4,256,512]{2,1,0:T(8,128)} copy(f32[4,256,512]{1,2,0:T(8,128)} %convolution_bitcast_fusion) | data formatting | bytes 4194304
  133.2 17.4 %while.33 = (s32[]{:T(128)}, f32[4,4,8,512]{3,2,1,0:T(8,128)S(1)}, s32[4,4,8,512]{3,2,1,0:T(8,128)S(1)}, f32[4,256,512]{2,1,0:T(8,128)}, s32[]{:T(128)}) while((s32[]{:T(128)}, f32[4,4,8,512]{3,2,1,0:T(8,128)S(1)}, s32[4,4,8,512]{3,2,1,0:T(8,128)S(1)}, f32[4,256,512]{2,1,0:T(8,128)}, s32[]{:T(128)}) %tuple.70), condition=%wide.region_3.4_spmd.clone, body=%wide.region_1.3_spmd.clone.sunk | while | flops 12566530 | bytes 2490437 | solution.py:47
  133.2 4.3 %select_reduce_fusion.6 = f32[4,8,512]{2,1,0:T(8,128)S(1)} fusion(f32[4,256,512]{2,1,0:T(8,128)} %get-tuple-element.285, s32[4,8,512]{2,1,0:T(8,128)S(1)} %dynamic-slice_bitcast_fusion.10), kind=kLoop, calls=%fused_computation.4.clone.1 | loop fusion | flops 12566528 | bytes 2228224 | tf_op jit(solution)/shard_map/while/body/eval_jaxpr/reduce_sum | solution.py:45
  137.6 4.3 %select_reduce_fusion.6 = f32[4,8,512]{2,1,0:T(8,128)S(1)} fusion(f32[4,256,512]{2,1,0:T(8,128)} %get-tuple-element.285, s32[4,8,512]{2,1,0:T(8,128)S(1)} %dynamic-slice_bitcast_fusion.10), kind=kLoop, calls=%fused_computation.4.clone.1 | loop fusion | flops 12566528 | bytes 2228224 | tf_op jit(solution)/shard_map/while/body/eval_jaxpr/reduce_sum | solution.py:45
  142.0 4.3 %select_reduce_fusion.6 = f32[4,8,512]{2,1,0:T(8,128)S(1)} fusion(f32[4,256,512]{2,1,0:T(8,128)} %get-tuple-element.285, s32[4,8,512]{2,1,0:T(8,128)S(1)} %dynamic-slice_bitcast_fusion.10), kind=kLoop, calls=%fused_computation.4.clone.1 | loop fusion | flops 12566528 | bytes 2228224 | tf_op jit(solution)/shard_map/while/body/eval_jaxpr/reduce_sum | solution.py:45
  146.4 4.3 %select_reduce_fusion.6 = f32[4,8,512]{2,1,0:T(8,128)S(1)} fusion(f32[4,256,512]{2,1,0:T(8,128)} %get-tuple-element.285, s32[4,8,512]{2,1,0:T(8,128)S(1)} %dynamic-slice_bitcast_fusion.10), kind=kLoop, calls=%fused_computation.4.clone.1 | loop fusion | flops 12566528 | bytes 2228224 | tf_op jit(solution)/shard_map/while/body/eval_jaxpr/reduce_sum | solution.py:45
  150.7 0.7 copy.42
  151.4 0.0 all-gather.5.cloned.1.call-update
  151.4 31.4 %while.34 = (s32[]{:T(128)}, f32[4,256,512]{2,1,0:T(8,128)}, s32[4,4,8,512]{3,2,1,0:T(8,128)S(1)}, f32[4,4,8,512]{3,2,1,0:T(8,128)S(1)}, s32[]{:T(128)}, /*index=5*/s32[]{:T(128)}) while((s32[]{:T(128)}, f32[4,256,512]{2,1,0:T(8,128)}, s32[4,4,8,512]{3,2,1,0:T(8,128)S(1)}, f32[4,4,8,512]{3,2,1,0:T(8,128)S(1)}, s32[]{:T(128)}, ...), condition=%wide.region_6.7_spmd.clone, body=%wide.region_4.6_spmd.clone.sunk | while | flops 13107203 | bytes 8781911 | solution.py:65
  151.4 3.9 %select_reduce_fusion.7 = f32[4,256,512]{2,1,0:T(8,128)} fusion(f32[4,8,512]{2,1,0:T(8,128)S(1)} %dynamic-slice_bitcast_fusion.11, s32[4,8,512]{2,1,0:T(8,128)S(1)} %dynamic-slice_bitcast_fusion.12), kind=kLoop, calls=%fused_computation.8.clone.1 | loop fusion | flops 12058624 | bytes 2228224 | tf_op jit(solution)/shard_map/while/body/eval_jaxpr/reduce_sum | solution.py:62
  155.4 3.4 %select_add_fusion.4 = f32[4,256,512]{2,1,0:T(8,128)} fusion(f32[4,256,512]{2,1,0:T(8,128)} %select_reduce_fusion.7, f32[4,256,512]{2,1,0:T(8,128)} %get-tuple-element.294, pred[]{:T(512)S(6)} %compare.6), kind=kLoop, calls=%fused_computation.9.clone.1 | loop fusion | flops 1048576 | bytes 6291457 | tf_op jit(solution)/shard_map/while/body/eval_jaxpr/add | solution.py:62
  158.8 3.9 %select_reduce_fusion.7 = f32[4,256,512]{2,1,0:T(8,128)} fusion(f32[4,8,512]{2,1,0:T(8,128)S(1)} %dynamic-slice_bitcast_fusion.11, s32[4,8,512]{2,1,0:T(8,128)S(1)} %dynamic-slice_bitcast_fusion.12), kind=kLoop, calls=%fused_computation.8.clone.1 | loop fusion | flops 12058624 | bytes 2228224 | tf_op jit(solution)/shard_map/while/body/eval_jaxpr/reduce_sum | solution.py:62
  162.7 4.0 %select_add_fusion.4 = f32[4,256,512]{2,1,0:T(8,128)} fusion(f32[4,256,512]{2,1,0:T(8,128)} %select_reduce_fusion.7, f32[4,256,512]{2,1,0:T(8,128)} %get-tuple-element.294, pred[]{:T(512)S(6)} %compare.6), kind=kLoop, calls=%fused_computation.9.clone.1 | loop fusion | flops 1048576 | bytes 6291457 | tf_op jit(solution)/shard_map/while/body/eval_jaxpr/add | solution.py:62
  166.8 3.9 %select_reduce_fusion.7 = f32[4,256,512]{2,1,0:T(8,128)} fusion(f32[4,8,512]{2,1,0:T(8,128)S(1)} %dynamic-slice_bitcast_fusion.11, s32[4,8,512]{2,1,0:T(8,128)S(1)} %dynamic-slice_bitcast_fusion.12), kind=kLoop, calls=%fused_computation.8.clone.1 | loop fusion | flops 12058624 | bytes 2228224 | tf_op jit(solution)/shard_map/while/body/eval_jaxpr/reduce_sum | solution.py:62
  170.7 4.0 %select_add_fusion.4 = f32[4,256,512]{2,1,0:T(8,128)} fusion(f32[4,256,512]{2,1,0:T(8,128)} %select_reduce_fusion.7, f32[4,256,512]{2,1,0:T(8,128)} %get-tuple-element.294, pred[]{:T(512)S(6)} %compare.6), kind=kLoop, calls=%fused_computation.9.clone.1 | loop fusion | flops 1048576 | bytes 6291457 | tf_op jit(solution)/shard_map/while/body/eval_jaxpr/add | solution.py:62
  174.8 3.9 %select_reduce_fusion.7 = f32[4,256,512]{2,1,0:T(8,128)} fusion(f32[4,8,512]{2,1,0:T(8,128)S(1)} %dynamic-slice_bitcast_fusion.11, s32[4,8,512]{2,1,0:T(8,128)S(1)} %dynamic-slice_bitcast_fusion.12), kind=kLoop, calls=%fused_computation.8.clone.1 | loop fusion | flops 12058624 | bytes 2228224 | tf_op jit(solution)/shard_map/while/body/eval_jaxpr/reduce_sum | solution.py:62
  178.7 4.0 %select_add_fusion.4 = f32[4,256,512]{2,1,0:T(8,128)} fusion(f32[4,256,512]{2,1,0:T(8,128)} %select_reduce_fusion.7, f32[4,256,512]{2,1,0:T(8,128)} %get-tuple-element.294, pred[]{:T(512)S(6)} %compare.6), kind=kLoop, calls=%fused_computation.9.clone.1 | loop fusion | flops 1048576 | bytes 6291457 | tf_op jit(solution)/shard_map/while/body/eval_jaxpr/add | solution.py:62
  182.8 6.9 %bitcast_subtract_fusion = f32[4,256,512]{2,1,0:T(8,128)} fusion(f32[4,256,512]{2,1,0:T(8,128)} %bitcast.65, f32[4,256,512]{2,1,0:T(8,128)} %get-tuple-element.85, f32[256]{0:T(256)S(1)} %get-tuple-element.196, f32[256]{0:T(256)S(1)} %get-tuple-element.195), kind=kOutput, calls=%fused_computation.19 | convolution fusion | flops 1611333632 | bytes 6293504 | tf_op jit(solution)/shard_map/kn,bkc->bnc/dot_general | solution.py:27
  189.6 0.0 all-gather.5.cloned.1.call-done
  189.6 1.4 convert_reduce_fusion
  191.1 31.8 %while.35 = (s32[]{:T(128)}, f32[4,256,512]{2,1,0:T(8,128)}, s32[4,4,8,512]{3,2,1,0:T(8,128)S(1)}, f32[4,4,8,512]{3,2,0,1:T(8,128)S(1)}, s32[]{:T(128)}, /*index=5*/s32[]{:T(128)}) while((s32[]{:T(128)}, f32[4,256,512]{2,1,0:T(8,128)}, s32[4,4,8,512]{3,2,1,0:T(8,128)S(1)}, f32[4,4,8,512]{3,2,0,1:T(8,128)S(1)}, s32[]{:T(128)}, ...), condition=%wide.region_10.11_spmd.clone, body=%wide.region_8.10_spmd.clone.sunk | while | flops 13107203 | bytes 8781911 | solution.py:65
  191.3 3.9 %select_reduce_fusion.8 = f32[4,256,512]{2,1,0:T(8,128)} fusion(f32[4,8,512]{2,1,0:T(8,128)S(1)} %dynamic-slice_bitcast_fusion.13, s32[4,8,512]{2,1,0:T(8,128)S(1)} %dynamic-slice_bitcast_fusion.14), kind=kLoop, calls=%fused_computation.13.clone.1 | loop fusion | flops 12058624 | bytes 2228224 | tf_op jit(solution)/shard_map/while/body/eval_jaxpr/reduce_sum | solution.py:62
  195.3 3.5 %select_add_fusion.5 = f32[4,256,512]{2,1,0:T(8,128)} fusion(f32[4,256,512]{2,1,0:T(8,128)} %select_reduce_fusion.8, f32[4,256,512]{2,1,0:T(8,128)} %get-tuple-element.312, pred[]{:T(512)S(6)} %compare.7), kind=kLoop, calls=%fused_computation.14.clone.1 | loop fusion | flops 1048576 | bytes 6291457 | tf_op jit(solution)/shard_map/while/body/eval_jaxpr/add | solution.py:62
  198.8 3.9 %select_reduce_fusion.8 = f32[4,256,512]{2,1,0:T(8,128)} fusion(f32[4,8,512]{2,1,0:T(8,128)S(1)} %dynamic-slice_bitcast_fusion.13, s32[4,8,512]{2,1,0:T(8,128)S(1)} %dynamic-slice_bitcast_fusion.14), kind=kLoop, calls=%fused_computation.13.clone.1 | loop fusion | flops 12058624 | bytes 2228224 | tf_op jit(solution)/shard_map/while/body/eval_jaxpr/reduce_sum | solution.py:62
  202.7 4.1 %select_add_fusion.5 = f32[4,256,512]{2,1,0:T(8,128)} fusion(f32[4,256,512]{2,1,0:T(8,128)} %select_reduce_fusion.8, f32[4,256,512]{2,1,0:T(8,128)} %get-tuple-element.312, pred[]{:T(512)S(6)} %compare.7), kind=kLoop, calls=%fused_computation.14.clone.1 | loop fusion | flops 1048576 | bytes 6291457 | tf_op jit(solution)/shard_map/while/body/eval_jaxpr/add | solution.py:62
  206.8 3.9 %select_reduce_fusion.8 = f32[4,256,512]{2,1,0:T(8,128)} fusion(f32[4,8,512]{2,1,0:T(8,128)S(1)} %dynamic-slice_bitcast_fusion.13, s32[4,8,512]{2,1,0:T(8,128)S(1)} %dynamic-slice_bitcast_fusion.14), kind=kLoop, calls=%fused_computation.13.clone.1 | loop fusion | flops 12058624 | bytes 2228224 | tf_op jit(solution)/shard_map/while/body/eval_jaxpr/reduce_sum | solution.py:62
  210.8 4.1 %select_add_fusion.5 = f32[4,256,512]{2,1,0:T(8,128)} fusion(f32[4,256,512]{2,1,0:T(8,128)} %select_reduce_fusion.8, f32[4,256,512]{2,1,0:T(8,128)} %get-tuple-element.312, pred[]{:T(512)S(6)} %compare.7), kind=kLoop, calls=%fused_computation.14.clone.1 | loop fusion | flops 1048576 | bytes 6291457 | tf_op jit(solution)/shard_map/while/body/eval_jaxpr/add | solution.py:62
  214.9 3.9 %select_reduce_fusion.8 = f32[4,256,512]{2,1,0:T(8,128)} fusion(f32[4,8,512]{2,1,0:T(8,128)S(1)} %dynamic-slice_bitcast_fusion.13, s32[4,8,512]{2,1,0:T(8,128)S(1)} %dynamic-slice_bitcast_fusion.14), kind=kLoop, calls=%fused_computation.13.clone.1 | loop fusion | flops 12058624 | bytes 2228224 | tf_op jit(solution)/shard_map/while/body/eval_jaxpr/reduce_sum | solution.py:62
  218.8 4.1 %select_add_fusion.5 = f32[4,256,512]{2,1,0:T(8,128)} fusion(f32[4,256,512]{2,1,0:T(8,128)} %select_reduce_fusion.8, f32[4,256,512]{2,1,0:T(8,128)} %get-tuple-element.312, pred[]{:T(512)S(6)} %compare.7), kind=kLoop, calls=%fused_computation.14.clone.1 | loop fusion | flops 1048576 | bytes 6291457 | tf_op jit(solution)/shard_map/while/body/eval_jaxpr/add | solution.py:62
  222.9 5.5 %convolution_convert_fusion.2 = bf16[4,512,256]{1,2,0:T(8,128)(2,1)} fusion(f32[4,256,512]{2,1,0:T(8,128)} %get-tuple-element.86, f32[256]{0:T(256)S(1)} %get-tuple-element.196, f32[256]{0:T(256)S(1)} %get-tuple-element.195), kind=kOutput, calls=%fused_computation.23 | convolution fusion | flops 1611333632 | bytes 3147776 | tf_op jit(solution)/shard_map/kn,bkc->bnc/dot_general | solution.py:27
  (30 shorter events, 0.3 us)
Async XLA Ops:
  7.2 1.4 copy-start
  7.2 58.1 %all-gather.3.cloned.1.call-start = ((), (), s32[]{:S(2)}) async-start(), calls=%async_computation.1 | async-start | bytes 5242880 | tf_op jit(solution)/shard_map/all_gather | solution.py:78
  7.9 113.1 %reduce-scatter.2.cloned.1.call-start = ((), (), s32[]{:S(2)}) async-start(), calls=%async_computation.2 | async-start | bytes 5242880 | tf_op jit(solution)/shard_map/reduce_scatter | solution.py:80
  12.8 0.9 copy-start.3
  12.8 52.5 %copy-start.2 = (bf16[192,512]{1,0:T(8,128)(2,1)S(1)}, bf16[192,512]{1,0:T(8,128)(2,1)}, u32[]{:S(2)}) copy-start(bf16[192,512]{1,0:T(8,128)(2,1)} %param.12) | copy-start | bytes 589828
  12.8 176.8 %all-gather.5.cloned.1.call-start = ((), (), s32[]{:S(2)}) async-start(), calls=%async_computation.3 | async-start | bytes 1179648 | tf_op jit(solution)/shard_map/all_gather | solution.py:97
  123.3 1.3 copy-start.1
Sparse Core Ops, SparseCore 0:
  9.9 55.3 all-gather.2
  68.3 52.6 reduce-scatter.1
  151.5 22.0 all-gather.4
where the time goes:
time: 236 us; the launch traced here: 235 us
  waiting for transfers between devices  103 us (44%)
  other arithmetic  83.7 us (35%)
  matrix products  27.2 us (12%)
  between operations  13.8 us (6%)
  local copies, waits for them, and re-layouts  6.61 us (3%)
    all_gather x1, waiting for transfers between devices, on_device(): lax.all_gather(weight, 'fsdp', axis=0, tiled=True)  51.5 us
    reduce_scatter x1, waiting for transfers between devices, on_device(): lax.psum_scatter(lax.dot_general(activations, cotangent, (((0,), (0,)), (...  50.9 us
    reduce_sum x8, other arithmetic, add_group(): jnp.sum(jnp.where(onehot, amounts[:, :, None, :], 0.0), axis=1)  31.6 us
    add x8, other arithmetic, add_group(): dense + jnp.sum(jnp.where(onehot, amounts[:, :, None, :], 0.0), axis=1)  31.2 us
    reduce_sum x4, other arithmetic, one_group(): return jnp.sum(jnp.where(onehot, coeffs[:, None, :, :], 0.0), axis=2)  17.2 us
    dot_general x2, matrix products, inverse_blocks(): jnp.einsum('kn,bkc->bnc', table, coeffs, precision=lax.Precision.HIGHEST)  12.4 us
    unnamed x10, local copies, waits for them, and re-layouts  5.73 us
    dot_general x1, matrix products, forward_blocks(): jnp.einsum('kn,bnc->bkc', table, blocks, precision=lax.Precision.HIGHEST)  5.73 us
  transfers between devices with their start and end apart: 3, of which 2 were waited for; matrix products, arithmetic and copies ran while one was open for 20% of the time, Pallas kernels for 0%

commit v1 on v0

v1 whole, which is shorter than its diff:
```python
import functools

import jax
import jax.numpy as jnp
import numpy as np
from jax import lax
from jax.experimental import pallas as pl
from jax.experimental.pallas import tpu as pltpu
from jax.sharding import PartitionSpec as P

SPAN = 256
MOMENTUM_DECAY = 0.999
LANES = 128
SUBLANES = 8
VMEM_LIMIT = 48 * 1024 * 1024


def transform_table():
    freq = np.arange(SPAN, dtype=np.float64)[:, None]
    place = np.arange(SPAN, dtype=np.float64)[None, :]
    scales = np.where(freq == 0.0, np.sqrt(1.0 / SPAN), np.sqrt(2.0 / SPAN))
    table = scales * np.cos(np.pi * (2.0 * place + 1.0) * freq / (2.0 * SPAN))
    high = table.astype(jnp.bfloat16)
    low = (table - high.astype(np.float64)).astype(jnp.bfloat16)
    return high, low


def two_terms(x):
    high = x.astype(jnp.bfloat16)
    return high, (x - high.astype(jnp.float32)).astype(jnp.bfloat16)


def dot(left, right):
    return jnp.dot(left, right, preferred_element_type=jnp.float32)


def split_dot(table_high, table_low, x):
    high, low = two_terms(x)
    return dot(table_high, high) + (dot(table_high, low) + dot(table_low, high))


def params(**more):
    return pltpu.CompilerParams(vmem_limit_bytes=VMEM_LIMIT, **more)


def inverse_index_kernel(positions_ref, inverse_ref):
    picks, columns = positions_ref.shape[1:]
    chunk = 64

    def one_chunk(at, carry):
        start = pl.multiple_of(at * chunk, chunk)
        for c in range(0, columns, LANES):
            where = positions_ref[0, :, c : c + LANES]
            level = lax.broadcasted_iota(jnp.int32, (chunk, LANES), 0) + start
            found = jnp.full((chunk, LANES), -1, jnp.int32)
            for i in range(picks):
                found = jnp.where(where[i : i + 1, :] == level, i, found)
            inverse_ref[0, pl.ds(start, chunk), c : c + LANES] = found
        return carry

    lax.fori_loop(0, SPAN // chunk, one_chunk, 0)


def inverse_index(positions):
    blocks, picks, columns = positions.shape
    return pl.pallas_call(
        inverse_index_kernel,
        out_shape=jax.ShapeDtypeStruct((blocks, SPAN, columns), jnp.int32),
        grid=(blocks,),
        in_specs=[pl.BlockSpec((1, picks, columns), lambda b: (b, 0, 0))],
        out_specs=pl.BlockSpec((1, SPAN, columns), lambda b: (b, 0, 0)),
        compiler_params=params(),
        cost_estimate=pl.CostEstimate(
            flops=2 * blocks * picks * SPAN * columns,
            bytes_accessed=4 * blocks * SPAN * columns,
            transcendentals=0,
        ),
        name="inverse_index",
    )(positions)


def outer_kernel(groups, *refs):
    weight_ref = refs[groups]
    for s in range(groups):
        refs[groups + 1 + s][...] = lax.dot_general(
            refs[s][...],
            weight_ref[...],
            (((1,), (1,)), ((), ())),
            preferred_element_type=jnp.float32,
        ).astype(jnp.bfloat16)


def input_gradients(cotangents, weight):
    tokens, outputs = cotangents[0].shape
    rows = weight.shape[0]
    groups = len(cotangents)
    return pl.pallas_call(
        functools.partial(outer_kernel, groups),
        out_shape=[jax.ShapeDtypeStruct((tokens, rows), jnp.bfloat16)] * groups,
        compiler_params=params(),
        cost_estimate=pl.CostEstimate(
            flops=2 * groups * tokens * rows * outputs,
            bytes_accessed=2 * (groups * tokens * (rows + outputs) + rows * outputs),
            transcendentals=0,
        ),
        name="input_gradients",
    )(*cotangents, weight)


def moment_kernel(groups, place_ref, *refs):
    inputs, cotangents = refs[:groups], refs[groups : 2 * groups]
    momentum_ref, positions_ref, inverse_ref, high_ref, low_ref = refs[2 * groups : 2 * groups + 5]
    moment_ref, masked_ref, mine_ref, theirs_ref, coeffs_ref = refs[2 * groups + 5 :]
    picks, columns = positions_ref.shape[1:]
    gradient = None
    for s in range(groups):
        term = lax.dot_general(
            inputs[s][...],
            cotangents[s][...],
            (((0,), (0,)), ((), ())),
            preferred_element_type=jnp.float32,
        )
        gradient = term if gradient is None else gradient + term
    moment = MOMENTUM_DECAY * momentum_ref[0] + gradient
    moment_ref[...] = moment
    coeffs = split_dot(high_ref[...], low_ref[...], moment)
    coeffs_ref[...] = coeffs
    masked_ref[...] = jnp.where(inverse_ref[0] >= 0, coeffs, 0.0).astype(jnp.bfloat16)
    half = picks // 2
    parts = []
    for c in range(0, columns, LANES):
        found = []
        for p in range(0, picks, SUBLANES):
            where = positions_ref[0, p : p + SUBLANES, c : c + LANES]
            inside, group = where & (SUBLANES - 1), where // SUBLANES
            total = jnp.zeros((SUBLANES, LANES), jnp.float32)
            for g in range(SPAN // SUBLANES):
                rows = coeffs_ref[g * SUBLANES : (g + 1) * SUBLANES, c : c + LANES]
                total = jnp.where(
                    group == g, jnp.take_along_axis(rows, inside, axis=0), total
                )
            found.append(total)
        parts.append(jnp.concatenate(found, axis=0).astype(jnp.bfloat16))
    bands = jnp.concatenate(parts, axis=1)
    second = place_ref[1] == 1
    mine_ref[0] = jnp.where(second, bands[half:], bands[:half])
    theirs_ref[0] = jnp.where(second, bands[:half], bands[half:])


def moments(place, own_inputs, inputs, cotangents, momentum, positions, inverse, high, low):
    groups = len(cotangents)
    tokens, columns = cotangents[0].shape
    blocks, picks, _ = positions.shape
    whole = lambda b, place: (0, 0)
    half_shape = jax.ShapeDtypeStruct((blocks, picks // 2, columns), jnp.bfloat16)
    by_block = lambda b, place: (b, 0, 0)
    return pl.pallas_call(
        functools.partial(moment_kernel, groups),
        out_shape=[
            jax.ShapeDtypeStruct((blocks * SPAN, columns), jnp.float32),
            jax.ShapeDtypeStruct((blocks * SPAN, columns), jnp.bfloat16),
            half_shape,
            half_shape,
        ],
        grid_spec=pltpu.PrefetchScalarGridSpec(
            num_scalar_prefetch=1,
            grid=(blocks,),
            in_specs=[pl.BlockSpec((tokens, SPAN), lambda b, place: (0, place[0] * blocks + b))]
            + [pl.BlockSpec((tokens, SPAN), lambda b, place: (0, b))] * (groups - 1)
            + [pl.BlockSpec((tokens, columns), whole)] * groups
            + [
                pl.BlockSpec((1, SPAN, columns), lambda b, place: (0, b, 0)),
                pl.BlockSpec((1, picks, columns), by_block),
                pl.BlockSpec((1, SPAN, columns), by_block),
                pl.BlockSpec((SPAN, SPAN), whole),
                pl.BlockSpec((SPAN, SPAN), whole),
            ],
            out_specs=[
                pl.BlockSpec((SPAN, columns), lambda b, place: (b, 0)),
                pl.BlockSpec((SPAN, columns), lambda b, place: (b, 0)),
                pl.BlockSpec((1, picks // 2, columns), by_block),
                pl.BlockSpec((1, picks // 2, columns), by_block),
            ],
            scratch_shapes=[pltpu.VMEM((SPAN, columns), jnp.float32)],
        ),
        compiler_params=params(),
        cost_estimate=pl.CostEstimate(
            flops=2 * blocks * SPAN * columns * (groups * tokens + 3 * SPAN),
            bytes_accessed=blocks * SPAN * (groups * tokens * 2 + 14 * columns),
            transcendentals=0,
        ),
        name="moment",
    )(place, own_inputs, *inputs, *cotangents, momentum, positions, inverse, high, low)


def feedback_kernel(moment_ref, masked_ref, high_ref, low_ref, kept_ref):
    sent = dot(high_ref[...], masked_ref[...]) + dot(low_ref[...], masked_ref[...])
    kept_ref[0] = moment_ref[...] - sent


def feedback(moment, masked, high, low):
    rows, columns = moment.shape
    whole = lambda b: (0, 0)
    return pl.pallas_call(
        feedback_kernel,
        out_shape=jax.ShapeDtypeStruct((1, rows, columns), jnp.float32),
        grid=(rows // SPAN,),
        in_specs=[
            pl.BlockSpec((SPAN, columns), lambda b: (b, 0)),
            pl.BlockSpec((SPAN, columns), lambda b: (b, 0)),
            pl.BlockSpec((SPAN, SPAN), whole),
            pl.BlockSpec((SPAN, SPAN), whole),
        ],
        out_specs=pl.BlockSpec((1, SPAN, columns), lambda b: (0, b, 0)),
        compiler_params=params(),
        cost_estimate=pl.CostEstimate(
            flops=4 * rows * columns * SPAN, bytes_accessed=10 * rows * columns, transcendentals=0
        ),
        name="feedback",
    )(moment, masked, high, low)


def decode_kernel(replicas, place_ref, mine_ref, theirs_ref, inverse_ref, high_ref, low_ref, update_ref, dense_ref):
    columns = mine_ref.shape[2]
    half = mine_ref.shape[1]
    second = place_ref[1] == 1
    mine = mine_ref[0].astype(jnp.float32) * (1.0 / replicas)
    theirs = theirs_ref[0].astype(jnp.float32) * (1.0 / replicas)
    first_half = jnp.where(second, theirs, mine)
    second_half = jnp.where(second, mine, theirs)
    for c in range(0, columns, LANES):
        source = [
            part[p : p + SUBLANES, c : c + LANES]
            for part in (first_half, second_half)
            for p in range(0, half, SUBLANES)
        ]
        for g in range(0, SPAN, SUBLANES):
            pick = inverse_ref[0, g : g + SUBLANES, c : c + LANES]
            inside, group = pick & (SUBLANES - 1), pick >> 3
            total = jnp.zeros((SUBLANES, LANES), jnp.float32)
            for s, rows in enumerate(source):
                total = jnp.where(group == s, jnp.take_along_axis(rows, inside, axis=0), total)
            dense_ref[g : g + SUBLANES, c : c + LANES] = total
    update_ref[...] = split_dot(high_ref[...], low_ref[...], dense_ref[...]).astype(jnp.bfloat16)


def decode(place, mine, theirs, inverse, high, low, replicas):
    blocks, half, columns = mine.shape
    whole = lambda b, place: (0, 0)
    by_block = lambda b, place: (b, 0, 0)
    return pl.pallas_call(
        functools.partial(decode_kernel, replicas),
        out_shape=jax.ShapeDtypeStruct((blocks * SPAN, columns), jnp.bfloat16),
        grid_spec=pltpu.PrefetchScalarGridSpec(
            num_scalar_prefetch=1,
            grid=(blocks,),
            in_specs=[
                pl.BlockSpec((1, half, columns), by_block),
                pl.BlockSpec((1, half, columns), by_block),
                pl.BlockSpec((1, SPAN, columns), by_block),
                pl.BlockSpec((SPAN, SPAN), whole),
                pl.BlockSpec((SPAN, SPAN), whole),
            ],
            out_specs=pl.BlockSpec((SPAN, columns), lambda b, place: (b, 0)),
            scratch_shapes=[pltpu.VMEM((SPAN, columns), jnp.float32)],
        ),
        compiler_params=params(),
        cost_estimate=pl.CostEstimate(
            flops=6 * blocks * SPAN * SPAN * columns,
            bytes_accessed=6 * blocks * SPAN * columns,
            transcendentals=0,
        ),
        name="decode",
    )(place, mine, theirs, inverse, high, low)


def assemble_kernel(groups, place_ref, *refs):
    parts, out_ref, sems = refs[:groups], refs[groups], refs[groups + 1]
    width = parts[0].shape[1]
    copies = []
    for m in range(groups):
        at = pl.multiple_of((place_ref[0] ^ m) * width, width)
        copies.append(pltpu.make_async_copy(parts[m], out_ref.at[:, pl.ds(at, width)], sems.at[m]))
    for copy in copies:
        copy.start()
    for copy in copies:
        copy.wait()


def assemble(place, parts):
    groups = len(parts)
    tokens, width = parts[0].shape
    return pl.pallas_call(
        functools.partial(assemble_kernel, groups),
        out_shape=jax.ShapeDtypeStruct((tokens, groups * width), jnp.bfloat16),
        in_specs=[pl.BlockSpec(memory_space=pltpu.SMEM)] + [pl.BlockSpec(memory_space=pl.ANY)] * groups,
        out_specs=pl.BlockSpec(memory_space=pl.ANY),
        scratch_shapes=[pltpu.SemaphoreType.DMA((groups,))],
        compiler_params=params(),
        cost_estimate=pl.CostEstimate(
            flops=0, bytes_accessed=4 * groups * tokens * width, transcendentals=0
        ),
        name="assemble",
    )(place, *parts)


def swap(x, axis, mask):
    size = lax.axis_size(axis)
    return lax.ppermute(x, axis, [(s, s ^ mask) for s in range(size)])


def sum_over_chips(x):
    replicas = lax.axis_size("dp")
    stride = 2
    total = x
    while stride < replicas:
        sent = total.astype(jnp.bfloat16)
        parts = [sent] + [swap(sent, "dp", stride * m) for m in (1, 2, 3) if stride * m < replicas]
        parts = [part.astype(jnp.float32) for part in parts]
        total = parts[0] + parts[1] if len(parts) == 2 else (parts[0] + parts[1]) + (parts[2] + parts[3])
        stride *= 4
    return total.astype(jnp.bfloat16)


def on_device(activations, cotangent, weight, momentum, positions):
    groups, replicas = lax.axis_size("fsdp"), lax.axis_size("dp")
    rows = weight.shape[0]
    index = lax.axis_index("fsdp")
    place = jnp.stack([index, lax.axis_index("dp") % 2]).astype(jnp.int32)
    high, low = transform_table()

    cotangents = [cotangent] + [swap(cotangent, "fsdp", m) for m in range(1, groups)]
    inputs = [
        swap(lax.dynamic_slice_in_dim(activations, (index ^ m) * rows, rows, 1), "fsdp", m)
        for m in range(1, groups)
    ]
    inverse = inverse_index(positions)
    outer = input_gradients(cotangents, weight)
    grad_input = assemble(
        place, [outer[0]] + [swap(outer[m], "fsdp", m) for m in range(1, groups)]
    )

    moment, masked, mine, theirs = moments(
        place, activations, inputs, cotangents, momentum, positions, inverse, high, low
    )
    chip = mine.astype(jnp.float32) + swap(theirs, "dp", 1).astype(jnp.float32)
    new_momentum = feedback(moment, masked, high.T, low.T)
    summed = sum_over_chips(chip)
    update = decode(place, summed, swap(summed, "dp", 1), inverse, high.T, low.T, replicas)
    return grad_input, new_momentum, update


def solution(mesh):
    placed = (
        P(("dp", "fsdp"), None),
        P(("dp", "fsdp"), None),
        P("fsdp", None),
        P("dp", "fsdp", None),
        P("fsdp", None, None),
    )
    return jax.shard_map(
        on_device,
        mesh=mesh,
        in_specs=placed,
        out_specs=(P(("dp", "fsdp"), None), P("dp", "fsdp", None), P("fsdp", None)),
        check_vma=False,
    )
```

time: 236 us -> 71.4 us (0.30)
  other arithmetic: 83.7 us -> 0.13 us
  waiting for transfers between devices: 103 us -> 25.2 us
  matrix products: 27.2 us -> 0 us
  Pallas kernels: 0 us -> 22.1 us
  starting transfers between devices: 0.12 us -> 19.1 us
  between operations: 13.8 us -> 0.82 us
  local copies, waits for them, and re-layouts: 6.61 us -> 3.78 us
    all_gather x2 -> x0, waiting for transfers between devices: 51.5 us -> none  [the longest x1 51.5 us: on_device(): lax.all_gather(weight, 'fsdp', axis=0, tiled=True)]
    reduce_scatter x1 -> x0, waiting for transfers between devices: 50.9 us -> none  [on_device(): lax.psum_scatter(lax.dot_general(activations, cotangent, (((0,), (0,)), (...]
    reduce_sum x13 -> x0, other arithmetic: 50.2 us -> none  [the longest x8 31.6 us: add_group(): jnp.sum(jnp.where(onehot, amounts[:, :, None, :], 0.0), axis=1)]
    add x9 -> x0, other arithmetic: 33.4 us -> none  [the longest x8 31.2 us: add_group(): dense + jnp.sum(jnp.where(onehot, amounts[:, :, None, :], 0.0), axis=1)]
    dot_general x5 -> x0, matrix products: 27.2 us -> none  [the longest x2 12.4 us: inverse_blocks(): jnp.einsum('kn,bkc->bnc', table, coeffs, precision=lax.Precision.HIGHEST)]
    ppermute x0 -> x14, waiting for transfers between devices: none -> 25.2 us  [swap(): return lax.ppermute(x, axis, [(s, s ^ mask) for s in range(size)])]
    pallas_call x0 -> x6, Pallas kernels: none -> 22.1 us  [the longest x1 6.89 us: moments(): pl.pallas_call(functools.partial(moment_kernel, groups), out_shape=[jax.S...]
    ppermute x0 -> x14, starting transfers between devices: none -> 19.1 us  [swap(): return lax.ppermute(x, axis, [(s, s ^ mask) for s in range(size)])]
  transfers between devices with their start and end apart: 3 -> 14, of which waited for: 2 -> 6; matrix products, arithmetic and copies ran while one was open for 20% -> 0% of each run, Pallas kernels for 0% -> 19%
where the time goes in v1:
time: 71.4 us; the launch traced here: 71.2 us
  waiting for transfers between devices  25.2 us (35%)
  Pallas kernels  22.1 us (31%)
  starting transfers between devices  19.1 us (27%)
  local copies, waits for them, and re-layouts  3.78 us (5%)
  between operations  0.82 us (1%)
    ppermute x14, waiting for transfers between devices, swap(): return lax.ppermute(x, axis, [(s, s ^ mask) for s in range(size)])  25.2 us
    ppermute x14, starting transfers between devices, swap(): return lax.ppermute(x, axis, [(s, s ^ mask) for s in range(size)])  19.1 us
    pallas_call x1, Pallas kernels, moments(): pl.pallas_call(functools.partial(moment_kernel, groups), out_shape=[jax.S...  6.89 us
    pallas_call x1, Pallas kernels, inverse_index(): pl.pallas_call(inverse_index_kernel, out_shape=jax.ShapeDtypeStruct((bloc...  4.51 us
    pallas_call x1, Pallas kernels, decode(): pl.pallas_call(functools.partial(decode_kernel, replicas), out_shape=jax....  3.97 us
    pallas_call x1, Pallas kernels, feedback(): pl.pallas_call(feedback_kernel, out_shape=jax.ShapeDtypeStruct((1, rows,...  2.53 us
    pallas_call x1, Pallas kernels, input_gradients(): pl.pallas_call(functools.partial(outer_kernel, groups), out_shape=[jax.Sh...  2.53 us
    dynamic_slice x1, local copies, waits for them, and re-layouts, on_device(): lax.dynamic_slice_in_dim(activations, (index ^ m) * rows, rows, 1)  2.42 us
  transfers between devices with their start and end apart: 14, of which 6 were waited for; matrix products, arithmetic and copies ran while one was open for 0% of the time, Pallas kernels for 19%

profile of v1, /device:TPU:0, one launch (start us, length us, event | category | flops | bytes accessed | tf_op | source)
XLA Modules:
  0.0 71.2 jit_solution(193354672674132816)
XLA Ops:
  0.6 0.0 copy-start.7
  0.6 0.0 copy-start.4
  0.7 0.0 copy-start.2
  0.7 0.0 copy-start.8
  0.7 2.4 %constant_dynamic-slice_fusion = (bf16[192,1024]{1,0:T(8,128)(2,1)}, bf16[192,1024]{1,0:T(8,128)(2,1)}, bf16[192,1024]{1,0:T(8,128)(2,1)}) fusion(bf16[192,4096]{1,0:T(8,128)(2,1)} %refs_0_.3, s32[]{:T(128)S(6)} %select_n.19, s32[]{:T(128)S(6)} %select_n.18, s32[]{:T(128)S(6)} %select_n.17), kind=kLoop, calls=%fused_computation.2 | loop fusion | bytes 2359308 | tf_op jit(solution)/shard_map/dynamic_slice | solution.py:334
  3.1 2.9 %collective-permute-start.6 = (bf16[192,1024]{1,0:T(8,128)(2,1)}, bf16[192,1024]{1,0:T(8,128)(2,1)S(1)}, u32[]{:S(2)}, u32[]{:S(2)}) collective-permute-start(bf16[192,1024]{1,0:T(8,128)(2,1)} %get-tuple-element.21), channel_id=1, source_target_pairs={{0,1},{1,0},{2,3},{3,2},{4,5},{5,4},{6,7},{7,6},{8,9},{9,8},{10,11... | collective-permute-start | bytes 1179656 | tf_op jit(solution)/shard_map/ppermute | solution.py:309
  6.1 0.0 copy-done.7
  6.1 0.0 collective-permute-start
  6.1 2.0 %collective-permute-start.7 = (bf16[192,1024]{1,0:T(8,128)(2,1)}, bf16[192,1024]{1,0:T(8,128)(2,1)S(1)}, u32[]{:S(2)}, u32[]{:S(2)}) collective-permute-start(bf16[192,1024]{1,0:T(8,128)(2,1)} %get-tuple-element.20), channel_id=1, source_target_pairs={{0,2},{1,3},{2,0},{3,1},{4,6},{5,7},{6,4},{7,5},{8,10},{9,11},{10,... | collective-permute-start | bytes 1179656 | tf_op jit(solution)/shard_map/ppermute | solution.py:309
  8.1 1.4 %collective-permute-start.8 = (bf16[192,1024]{1,0:T(8,128)(2,1)}, bf16[192,1024]{1,0:T(8,128)(2,1)S(1)}, u32[]{:S(2)}, u32[]{:S(2)}) collective-permute-start(bf16[192,1024]{1,0:T(8,128)(2,1)} %get-tuple-element.19), channel_id=1, source_target_pairs={{0,3},{1,2},{2,1},{3,0},{4,7},{5,6},{6,5},{7,4},{8,11},{9,10},{10,... | collective-permute-start | bytes 1179656 | tf_op jit(solution)/shard_map/ppermute | solution.py:309
  9.5 1.5 %collective-permute-start.1 = (bf16[192,512]{1,0:T(8,128)(2,1)S(1)}, bf16[192,512]{1,0:T(8,128)(2,1)}, u32[]{:S(2)}, u32[]{:S(2)}) collective-permute-start(bf16[192,512]{1,0:T(8,128)(2,1)S(1)} %copy-done.7), channel_id=1, source_target_pairs={{0,2},{1,3},{2,0},{3,1},{4,6},{5,7},{6,4},{7,5},{8,10},{9,11},{10,... | collective-permute-start | bytes 589832 | tf_op jit(solution)/shard_map/ppermute | solution.py:309
  11.1 9.4 %collective-permute-done.refs_1_.refs_5_ = bf16[192,512]{1,0:T(8,128)(2,1)S(1)} collective-permute-done((bf16[192,512]{1,0:T(8,128)(2,1)S(1)}, bf16[192,512]{1,0:T(8,128)(2,1)S(1)}, u32[]{:S(2)}, u32[]{:S(2)}) %collective-permute-start) | collective-permute-done | bytes 196640 | tf_op jit(solution)/shard_map/ppermute | solution.py:309
  20.4 3.0 %collective-permute-start.2 = (bf16[192,512]{1,0:T(8,128)(2,1)S(1)}, bf16[192,512]{1,0:T(8,128)(2,1)}, u32[]{:S(2)}, u32[]{:S(2)}) collective-permute-start(bf16[192,512]{1,0:T(8,128)(2,1)S(1)} %copy-done.7), channel_id=1, source_target_pairs={{0,3},{1,2},{2,1},{3,0},{4,7},{5,6},{6,5},{7,4},{8,11},{9,10},{10,... | collective-permute-start | bytes 589832 | tf_op jit(solution)/shard_map/ppermute | solution.py:309
  23.4 0.0 copy-done.4
  23.4 0.0 copy-start.9
  23.4 4.5 %inverse_index.1.refs_10_.inverse_ref = s32[4,256,512]{2,1,0:T(8,128)S(1)} custom-call(s32[4,32,512]{2,1,0:T(8,128)S(1)} %copy-done.4), custom_call_target="tpu_custom_call" | custom-call | flops 33554432 | bytes 2097152 | tf_op jit(solution)/shard_map/inverse_index/pallas_call | solution.py:66
  28.0 0.0 copy-start
  28.0 1.3 %copy-done = s32[4,256,512]{2,1,0:T(8,128)} copy-done((s32[4,256,512]{2,1,0:T(8,128)}, s32[4,256,512]{2,1,0:T(8,128)S(1)}, u32[]{:S(2)}) %copy-start) | copy-done | bytes 2097176
  29.3 0.1 pad_add_fusion.place_ref
  29.4 0.0 copy-start.10
  29.4 4.5 %collective-permute-done.1.refs_2_.refs_6_ = bf16[192,512]{1,0:T(8,128)(2,1)} collective-permute-done((bf16[192,512]{1,0:T(8,128)(2,1)S(1)}, bf16[192,512]{1,0:T(8,128)(2,1)}, u32[]{:S(2)}, u32[]{:S(2)}) %collective-permute-start.1) | collective-permute-done | bytes 196640 | tf_op jit(solution)/shard_map/ppermute | solution.py:309
  33.8 0.0 collective-permute-done.2.refs_3_.refs_7_
  33.8 0.0 collective-permute-done.6.refs_1_
  33.9 0.0 collective-permute-done.7.refs_2_
  33.9 0.0 collective-permute-done.8.refs_3_
  33.9 0.0 copy-done.2
  33.9 0.0 copy-done.8
  33.9 0.0 copy-done.9
  33.9 6.9 %moment.1 = (f32[1024,512]{1,0:T(8,128)}, bf16[1024,512]{1,0:T(8,128)(2,1)S(1)}, bf16[4,16,512]{2,1,0:T(8,128)(2,1)S(1)}, bf16[4,16,512]{2,1,0:T(8,128)(2,1)S(1)}) custom-call(s32[2]{0:T(128)S(1)} %pad_add_fusion.place_ref, bf16[192,4096]{1,0:T(8,128)(2,1)S(1)} %copy-done.2, bf16[192,1024]{1,0:T(8,128)(2,1)S(1)} %collective-permute-done.6.refs_1_, ...), custom_call_target="tpu_custom_call" | custom-call | flops 1610612736 | bytes 8912896 | tf_op jit(solution)/shard_map/moment/pallas_call | solution.py:157
  40.8 0.0 copy-start.3
  40.8 0.0 copy-start.5
  40.8 0.0 copy-start.6
  40.8 0.1 collective-permute-start.9
  40.9 1.2 %collective-permute-done.9 = bf16[4,16,512]{2,1,0:T(8,128)(2,1)S(1)} collective-permute-done((bf16[4,16,512]{2,1,0:T(8,128)(2,1)S(1)}, bf16[4,16,512]{2,1,0:T(8,128)(2,1)S(1)}, u32[]{:S(2)}, u32[]{:S(2)}) %collective-permute-start.9) | collective-permute-done | bytes 65568 | tf_op jit(solution)/shard_map/ppermute | solution.py:309
  42.1 1.9 %collective-permute-start.10 = (bf16[4,16,512]{2,1,0:T(8,128)(2,1)S(1)}, bf16[4,16,512]{2,1,0:T(8,128)(2,1)S(1)}, u32[]{:S(2)}, u32[]{:S(2)}) collective-permute-start(bf16[4,16,512]{2,1,0:T(8,128)(2,1)S(1)} %add_convert_fusion.1), channel_id=1, source_target_pairs={{0,8},{4,12},{8,0},{12,4},{16,24},{20,28},{24,16},{28,20},{1,9},{5... | collective-permute-start | bytes 196616 | tf_op jit(solution)/shard_map/ppermute | solution.py:309
  44.0 2.6 %collective-permute-start.11 = (bf16[4,16,512]{2,1,0:T(8,128)(2,1)S(1)}, bf16[4,16,512]{2,1,0:T(8,128)(2,1)S(1)}, u32[]{:S(2)}, u32[]{:S(2)}) collective-permute-start(bf16[4,16,512]{2,1,0:T(8,128)(2,1)S(1)} %add_convert_fusion.1), channel_id=1, source_target_pairs={{0,16},{4,20},{8,24},{12,28},{16,0},{20,4},{24,8},{28,12},{1,17},{... | collective-permute-start | bytes 196616 | tf_op jit(solution)/shard_map/ppermute | solution.py:309
  46.6 0.0 collective-permute-start.12
  46.6 0.0 copy-done.10
  46.6 2.5 %input_gradients.1 = (bf16[192,1024]{1,0:T(8,128)(2,1)S(1)}, bf16[192,1024]{1,0:T(8,128)(2,1)S(1)}, bf16[192,1024]{1,0:T(8,128)(2,1)S(1)}, bf16[192,1024]{1,0:T(8,128)(2,1)S(1)}) custom-call(bf16[192,512]{1,0:T(8,128)(2,1)S(1)} %copy-done.7, bf16[192,512]{1,0:T(8,128)(2,1)S(1)} %collective-permute-done.refs_1_.refs_5_, ...), custom_call_target="tpu_custom_call" | custom-call | flops 805306368 | bytes 3407872 | tf_op jit(solution)/shard_map/input_gradients/pallas_call | solution.py:97
  49.1 1.8 %collective-permute-start.3 = (bf16[192,1024]{1,0:T(8,128)(2,1)S(1)}, bf16[192,1024]{1,0:T(8,128)(2,1)S(1)}, u32[]{:S(2)}, u32[]{:S(2)}) collective-permute-start(bf16[192,1024]{1,0:T(8,128)(2,1)S(1)} %get-tuple-element.12), channel_id=1, source_target_pairs={{0,1},{1,0},{2,3},{3,2},{4,5},{5,4},{6,7},{7,6},{8,9},{9,8},{10,11... | collective-permute-start | bytes 1179656 | tf_op jit(solution)/shard_map/ppermute | solution.py:309
  50.9 1.5 %collective-permute-start.4 = (bf16[192,1024]{1,0:T(8,128)(2,1)S(1)}, bf16[192,1024]{1,0:T(8,128)(2,1)S(1)}, u32[]{:S(2)}, u32[]{:S(2)}) collective-permute-start(bf16[192,1024]{1,0:T(8,128)(2,1)S(1)} %get-tuple-element.13), channel_id=1, source_target_pairs={{0,2},{1,3},{2,0},{3,1},{4,6},{5,7},{6,4},{7,5},{8,10},{9,11},{10,... | collective-permute-start | bytes 1179656 | tf_op jit(solution)/shard_map/ppermute | solution.py:309
  52.4 0.0 collective-permute-done.10
  52.4 0.3 collective-permute-start.5
  52.7 0.0 collective-permute-done.11
  52.7 0.1 collective-permute-done.12
  52.8 0.1 collective-permute-start.13
  52.9 0.0 copy-done.3
  52.9 0.0 copy-done.5
  52.9 0.0 copy-done.6
  52.9 0.0 copy-start.1
  52.9 2.5 %feedback.1 = f32[1,1024,512]{2,1,0:T(8,128)} custom-call(f32[1024,512]{1,0:T(8,128)S(1)} %copy-done.3, bf16[1024,512]{1,0:T(8,128)(2,1)S(1)} %get-tuple-element.16.masked_ref, bf16[256,256]{1,0:T(8,128)(2,1)S(1)} %copy-done.5, bf16[256,256]{1,0:T(8,128)(2,1)S(1)} %copy-done.6), custom_call_target="tpu_custom_call" | custom-call | flops 536870912 | bytes 5242880 | tf_op jit(solution)/shard_map/feedback/pallas_call | solution.py:204
  55.4 0.0 collective-permute-done.13.theirs_ref
  55.5 0.0 copy-done.1
  55.5 4.0 %decode.1 = bf16[1024,512]{1,0:T(8,128)(2,1)} custom-call(s32[2]{0:T(128)S(1)} %pad_add_fusion.place_ref, bf16[4,16,512]{2,1,0:T(8,128)(2,1)S(1)} %add_convert_fusion.mine_ref, bf16[4,16,512]{2,1,0:T(8,128)(2,1)S(1)} %collective-permute-done.13.theirs_ref, s32[4,256,512]{2,1,0:T(8,128)S(1)} %copy-done.1, bf16[256,256]{1,0:T(8,128)(2,1)S(1)} %copy-done.5, ...), custom_call_target="tpu_custom_call" | custom-call | flops 805306368 | bytes 3145728 | tf_op jit(solution)/shard_map/decode/pallas_call | solution.py:251
  59.4 1.8 %collective-permute-done.3.refs_1_ = bf16[192,1024]{1,0:T(8,128)(2,1)S(1)} collective-permute-done((bf16[192,1024]{1,0:T(8,128)(2,1)S(1)}, bf16[192,1024]{1,0:T(8,128)(2,1)S(1)}, u32[]{:S(2)}, u32[]{:S(2)}) %collective-permute-start.3) | collective-permute-done | bytes 393248 | tf_op jit(solution)/shard_map/ppermute | solution.py:309
  61.2 8.2 %collective-permute-done.4.refs_2_ = bf16[192,1024]{1,0:T(8,128)(2,1)S(1)} collective-permute-done((bf16[192,1024]{1,0:T(8,128)(2,1)S(1)}, bf16[192,1024]{1,0:T(8,128)(2,1)S(1)}, u32[]{:S(2)}, u32[]{:S(2)}) %collective-permute-start.4) | collective-permute-done | bytes 393248 | tf_op jit(solution)/shard_map/ppermute | solution.py:309
  69.5 0.0 collective-permute-done.5.refs_3_
  69.5 1.7 %assemble.1 = bf16[192,4096]{1,0:T(8,128)(2,1)} custom-call(s32[2]{0:T(128)S(1)} %pad_add_fusion.place_ref, bf16[192,1024]{1,0:T(8,128)(2,1)S(1)} %get-tuple-element.11.refs_0_, bf16[192,1024]{1,0:T(8,128)(2,1)S(1)} %collective-permute-done.3.refs_1_, bf16[192,1024]{1,0:T(8,128)(2,1)S(1)} %collective-permute-done.4.refs_2_, ...), custom_call_target="tpu_custom_call" | custom-call | bytes 3145728 | tf_op jit(solution)/shard_map/assemble/pallas_call | solution.py:293
  (2 shorter events, 0.1 us)
Async XLA Ops:
  0.6 5.4 %copy-start.7 = (bf16[192,512]{1,0:T(8,128)(2,1)S(1)}, bf16[192,512]{1,0:T(8,128)(2,1)}, u32[]{:S(2)}) copy-start(bf16[192,512]{1,0:T(8,128)(2,1)} %refs_4_.3) | copy-start | bytes 589828
  0.6 22.8 %copy-start.4 = (s32[4,32,512]{2,1,0:T(8,128)S(1)}, s32[4,32,512]{2,1,0:T(8,128)}, u32[]{:S(2)}) copy-start(s32[4,32,512]{2,1,0:T(8,128)} %refs_9_.1) | copy-start | bytes 786436
  0.7 33.2 %copy-start.2 = (bf16[192,4096]{1,0:T(8,128)(2,1)S(1)}, bf16[192,4096]{1,0:T(8,128)(2,1)}, u32[]{:S(2)}) copy-start(bf16[192,4096]{1,0:T(8,128)(2,1)} %refs_0_.3) | copy-start | bytes 4718596
  0.7 33.2 %copy-start.8 = (bf16[256,256]{1,0:T(8,128)(2,1)S(1)}, bf16[256,256]{1,0:T(8,128)(2,1)}, u32[]{:S(2)}) copy-start(bf16[256,256]{1,0:T(8,128)(2,1)} %constant.38.clone.refs_11_) | copy-start | bytes 393220
  3.1 30.7 %collective-permute-start.6 = (bf16[192,1024]{1,0:T(8,128)(2,1)}, bf16[192,1024]{1,0:T(8,128)(2,1)S(1)}, u32[]{:S(2)}, u32[]{:S(2)}) collective-permute-start(bf16[192,1024]{1,0:T(8,128)(2,1)} %get-tuple-element.21), channel_id=1, source_target_pairs={{0,1},{1,0},{2,3},{3,2},{4,5},{5,4},{6,7},{7,6},{8,9},{9,8},{10,11... | collective-permute-start | bytes 1179656 | tf_op jit(solution)/shard_map/ppermute | solution.py:309
  6.1 14.4 %collective-permute-start = (bf16[192,512]{1,0:T(8,128)(2,1)S(1)}, bf16[192,512]{1,0:T(8,128)(2,1)S(1)}, u32[]{:S(2)}, u32[]{:S(2)}) collective-permute-start(bf16[192,512]{1,0:T(8,128)(2,1)S(1)} %copy-done.7), channel_id=1, source_target_pairs={{0,1},{1,0},{2,3},{3,2},{4,5},{5,4},{6,7},{7,6},{8,9},{9,8},{10,11... | collective-permute-start | bytes 589832 | tf_op jit(solution)/shard_map/ppermute | solution.py:309
  6.1 27.8 %collective-permute-start.7 = (bf16[192,1024]{1,0:T(8,128)(2,1)}, bf16[192,1024]{1,0:T(8,128)(2,1)S(1)}, u32[]{:S(2)}, u32[]{:S(2)}) collective-permute-start(bf16[192,1024]{1,0:T(8,128)(2,1)} %get-tuple-element.20), channel_id=1, source_target_pairs={{0,2},{1,3},{2,0},{3,1},{4,6},{5,7},{6,4},{7,5},{8,10},{9,11},{10,... | collective-permute-start | bytes 1179656 | tf_op jit(solution)/shard_map/ppermute | solution.py:309
  8.1 25.8 %collective-permute-start.8 = (bf16[192,1024]{1,0:T(8,128)(2,1)}, bf16[192,1024]{1,0:T(8,128)(2,1)S(1)}, u32[]{:S(2)}, u32[]{:S(2)}) collective-permute-start(bf16[192,1024]{1,0:T(8,128)(2,1)} %get-tuple-element.19), channel_id=1, source_target_pairs={{0,3},{1,2},{2,1},{3,0},{4,7},{5,6},{6,5},{7,4},{8,11},{9,10},{10,... | collective-permute-start | bytes 1179656 | tf_op jit(solution)/shard_map/ppermute | solution.py:309
  9.5 24.3 %collective-permute-start.1 = (bf16[192,512]{1,0:T(8,128)(2,1)S(1)}, bf16[192,512]{1,0:T(8,128)(2,1)}, u32[]{:S(2)}, u32[]{:S(2)}) collective-permute-start(bf16[192,512]{1,0:T(8,128)(2,1)S(1)} %copy-done.7), channel_id=1, source_target_pairs={{0,2},{1,3},{2,0},{3,1},{4,6},{5,7},{6,4},{7,5},{8,10},{9,11},{10,... | collective-permute-start | bytes 589832 | tf_op jit(solution)/shard_map/ppermute | solution.py:309
  20.4 13.4 %collective-permute-start.2 = (bf16[192,512]{1,0:T(8,128)(2,1)S(1)}, bf16[192,512]{1,0:T(8,128)(2,1)}, u32[]{:S(2)}, u32[]{:S(2)}) collective-permute-start(bf16[192,512]{1,0:T(8,128)(2,1)S(1)} %copy-done.7), channel_id=1, source_target_pairs={{0,3},{1,2},{2,1},{3,0},{4,7},{5,6},{6,5},{7,4},{8,11},{9,10},{10,... | collective-permute-start | bytes 589832 | tf_op jit(solution)/shard_map/ppermute | solution.py:309
  23.4 10.5 %copy-start.9 = (bf16[256,256]{1,0:T(8,128)(2,1)S(1)}, bf16[256,256]{1,0:T(8,128)(2,1)}, u32[]{:S(2)}) copy-start(bf16[256,256]{1,0:T(8,128)(2,1)} %constant.39.clone.refs_12_) | copy-start | bytes 393220
  28.0 1.3 %copy-start = (s32[4,256,512]{2,1,0:T(8,128)}, s32[4,256,512]{2,1,0:T(8,128)S(1)}, u32[]{:S(2)}) copy-start(s32[4,256,512]{2,1,0:T(8,128)S(1)} %inverse_index.1.refs_10_.inverse_ref) | copy-start | bytes 6291460
  29.4 17.2 %copy-start.10 = (bf16[1024,512]{1,0:T(8,128)(2,1)S(1)}, bf16[1024,512]{1,0:T(8,128)(2,1)}, u32[]{:S(2)}) copy-start(bf16[1024,512]{1,0:T(8,128)(2,1)} %refs_4_.2) | copy-start | bytes 3145732
  40.8 12.1 %copy-start.3 = (f32[1024,512]{1,0:T(8,128)S(1)}, f32[1024,512]{1,0:T(8,128)}, u32[]{:S(2)}) copy-start(f32[1024,512]{1,0:T(8,128)} %get-tuple-element.15.moment_ref) | copy-start | bytes 6291460
  40.8 12.1 %copy-start.5 = (bf16[256,256]{1,0:T(8,128)(2,1)S(1)}, bf16[256,256]{1,0:T(8,128)(2,1)}, u32[]{:S(2)}) copy-start(bf16[256,256]{1,0:T(8,128)(2,1)} %constant.40.clone.high_ref) | copy-start | bytes 393220
  40.8 12.1 %copy-start.6 = (bf16[256,256]{1,0:T(8,128)(2,1)S(1)}, bf16[256,256]{1,0:T(8,128)(2,1)}, u32[]{:S(2)}) copy-start(bf16[256,256]{1,0:T(8,128)(2,1)} %constant.41.clone.low_ref) | copy-start | bytes 393220
  40.8 1.3 %collective-permute-start.9 = (bf16[4,16,512]{2,1,0:T(8,128)(2,1)S(1)}, bf16[4,16,512]{2,1,0:T(8,128)(2,1)S(1)}, u32[]{:S(2)}, u32[]{:S(2)}) collective-permute-start(bf16[4,16,512]{2,1,0:T(8,128)(2,1)S(1)} %get-tuple-element.18), channel_id=1, source_target_pairs={{0,4},{4,0},{8,12},{12,8},{16,20},{20,16},{24,28},{28,24},{1,5},{5... | collective-permute-start | bytes 196616 | tf_op jit(solution)/shard_map/ppermute | solution.py:309
  42.1 10.3 %collective-permute-start.10 = (bf16[4,16,512]{2,1,0:T(8,128)(2,1)S(1)}, bf16[4,16,512]{2,1,0:T(8,128)(2,1)S(1)}, u32[]{:S(2)}, u32[]{:S(2)}) collective-permute-start(bf16[4,16,512]{2,1,0:T(8,128)(2,1)S(1)} %add_convert_fusion.1), channel_id=1, source_target_pairs={{0,8},{4,12},{8,0},{12,4},{16,24},{20,28},{24,16},{28,20},{1,9},{5... | collective-permute-start | bytes 196616 | tf_op jit(solution)/shard_map/ppermute | solution.py:309
  44.0 8.7 %collective-permute-start.11 = (bf16[4,16,512]{2,1,0:T(8,128)(2,1)S(1)}, bf16[4,16,512]{2,1,0:T(8,128)(2,1)S(1)}, u32[]{:S(2)}, u32[]{:S(2)}) collective-permute-start(bf16[4,16,512]{2,1,0:T(8,128)(2,1)S(1)} %add_convert_fusion.1), channel_id=1, source_target_pairs={{0,16},{4,20},{8,24},{12,28},{16,0},{20,4},{24,8},{28,12},{1,17},{... | collective-permute-start | bytes 196616 | tf_op jit(solution)/shard_map/ppermute | solution.py:309
  46.6 6.2 %collective-permute-start.12 = (bf16[4,16,512]{2,1,0:T(8,128)(2,1)S(1)}, bf16[4,16,512]{2,1,0:T(8,128)(2,1)S(1)}, u32[]{:S(2)}, u32[]{:S(2)}) collective-permute-start(bf16[4,16,512]{2,1,0:T(8,128)(2,1)S(1)} %add_convert_fusion.1), channel_id=1, source_target_pairs={{0,24},{4,28},{8,16},{12,20},{16,8},{20,12},{24,0},{28,4},{1,25},{... | collective-permute-start | bytes 196616 | tf_op jit(solution)/shard_map/ppermute | solution.py:309
  49.1 12.1 %collective-permute-start.3 = (bf16[192,1024]{1,0:T(8,128)(2,1)S(1)}, bf16[192,1024]{1,0:T(8,128)(2,1)S(1)}, u32[]{:S(2)}, u32[]{:S(2)}) collective-permute-start(bf16[192,1024]{1,0:T(8,128)(2,1)S(1)} %get-tuple-element.12), channel_id=1, source_target_pairs={{0,1},{1,0},{2,3},{3,2},{4,5},{5,4},{6,7},{7,6},{8,9},{9,8},{10,11... | collective-permute-start | bytes 1179656 | tf_op jit(solution)/shard_map/ppermute | solution.py:309
  50.9 18.5 %collective-permute-start.4 = (bf16[192,1024]{1,0:T(8,128)(2,1)S(1)}, bf16[192,1024]{1,0:T(8,128)(2,1)S(1)}, u32[]{:S(2)}, u32[]{:S(2)}) collective-permute-start(bf16[192,1024]{1,0:T(8,128)(2,1)S(1)} %get-tuple-element.13), channel_id=1, source_target_pairs={{0,2},{1,3},{2,0},{3,1},{4,6},{5,7},{6,4},{7,5},{8,10},{9,11},{10,... | collective-permute-start | bytes 1179656 | tf_op jit(solution)/shard_map/ppermute | solution.py:309
  52.4 17.0 %collective-permute-start.5 = (bf16[192,1024]{1,0:T(8,128)(2,1)S(1)}, bf16[192,1024]{1,0:T(8,128)(2,1)S(1)}, u32[]{:S(2)}, u32[]{:S(2)}) collective-permute-start(bf16[192,1024]{1,0:T(8,128)(2,1)S(1)} %get-tuple-element.14), channel_id=1, source_target_pairs={{0,3},{1,2},{2,1},{3,0},{4,7},{5,6},{6,5},{7,4},{8,11},{9,10},{10,... | collective-permute-start | bytes 1179656 | tf_op jit(solution)/shard_map/ppermute | solution.py:309
  52.8 2.7 %collective-permute-start.13 = (bf16[4,16,512]{2,1,0:T(8,128)(2,1)S(1)}, bf16[4,16,512]{2,1,0:T(8,128)(2,1)S(1)}, u32[]{:S(2)}, u32[]{:S(2)}) collective-permute-start(bf16[4,16,512]{2,1,0:T(8,128)(2,1)S(1)} %add_convert_fusion.mine_ref), channel_id=1, source_target_pairs={{0,4},{4,0},{8,12},{12,8},{16,20},{20,16},{24,28},{28,24},{1,5},{5... | collective-permute-start | bytes 196616 | tf_op jit(solution)/shard_map/ppermute | solution.py:309
  52.9 2.5 %copy-start.1 = (s32[4,256,512]{2,1,0:T(8,128)S(1)}, s32[4,256,512]{2,1,0:T(8,128)}, u32[]{:S(2)}) copy-start(s32[4,256,512]{2,1,0:T(8,128)} %copy-done) | copy-start | bytes 6291460

commit v2 on v1

--- a/solution.py
+++ b/solution.py
@@ -12,7 +12,7 @@
 MOMENTUM_DECAY = 0.999
 LANES = 128
 SUBLANES = 8
-VMEM_LIMIT = 48 * 1024 * 1024
+VMEM_LIMIT = 16 * 1024 * 1024
 
 
 def transform_table():
@@ -220,7 +220,20 @@
     )(moment, masked, high, low)
 
 
-def decode_kernel(replicas, place_ref, mine_ref, theirs_ref, inverse_ref, high_ref, low_ref, update_ref, dense_ref):
+def decode_kernel(replicas, groups, place_ref, mine_ref, theirs_ref, inverse_ref, high_ref, low_ref, *refs):
+    parts, update_ref, whole_ref, dense_ref, sems = refs[:groups], *refs[groups:]
+    width = parts[0].shape[1]
+
+    def copies():
+        for m in range(groups):
+            at = pl.multiple_of((place_ref[0] ^ m) * width, width)
+            yield pltpu.make_async_copy(parts[m], whole_ref.at[:, pl.ds(at, width)], sems.at[m])
+
+    @pl.when(pl.program_id(0) == 0)
+    def _():
+        for copy in copies():
+            copy.start()
+
     columns = mine_ref.shape[2]
     half = mine_ref.shape[1]
     second = place_ref[1] == 1
@@ -243,14 +256,24 @@
             dense_ref[g : g + SUBLANES, c : c + LANES] = total
     update_ref[...] = split_dot(high_ref[...], low_ref[...], dense_ref[...]).astype(jnp.bfloat16)
 
-
-def decode(place, mine, theirs, inverse, high, low, replicas):
+    @pl.when(pl.program_id(0) == pl.num_programs(0) - 1)
+    def _():
+        for copy in copies():
+            copy.wait()
+
+
+def decode(place, mine, theirs, inverse, high, low, parts, replicas):
     blocks, half, columns = mine.shape
+    groups = len(parts)
+    tokens, width = parts[0].shape
     whole = lambda b, place: (0, 0)
     by_block = lambda b, place: (b, 0, 0)
     return pl.pallas_call(
-        functools.partial(decode_kernel, replicas),
-        out_shape=jax.ShapeDtypeStruct((blocks * SPAN, columns), jnp.bfloat16),
+        functools.partial(decode_kernel, replicas, groups),
+        out_shape=[
+            jax.ShapeDtypeStruct((blocks * SPAN, columns), jnp.bfloat16),
+            jax.ShapeDtypeStruct((tokens, groups * width), jnp.bfloat16),
+        ],
         grid_spec=pltpu.PrefetchScalarGridSpec(
             num_scalar_prefetch=1,
             grid=(blocks,),
@@ -260,48 +283,25 @@
                 pl.BlockSpec((1, SPAN, columns), by_block),
                 pl.BlockSpec((SPAN, SPAN), whole),
                 pl.BlockSpec((SPAN, SPAN), whole),
+            ]
+            + [pl.BlockSpec(memory_space=pl.ANY)] * groups,
+            out_specs=[
+                pl.BlockSpec((SPAN, columns), lambda b, place: (b, 0)),
+                pl.BlockSpec(memory_space=pl.ANY),
             ],
-            out_specs=pl.BlockSpec((SPAN, columns), lambda b, place: (b, 0)),
-            scratch_shapes=[pltpu.VMEM((SPAN, columns), jnp.float32)],
+            scratch_shapes=[
+                pltpu.VMEM((SPAN, columns), jnp.float32),
+                pltpu.SemaphoreType.DMA((groups,)),
+            ],
         ),
         compiler_params=params(),
         cost_estimate=pl.CostEstimate(
             flops=6 * blocks * SPAN * SPAN * columns,
-            bytes_accessed=6 * blocks * SPAN * columns,
+            bytes_accessed=6 * blocks * SPAN * columns + 4 * groups * tokens * width,
             transcendentals=0,
         ),
         name="decode",
-    )(place, mine, theirs, inverse, high, low)
-
-
-def assemble_kernel(groups, place_ref, *refs):
-    parts, out_ref, sems = refs[:groups], refs[groups], refs[groups + 1]
-    width = parts[0].shape[1]
-    copies = []
-    for m in range(groups):
-        at = pl.multiple_of((place_ref[0] ^ m) * width, width)
-        copies.append(pltpu.make_async_copy(parts[m], out_ref.at[:, pl.ds(at, width)], sems.at[m]))
-    for copy in copies:
-        copy.start()
-    for copy in copies:
-        copy.wait()
-
-
-def assemble(place, parts):
-    groups = len(parts)
-    tokens, width = parts[0].shape
-    return pl.pallas_call(
-        functools.partial(assemble_kernel, groups),
-        out_shape=jax.ShapeDtypeStruct((tokens, groups * width), jnp.bfloat16),
-        in_specs=[pl.BlockSpec(memory_space=pltpu.SMEM)] + [pl.BlockSpec(memory_space=pl.ANY)] * groups,
-        out_specs=pl.BlockSpec(memory_space=pl.ANY),
-        scratch_shapes=[pltpu.SemaphoreType.DMA((groups,))],
-        compiler_params=params(),
-        cost_estimate=pl.CostEstimate(
-            flops=0, bytes_accessed=4 * groups * tokens * width, transcendentals=0
-        ),
-        name="assemble",
-    )(place, *parts)
+    )(place, mine, theirs, inverse, high, low, *parts)
 
 
 def swap(x, axis, mask):
@@ -330,23 +330,27 @@
     high, low = transform_table()
 
     cotangents = [cotangent] + [swap(cotangent, "fsdp", m) for m in range(1, groups)]
-    inputs = [
-        swap(lax.dynamic_slice_in_dim(activations, (index ^ m) * rows, rows, 1), "fsdp", m)
-        for m in range(1, groups)
+    inverse = inverse_index(positions)
+    sent = [
+        lax.dynamic_slice_in_dim(activations, (index ^ m) * rows, rows, 1) for m in range(1, groups)
     ]
-    inverse = inverse_index(positions)
+    sent, cotangents = lax.optimization_barrier((sent, cotangents))
+    inputs = [swap(sent[m - 1], "fsdp", m) for m in range(1, groups)]
     outer = input_gradients(cotangents, weight)
-    grad_input = assemble(
-        place, [outer[0]] + [swap(outer[m], "fsdp", m) for m in range(1, groups)]
-    )
+    inputs, inverse, _ = lax.optimization_barrier((inputs, inverse, outer))
+    parts = [outer[0]] + [swap(outer[m], "fsdp", m) for m in range(1, groups)]
 
     moment, masked, mine, theirs = moments(
         place, activations, inputs, cotangents, momentum, positions, inverse, high, low
     )
     chip = mine.astype(jnp.float32) + swap(theirs, "dp", 1).astype(jnp.float32)
+    moment, parts[1], parts[2] = lax.optimization_barrier((moment, parts[1], parts[2]))
     new_momentum = feedback(moment, masked, high.T, low.T)
     summed = sum_over_chips(chip)
-    update = decode(place, summed, swap(summed, "dp", 1), inverse, high.T, low.T, replicas)
+    summed, new_momentum = lax.optimization_barrier((summed, new_momentum))
+    update, grad_input = decode(
+        place, summed, swap(summed, "dp", 1), inverse, high.T, low.T, parts, replicas
+    )
     return grad_input, new_momentum, update
 
 

time: 71.4 us -> 58 us (0.81)
  Pallas kernels: 22.1 us -> 17.7 us
  waiting for transfers between devices: 25.2 us -> 20.8 us
  starting transfers between devices: 19.1 us -> 16 us
  local copies, waits for them, and re-layouts: 3.78 us -> 2.41 us
    ppermute x14, waiting for transfers between devices: 25.2 us -> 20.8 us  [swap(): return lax.ppermute(x, axis, [(s, s ^ mask) for s in range(size)])]
    ppermute x14, starting transfers between devices: 19.1 us -> 16 us  [swap(): return lax.ppermute(x, axis, [(s, s ^ mask) for s in range(size)])]
    pallas_call x1, Pallas kernels: 6.89 us -> 4.97 us  [moments(): pl.pallas_call(functools.partial(moment_kernel, groups), out_shape=[jax.S...]
    pallas_call x2 -> x1, Pallas kernels: 5.68 us -> 4.19 us  [decode(): pl.pallas_call(functools.partial(decode_kernel, replicas, groups), out_sh...]
    unnamed x22 -> x18, local copies, waits for them, and re-layouts: 1.37 us -> 0.04 us
    pallas_call x1, Pallas kernels: 2.53 us -> 1.51 us  [input_gradients(): pl.pallas_call(functools.partial(outer_kernel, groups), out_shape=[jax.Sh...]
  transfers between devices with their start and end apart: 14 -> 14, of which waited for: 6 -> 7; matrix products, arithmetic and copies ran while one was open for 0% -> 4% of each run, Pallas kernels for 19% -> 23%
where the time goes in v2:
time: 58 us; the launch traced here: 57.9 us
  waiting for transfers between devices  20.8 us (36%)
  Pallas kernels  17.7 us (31%)
  starting transfers between devices  16 us (28%)
  local copies, waits for them, and re-layouts  2.41 us (4%)
  between operations  0.75 us (1%)
    ppermute x14, waiting for transfers between devices, swap(): return lax.ppermute(x, axis, [(s, s ^ mask) for s in range(size)])  20.8 us
    ppermute x14, starting transfers between devices, swap(): return lax.ppermute(x, axis, [(s, s ^ mask) for s in range(size)])  16 us
    pallas_call x1, Pallas kernels, moments(): pl.pallas_call(functools.partial(moment_kernel, groups), out_shape=[jax.S...  4.97 us
    pallas_call x1, Pallas kernels, inverse_index(): pl.pallas_call(inverse_index_kernel, out_shape=jax.ShapeDtypeStruct((bloc...  4.53 us
    pallas_call x1, Pallas kernels, decode(): pl.pallas_call(functools.partial(decode_kernel, replicas, groups), out_sh...  4.19 us
    pallas_call x1, Pallas kernels, feedback(): pl.pallas_call(feedback_kernel, out_shape=jax.ShapeDtypeStruct((1, rows,...  2.53 us
    dynamic_slice x1, local copies, waits for them, and re-layouts, on_device(): lax.dynamic_slice_in_dim(activations, (index ^ m) * rows, rows, 1)  2.36 us
    pallas_call x1, Pallas kernels, input_gradients(): pl.pallas_call(functools.partial(outer_kernel, groups), out_shape=[jax.Sh...  1.51 us
  transfers between devices with their start and end apart: 14, of which 7 were waited for; matrix products, arithmetic and copies ran while one was open for 4% of the time, Pallas kernels for 23%

profile of v2, /device:TPU:0, one launch (start us, length us, event | category | flops | bytes accessed | tf_op | source)
XLA Modules:
  0.0 57.9 jit_solution(8141187597853452023)
XLA Ops:
  0.6 0.0 copy-start.2
  0.6 3.0 %collective-permute-start = (bf16[192,512]{1,0:T(8,128)(2,1)}, bf16[192,512]{1,0:T(8,128)(2,1)S(1)}, u32[]{:S(2)}, u32[]{:S(2)}) collective-permute-start(bf16[192,512]{1,0:T(8,128)(2,1)} %refs_4_.2), channel_id=1, source_target_pairs={{0,1},{1,0},{2,3},{3,2},{4,5},{5,4},{6,7},{7,6},{8,9},{9,8},{10,11... | collective-permute-start | bytes 589832 | tf_op jit(solution)/shard_map/ppermute | solution.py:309
  3.6 1.5 %collective-permute-start.1 = (bf16[192,512]{1,0:T(8,128)(2,1)}, bf16[192,512]{1,0:T(8,128)(2,1)S(1)}, u32[]{:S(2)}, u32[]{:S(2)}) collective-permute-start(bf16[192,512]{1,0:T(8,128)(2,1)} %refs_4_.2), channel_id=1, source_target_pairs={{0,2},{1,3},{2,0},{3,1},{4,6},{5,7},{6,4},{7,5},{8,10},{9,11},{10,... | collective-permute-start | bytes 589832 | tf_op jit(solution)/shard_map/ppermute | solution.py:309
  5.2 0.0 collective-permute-start.2
  5.2 0.0 copy-start.5
  5.2 0.0 copy-start.8
  5.2 2.4 %constant_dynamic-slice_fusion = (bf16[192,1024]{1,0:T(8,128)(2,1)}, bf16[192,1024]{1,0:T(8,128)(2,1)}, bf16[192,1024]{1,0:T(8,128)(2,1)}) fusion(bf16[192,4096]{1,0:T(8,128)(2,1)} %refs_0_.2, s32[]{:T(128)S(6)} %select_n.19, s32[]{:T(128)S(6)} %select_n.18, s32[]{:T(128)S(6)} %select_n.17), kind=kLoop, calls=%fused_computation.2 | loop fusion | bytes 2359308 | tf_op jit(solution)/shard_map/dynamic_slice | solution.py:335
  7.6 2.0 %collective-permute-done.refs_1_.refs_5_ = bf16[192,512]{1,0:T(8,128)(2,1)S(1)} collective-permute-done((bf16[192,512]{1,0:T(8,128)(2,1)}, bf16[192,512]{1,0:T(8,128)(2,1)S(1)}, u32[]{:S(2)}, u32[]{:S(2)}) %collective-permute-start) | collective-permute-done | bytes 196640 | tf_op jit(solution)/shard_map/ppermute | solution.py:309
  9.6 4.8 %collective-permute-done.1.refs_2_.refs_6_ = bf16[192,512]{1,0:T(8,128)(2,1)S(1)} collective-permute-done((bf16[192,512]{1,0:T(8,128)(2,1)}, bf16[192,512]{1,0:T(8,128)(2,1)S(1)}, u32[]{:S(2)}, u32[]{:S(2)}) %collective-permute-start.1) | collective-permute-done | bytes 196640 | tf_op jit(solution)/shard_map/ppermute | solution.py:309
  14.4 0.0 collective-permute-done.2.refs_3_.refs_7_
  14.4 1.2 %collective-permute-start.3 = (bf16[192,1024]{1,0:T(8,128)(2,1)}, bf16[192,1024]{1,0:T(8,128)(2,1)S(1)}, u32[]{:S(2)}, u32[]{:S(2)}) collective-permute-start(bf16[192,1024]{1,0:T(8,128)(2,1)} %get-tuple-element.29), channel_id=1, source_target_pairs={{0,1},{1,0},{2,3},{3,2},{4,5},{5,4},{6,7},{7,6},{8,9},{9,8},{10,11... | collective-permute-start | bytes 1179656 | tf_op jit(solution)/shard_map/ppermute | solution.py:309
  15.7 0.8 %collective-permute-start.4 = (bf16[192,1024]{1,0:T(8,128)(2,1)}, bf16[192,1024]{1,0:T(8,128)(2,1)S(1)}, u32[]{:S(2)}, u32[]{:S(2)}) collective-permute-start(bf16[192,1024]{1,0:T(8,128)(2,1)} %get-tuple-element.30), channel_id=1, source_target_pairs={{0,2},{1,3},{2,0},{3,1},{4,6},{5,7},{6,4},{7,5},{8,10},{9,11},{10,... | collective-permute-start | bytes 1179656 | tf_op jit(solution)/shard_map/ppermute | solution.py:309
  16.5 1.4 %collective-permute-start.5 = (bf16[192,1024]{1,0:T(8,128)(2,1)}, bf16[192,1024]{1,0:T(8,128)(2,1)S(1)}, u32[]{:S(2)}, u32[]{:S(2)}) collective-permute-start(bf16[192,1024]{1,0:T(8,128)(2,1)} %get-tuple-element.31), channel_id=1, source_target_pairs={{0,3},{1,2},{2,1},{3,0},{4,7},{5,6},{6,5},{7,4},{8,11},{9,10},{10,... | collective-permute-start | bytes 1179656 | tf_op jit(solution)/shard_map/ppermute | solution.py:309
  17.9 0.0 copy-done.2
  17.9 0.0 copy-start
  17.9 0.0 copy-start.1
  17.9 0.0 copy-start.6
  17.9 0.0 copy-start.7
  17.9 4.5 %inverse_index.1.refs_10_.inverse_ref = s32[4,256,512]{2,1,0:T(8,128)S(1)} custom-call(s32[4,32,512]{2,1,0:T(8,128)S(1)} %copy-done.2), custom_call_target="tpu_custom_call" | custom-call | flops 33554432 | bytes 2097152 | tf_op jit(solution)/shard_map/inverse_index/pallas_call | solution.py:66
  22.5 0.1 pad_add_fusion.place_ref
  22.6 0.0 copy-done.5
  22.6 0.0 copy-done.8
  22.6 1.5 %input_gradients.1 = (bf16[192,1024]{1,0:T(8,128)(2,1)S(1)}, bf16[192,1024]{1,0:T(8,128)(2,1)S(1)}, bf16[192,1024]{1,0:T(8,128)(2,1)S(1)}, bf16[192,1024]{1,0:T(8,128)(2,1)S(1)}) custom-call(bf16[192,512]{1,0:T(8,128)(2,1)S(1)} %copy-done.5, bf16[192,512]{1,0:T(8,128)(2,1)S(1)} %collective-permute-done.refs_1_.refs_5_, ...), custom_call_target="tpu_custom_call" | custom-call | flops 805306368 | bytes 3407872 | tf_op jit(solution)/shard_map/input_gradients/pallas_call | solution.py:97
  24.1 1.3 %collective-permute-start.10 = (bf16[192,1024]{1,0:T(8,128)(2,1)S(1)}, bf16[192,1024]{1,0:T(8,128)(2,1)S(1)}, u32[]{:S(2)}, u32[]{:S(2)}) collective-permute-start(bf16[192,1024]{1,0:T(8,128)(2,1)S(1)} %get-tuple-element.37), channel_id=1, source_target_pairs={{0,1},{1,0},{2,3},{3,2},{4,5},{5,4},{6,7},{7,6},{8,9},{9,8},{10,11... | collective-permute-start | bytes 1179656 | tf_op jit(solution)/shard_map/ppermute | solution.py:309
  25.4 0.8 %collective-permute-start.11 = (bf16[192,1024]{1,0:T(8,128)(2,1)S(1)}, bf16[192,1024]{1,0:T(8,128)(2,1)S(1)}, u32[]{:S(2)}, u32[]{:S(2)}) collective-permute-start(bf16[192,1024]{1,0:T(8,128)(2,1)S(1)} %get-tuple-element.38), channel_id=1, source_target_pairs={{0,2},{1,3},{2,0},{3,1},{4,6},{5,7},{6,4},{7,5},{8,10},{9,11},{10,... | collective-permute-start | bytes 1179656 | tf_op jit(solution)/shard_map/ppermute | solution.py:309
  26.2 0.5 collective-permute-done.3.refs_1_
  26.7 9.2 %collective-permute-done.4.refs_2_ = bf16[192,1024]{1,0:T(8,128)(2,1)S(1)} collective-permute-done((bf16[192,1024]{1,0:T(8,128)(2,1)}, bf16[192,1024]{1,0:T(8,128)(2,1)S(1)}, u32[]{:S(2)}, u32[]{:S(2)}) %collective-permute-start.4) | collective-permute-done | bytes 393248 | tf_op jit(solution)/shard_map/ppermute | solution.py:309
  35.9 0.2 collective-permute-done.5.refs_3_
  36.1 0.0 copy-done
  36.1 0.0 copy-done.1
  36.1 0.0 copy-done.6
  36.1 0.0 copy-done.7
  36.1 0.0 copy-start.3
  36.2 0.0 copy-start.4
  36.2 5.0 %moment.1 = (f32[1024,512]{1,0:T(8,128)S(1)}, bf16[1024,512]{1,0:T(8,128)(2,1)S(1)}, bf16[4,16,512]{2,1,0:T(8,128)(2,1)S(1)}, bf16[4,16,512]{2,1,0:T(8,128)(2,1)S(1)}) custom-call(s32[2]{0:T(128)S(1)} %pad_add_fusion.place_ref, bf16[192,4096]{1,0:T(8,128)(2,1)S(1)} %copy-done, bf16[192,1024]{1,0:T(8,128)(2,1)S(1)} %collective-permute-done.3.refs_1_, ...), custom_call_target="tpu_custom_call" | custom-call | flops 1610612736 | bytes 8912896 | tf_op jit(solution)/shard_map/moment/pallas_call | solution.py:157
  41.2 0.1 collective-permute-start.6
  41.2 1.2 %collective-permute-start.13 = (bf16[192,1024]{1,0:T(8,128)(2,1)S(1)}, bf16[192,1024]{1,0:T(8,128)(2,1)S(1)}, u32[]{:S(2)}, u32[]{:S(2)}) collective-permute-start(bf16[192,1024]{1,0:T(8,128)(2,1)S(1)} %get-tuple-element.39), channel_id=1, source_target_pairs={{0,3},{1,2},{2,1},{3,0},{4,7},{5,6},{6,5},{7,4},{8,11},{9,10},{10,... | collective-permute-start | bytes 1179656 | tf_op jit(solution)/shard_map/ppermute | solution.py:309
  42.5 0.0 collective-permute-done.6
  42.5 3.7 %collective-permute-start.9 = (bf16[4,16,512]{2,1,0:T(8,128)(2,1)S(1)}, bf16[4,16,512]{2,1,0:T(8,128)(2,1)S(1)}, u32[]{:S(2)}, u32[]{:S(2)}) collective-permute-start(bf16[4,16,512]{2,1,0:T(8,128)(2,1)S(1)} %add_convert_fusion.1), channel_id=1, source_target_pairs={{0,24},{4,28},{8,16},{12,20},{16,8},{20,12},{24,0},{28,4},{1,25},{... | collective-permute-start | bytes 196616 | tf_op jit(solution)/shard_map/ppermute | solution.py:309
  46.2 0.0 collective-permute-start.8
  46.2 0.0 collective-permute-done.10.refs_1_
  46.2 0.8 %collective-permute-start.7 = (bf16[4,16,512]{2,1,0:T(8,128)(2,1)S(1)}, bf16[4,16,512]{2,1,0:T(8,128)(2,1)S(1)}, u32[]{:S(2)}, u32[]{:S(2)}) collective-permute-start(bf16[4,16,512]{2,1,0:T(8,128)(2,1)S(1)} %add_convert_fusion.1), channel_id=1, source_target_pairs={{0,8},{4,12},{8,0},{12,4},{16,24},{20,28},{24,16},{28,20},{1,9},{5... | collective-permute-start | bytes 196616 | tf_op jit(solution)/shard_map/ppermute | solution.py:309
  47.0 0.0 collective-permute-done.11.refs_2_
  47.0 0.0 copy-done.3
  47.0 0.0 copy-done.4
  47.0 2.5 %feedback.1 = f32[1,1024,512]{2,1,0:T(8,128)} custom-call(f32[1024,512]{1,0:T(8,128)S(1)} %get-tuple-element.47.moment_ref, bf16[1024,512]{1,0:T(8,128)(2,1)S(1)} %get-tuple-element.48.masked_ref, bf16[256,256]{1,0:T(8,128)(2,1)S(1)} %copy-done.3, bf16[256,256]{1,0:T(8,128)(2,1)S(1)} %copy-done.4), custom_call_target="tpu_custom_call" | custom-call | flops 536870912 | bytes 5242880 | tf_op jit(solution)/shard_map/feedback/pallas_call | solution.py:204
  49.5 0.0 collective-permute-done.9
  49.5 2.5 %collective-permute-done.8 = bf16[4,16,512]{2,1,0:T(8,128)(2,1)S(1)} collective-permute-done((bf16[4,16,512]{2,1,0:T(8,128)(2,1)S(1)}, bf16[4,16,512]{2,1,0:T(8,128)(2,1)S(1)}, u32[]{:S(2)}, u32[]{:S(2)}) %collective-permute-start.8) | collective-permute-done | bytes 65568 | tf_op jit(solution)/shard_map/ppermute | solution.py:309
  52.1 0.0 collective-permute-done.7
  52.1 0.1 collective-permute-start.12
  52.2 1.5 %collective-permute-done.13.refs_3_ = bf16[192,1024]{1,0:T(8,128)(2,1)S(1)} collective-permute-done((bf16[192,1024]{1,0:T(8,128)(2,1)S(1)}, bf16[192,1024]{1,0:T(8,128)(2,1)S(1)}, u32[]{:S(2)}, u32[]{:S(2)}) %collective-permute-start.13) | collective-permute-done | bytes 393248 | tf_op jit(solution)/shard_map/ppermute | solution.py:309
  53.7 0.0 collective-permute-done.12.theirs_ref
  53.7 4.2 %decode.1 = (bf16[1024,512]{1,0:T(8,128)(2,1)}, bf16[192,4096]{1,0:T(8,128)(2,1)}) custom-call(s32[2]{0:T(128)S(1)} %pad_add_fusion.place_ref, bf16[4,16,512]{2,1,0:T(8,128)(2,1)S(1)} %add_convert_fusion.mine_ref, bf16[4,16,512]{2,1,0:T(8,128)(2,1)S(1)} %collective-permute-done.12.theirs_ref, s32[4,256,512]{2,1,0:T(8,128)S(1)} %inverse_index.1.refs_10_.inverse_ref, ...), custom_call_target="tpu_custom_call" | custom-call | flops 805306368 | bytes 6291456 | tf_op jit(solution)/shard_map/decode/pallas_call | solution.py:271
  (2 shorter events, 0.1 us)
Async XLA Ops:
  0.6 17.3 %copy-start.2 = (s32[4,32,512]{2,1,0:T(8,128)S(1)}, s32[4,32,512]{2,1,0:T(8,128)}, u32[]{:S(2)}) copy-start(s32[4,32,512]{2,1,0:T(8,128)} %refs_9_.1) | copy-start | bytes 786436
  0.6 8.9 %collective-permute-start = (bf16[192,512]{1,0:T(8,128)(2,1)}, bf16[192,512]{1,0:T(8,128)(2,1)S(1)}, u32[]{:S(2)}, u32[]{:S(2)}) collective-permute-start(bf16[192,512]{1,0:T(8,128)(2,1)} %refs_4_.2), channel_id=1, source_target_pairs={{0,1},{1,0},{2,3},{3,2},{4,5},{5,4},{6,7},{7,6},{8,9},{9,8},{10,11... | collective-permute-start | bytes 589832 | tf_op jit(solution)/shard_map/ppermute | solution.py:309
  3.6 10.8 %collective-permute-start.1 = (bf16[192,512]{1,0:T(8,128)(2,1)}, bf16[192,512]{1,0:T(8,128)(2,1)S(1)}, u32[]{:S(2)}, u32[]{:S(2)}) collective-permute-start(bf16[192,512]{1,0:T(8,128)(2,1)} %refs_4_.2), channel_id=1, source_target_pairs={{0,2},{1,3},{2,0},{3,1},{4,6},{5,7},{6,4},{7,5},{8,10},{9,11},{10,... | collective-permute-start | bytes 589832 | tf_op jit(solution)/shard_map/ppermute | solution.py:309
  5.2 9.3 %collective-permute-start.2 = (bf16[192,512]{1,0:T(8,128)(2,1)}, bf16[192,512]{1,0:T(8,128)(2,1)S(1)}, u32[]{:S(2)}, u32[]{:S(2)}) collective-permute-start(bf16[192,512]{1,0:T(8,128)(2,1)} %refs_4_.2), channel_id=1, source_target_pairs={{0,3},{1,2},{2,1},{3,0},{4,7},{5,6},{6,5},{7,4},{8,11},{9,10},{10,... | collective-permute-start | bytes 589832 | tf_op jit(solution)/shard_map/ppermute | solution.py:309
  5.2 17.4 %copy-start.5 = (bf16[192,512]{1,0:T(8,128)(2,1)S(1)}, bf16[192,512]{1,0:T(8,128)(2,1)}, u32[]{:S(2)}) copy-start(bf16[192,512]{1,0:T(8,128)(2,1)} %refs_4_.2) | copy-start | bytes 589828
  5.2 17.4 %copy-start.8 = (bf16[1024,512]{1,0:T(8,128)(2,1)S(1)}, bf16[1024,512]{1,0:T(8,128)(2,1)}, u32[]{:S(2)}) copy-start(bf16[1024,512]{1,0:T(8,128)(2,1)} %refs_4_.1) | copy-start | bytes 3145732
  14.4 12.3 %collective-permute-start.3 = (bf16[192,1024]{1,0:T(8,128)(2,1)}, bf16[192,1024]{1,0:T(8,128)(2,1)S(1)}, u32[]{:S(2)}, u32[]{:S(2)}) collective-permute-start(bf16[192,1024]{1,0:T(8,128)(2,1)} %get-tuple-element.29), channel_id=1, source_target_pairs={{0,1},{1,0},{2,3},{3,2},{4,5},{5,4},{6,7},{7,6},{8,9},{9,8},{10,11... | collective-permute-start | bytes 1179656 | tf_op jit(solution)/shard_map/ppermute | solution.py:309
  15.7 20.2 %collective-permute-start.4 = (bf16[192,1024]{1,0:T(8,128)(2,1)}, bf16[192,1024]{1,0:T(8,128)(2,1)S(1)}, u32[]{:S(2)}, u32[]{:S(2)}) collective-permute-start(bf16[192,1024]{1,0:T(8,128)(2,1)} %get-tuple-element.30), channel_id=1, source_target_pairs={{0,2},{1,3},{2,0},{3,1},{4,6},{5,7},{6,4},{7,5},{8,10},{9,11},{10,... | collective-permute-start | bytes 1179656 | tf_op jit(solution)/shard_map/ppermute | solution.py:309
  16.5 19.6 %collective-permute-start.5 = (bf16[192,1024]{1,0:T(8,128)(2,1)}, bf16[192,1024]{1,0:T(8,128)(2,1)S(1)}, u32[]{:S(2)}, u32[]{:S(2)}) collective-permute-start(bf16[192,1024]{1,0:T(8,128)(2,1)} %get-tuple-element.31), channel_id=1, source_target_pairs={{0,3},{1,2},{2,1},{3,0},{4,7},{5,6},{6,5},{7,4},{8,11},{9,10},{10,... | collective-permute-start | bytes 1179656 | tf_op jit(solution)/shard_map/ppermute | solution.py:309
  17.9 18.2 %copy-start = (bf16[192,4096]{1,0:T(8,128)(2,1)S(1)}, bf16[192,4096]{1,0:T(8,128)(2,1)}, u32[]{:S(2)}) copy-start(bf16[192,4096]{1,0:T(8,128)(2,1)} %refs_0_.2) | copy-start | bytes 4718596
  17.9 18.2 %copy-start.1 = (f32[1,1024,512]{2,1,0:T(8,128)S(1)}, f32[1,1024,512]{2,1,0:T(8,128)}, u32[]{:S(2)}) copy-start(f32[1,1024,512]{2,1,0:T(8,128)} %refs_8_.1) | copy-start | bytes 6291460
  17.9 18.2 %copy-start.6 = (bf16[256,256]{1,0:T(8,128)(2,1)S(1)}, bf16[256,256]{1,0:T(8,128)(2,1)}, u32[]{:S(2)}) copy-start(bf16[256,256]{1,0:T(8,128)(2,1)} %constant.38.clone.refs_11_) | copy-start | bytes 393220
  17.9 18.2 %copy-start.7 = (bf16[256,256]{1,0:T(8,128)(2,1)S(1)}, bf16[256,256]{1,0:T(8,128)(2,1)}, u32[]{:S(2)}) copy-start(bf16[256,256]{1,0:T(8,128)(2,1)} %constant.39.clone.refs_12_) | copy-start | bytes 393220
  24.1 22.1 %collective-permute-start.10 = (bf16[192,1024]{1,0:T(8,128)(2,1)S(1)}, bf16[192,1024]{1,0:T(8,128)(2,1)S(1)}, u32[]{:S(2)}, u32[]{:S(2)}) collective-permute-start(bf16[192,1024]{1,0:T(8,128)(2,1)S(1)} %get-tuple-element.37), channel_id=1, source_target_pairs={{0,1},{1,0},{2,3},{3,2},{4,5},{5,4},{6,7},{7,6},{8,9},{9,8},{10,11... | collective-permute-start | bytes 1179656 | tf_op jit(solution)/shard_map/ppermute | solution.py:309
  25.4 21.6 %collective-permute-start.11 = (bf16[192,1024]{1,0:T(8,128)(2,1)S(1)}, bf16[192,1024]{1,0:T(8,128)(2,1)S(1)}, u32[]{:S(2)}, u32[]{:S(2)}) collective-permute-start(bf16[192,1024]{1,0:T(8,128)(2,1)S(1)} %get-tuple-element.38), channel_id=1, source_target_pairs={{0,2},{1,3},{2,0},{3,1},{4,6},{5,7},{6,4},{7,5},{8,10},{9,11},{10,... | collective-permute-start | bytes 1179656 | tf_op jit(solution)/shard_map/ppermute | solution.py:309
  36.1 10.8 %copy-start.3 = (bf16[256,256]{1,0:T(8,128)(2,1)S(1)}, bf16[256,256]{1,0:T(8,128)(2,1)}, u32[]{:S(2)}) copy-start(bf16[256,256]{1,0:T(8,128)(2,1)} %constant.40.clone.high_ref) | copy-start | bytes 393220
  36.2 10.8 %copy-start.4 = (bf16[256,256]{1,0:T(8,128)(2,1)S(1)}, bf16[256,256]{1,0:T(8,128)(2,1)}, u32[]{:S(2)}) copy-start(bf16[256,256]{1,0:T(8,128)(2,1)} %constant.41.clone.low_ref) | copy-start | bytes 393220
  41.2 1.3 %collective-permute-start.6 = (bf16[4,16,512]{2,1,0:T(8,128)(2,1)S(1)}, bf16[4,16,512]{2,1,0:T(8,128)(2,1)S(1)}, u32[]{:S(2)}, u32[]{:S(2)}) collective-permute-start(bf16[4,16,512]{2,1,0:T(8,128)(2,1)S(1)} %get-tuple-element.45), channel_id=1, source_target_pairs={{0,4},{4,0},{8,12},{12,8},{16,20},{20,16},{24,28},{28,24},{1,5},{5... | collective-permute-start | bytes 196616 | tf_op jit(solution)/shard_map/ppermute | solution.py:309
  41.2 12.4 %collective-permute-start.13 = (bf16[192,1024]{1,0:T(8,128)(2,1)S(1)}, bf16[192,1024]{1,0:T(8,128)(2,1)S(1)}, u32[]{:S(2)}, u32[]{:S(2)}) collective-permute-start(bf16[192,1024]{1,0:T(8,128)(2,1)S(1)} %get-tuple-element.39), channel_id=1, source_target_pairs={{0,3},{1,2},{2,1},{3,0},{4,7},{5,6},{6,5},{7,4},{8,11},{9,10},{10,... | collective-permute-start | bytes 1179656 | tf_op jit(solution)/shard_map/ppermute | solution.py:309
  42.5 7.0 %collective-permute-start.9 = (bf16[4,16,512]{2,1,0:T(8,128)(2,1)S(1)}, bf16[4,16,512]{2,1,0:T(8,128)(2,1)S(1)}, u32[]{:S(2)}, u32[]{:S(2)}) collective-permute-start(bf16[4,16,512]{2,1,0:T(8,128)(2,1)S(1)} %add_convert_fusion.1), channel_id=1, source_target_pairs={{0,24},{4,28},{8,16},{12,20},{16,8},{20,12},{24,0},{28,4},{1,25},{... | collective-permute-start | bytes 196616 | tf_op jit(solution)/shard_map/ppermute | solution.py:309
  46.2 5.9 %collective-permute-start.8 = (bf16[4,16,512]{2,1,0:T(8,128)(2,1)S(1)}, bf16[4,16,512]{2,1,0:T(8,128)(2,1)S(1)}, u32[]{:S(2)}, u32[]{:S(2)}) collective-permute-start(bf16[4,16,512]{2,1,0:T(8,128)(2,1)S(1)} %add_convert_fusion.1), channel_id=1, source_target_pairs={{0,16},{4,20},{8,24},{12,28},{16,0},{20,4},{24,8},{28,12},{1,17},{... | collective-permute-start | bytes 196616 | tf_op jit(solution)/shard_map/ppermute | solution.py:309
  46.2 5.9 %collective-permute-start.7 = (bf16[4,16,512]{2,1,0:T(8,128)(2,1)S(1)}, bf16[4,16,512]{2,1,0:T(8,128)(2,1)S(1)}, u32[]{:S(2)}, u32[]{:S(2)}) collective-permute-start(bf16[4,16,512]{2,1,0:T(8,128)(2,1)S(1)} %add_convert_fusion.1), channel_id=1, source_target_pairs={{0,8},{4,12},{8,0},{12,4},{16,24},{20,28},{24,16},{28,20},{1,9},{5... | collective-permute-start | bytes 196616 | tf_op jit(solution)/shard_map/ppermute | solution.py:309
  52.1 1.6 %collective-permute-start.12 = (bf16[4,16,512]{2,1,0:T(8,128)(2,1)S(1)}, bf16[4,16,512]{2,1,0:T(8,128)(2,1)S(1)}, u32[]{:S(2)}, u32[]{:S(2)}) collective-permute-start(bf16[4,16,512]{2,1,0:T(8,128)(2,1)S(1)} %add_convert_fusion.mine_ref), channel_id=1, source_target_pairs={{0,4},{4,0},{8,12},{12,8},{16,20},{20,16},{24,28},{28,24},{1,5},{5... | collective-permute-start | bytes 196616 | tf_op jit(solution)/shard_map/ppermute | solution.py:309

commit v3 on v2

--- a/solution.py
+++ b/solution.py
@@ -79,6 +79,43 @@
     )(positions)
 
 
+def cut_kernel(groups, place_ref, activations_ref, *refs):
+    pieces, sems = refs[: groups - 1], refs[groups - 1]
+    rows = pieces[0].shape[1]
+    copies = []
+    for m in range(1, groups):
+        at = pl.multiple_of((place_ref[0] ^ m) * rows, rows)
+        copies.append(
+            pltpu.make_async_copy(
+                activations_ref.at[:, pl.ds(at, rows)], pieces[m - 1], sems.at[m - 1]
+            )
+        )
+    for copy in copies:
+        copy.start()
+    for copy in copies:
+        copy.wait()
+
+
+def cut(place, activations, groups):
+    tokens, width = activations.shape
+    rows = width // groups
+    return pl.pallas_call(
+        functools.partial(cut_kernel, groups),
+        out_shape=[jax.ShapeDtypeStruct((tokens, rows), jnp.bfloat16)] * (groups - 1),
+        in_specs=[
+            pl.BlockSpec(memory_space=pltpu.SMEM),
+            pl.BlockSpec(memory_space=pltpu.HBM),
+        ],
+        out_specs=[pl.BlockSpec(memory_space=pltpu.VMEM)] * (groups - 1),
+        scratch_shapes=[pltpu.SemaphoreType.DMA((groups - 1,))],
+        compiler_params=params(),
+        cost_estimate=pl.CostEstimate(
+            flops=0, bytes_accessed=4 * (groups - 1) * tokens * rows, transcendentals=0
+        ),
+        name="cut",
+    )(place, activations)
+
+
 def outer_kernel(groups, *refs):
     weight_ref = refs[groups]
     for s in range(groups):
@@ -99,7 +136,7 @@
         out_shape=[jax.ShapeDtypeStruct((tokens, rows), jnp.bfloat16)] * groups,
         compiler_params=params(),
         cost_estimate=pl.CostEstimate(
-            flops=2 * groups * tokens * rows * outputs,
+            flops=40 * groups * tokens * rows * outputs,
             bytes_accessed=2 * (groups * tokens * (rows + outputs) + rows * outputs),
             transcendentals=0,
         ),
@@ -309,17 +346,19 @@
     return lax.ppermute(x, axis, [(s, s ^ mask) for s in range(size)])
 
 
-def sum_over_chips(x):
+def sum_over_chips(x, after):
     replicas = lax.axis_size("dp")
     stride = 2
     total = x
     while stride < replicas:
         sent = total.astype(jnp.bfloat16)
-        parts = [sent] + [swap(sent, "dp", stride * m) for m in (1, 2, 3) if stride * m < replicas]
+        masks = [stride * m for m in (1, 2, 3) if stride * m < replicas]
+        late, after = lax.optimization_barrier((sent, after)) if stride == 2 else (sent, after)
+        parts = [sent] + [swap(sent if m == masks[-1] else late, "dp", m) for m in masks]
         parts = [part.astype(jnp.float32) for part in parts]
         total = parts[0] + parts[1] if len(parts) == 2 else (parts[0] + parts[1]) + (parts[2] + parts[3])
         stride *= 4
-    return total.astype(jnp.bfloat16)
+    return total.astype(jnp.bfloat16), after
 
 
 def on_device(activations, cotangent, weight, momentum, positions):
@@ -331,10 +370,7 @@
 
     cotangents = [cotangent] + [swap(cotangent, "fsdp", m) for m in range(1, groups)]
     inverse = inverse_index(positions)
-    sent = [
-        lax.dynamic_slice_in_dim(activations, (index ^ m) * rows, rows, 1) for m in range(1, groups)
-    ]
-    sent, cotangents = lax.optimization_barrier((sent, cotangents))
+    sent = cut(place, activations, groups)
     inputs = [swap(sent[m - 1], "fsdp", m) for m in range(1, groups)]
     outer = input_gradients(cotangents, weight)
     inputs, inverse, _ = lax.optimization_barrier((inputs, inverse, outer))
@@ -344,9 +380,8 @@
         place, activations, inputs, cotangents, momentum, positions, inverse, high, low
     )
     chip = mine.astype(jnp.float32) + swap(theirs, "dp", 1).astype(jnp.float32)
-    moment, parts[1], parts[2] = lax.optimization_barrier((moment, parts[1], parts[2]))
     new_momentum = feedback(moment, masked, high.T, low.T)
-    summed = sum_over_chips(chip)
+    summed, parts[1:-1] = sum_over_chips(chip, parts[1:-1])
     summed, new_momentum = lax.optimization_barrier((summed, new_momentum))
     update, grad_input = decode(
         place, summed, swap(summed, "dp", 1), inverse, high.T, low.T, parts, replicas

time: 58 us -> 55.1 us (0.950)
  waiting for transfers between devices: 20.8 us -> 13.9 us
  starting transfers between devices: 16 us -> 19.3 us
  Pallas kernels: 17.7 us -> 18.4 us
    ppermute x14, waiting for transfers between devices: 20.8 us -> 13.9 us  [swap(): return lax.ppermute(x, axis, [(s, s ^ mask) for s in range(size)])]
    ppermute x14, starting transfers between devices: 16 us -> 19.3 us  [swap(): return lax.ppermute(x, axis, [(s, s ^ mask) for s in range(size)])]
    unnamed x18 -> x22, local copies, waits for them, and re-layouts: 0.04 us -> 2.41 us
    dynamic_slice x1 -> x0, local copies, waits for them, and re-layouts: 2.36 us -> none  [on_device(): lax.dynamic_slice_in_dim(activations, (index ^ m) * rows, rows, 1)]
    pallas_call x0 -> x1, Pallas kernels: none -> 0.69 us  [cut(): pl.pallas_call(functools.partial(cut_kernel, groups), out_shape=[jax.Shap...]
  transfers between devices with their start and end apart: 14 -> 14, of which waited for: 7 -> 4; matrix products, arithmetic and copies ran while one was open for 4% -> 0% of each run, Pallas kernels for 23% -> 26%
where the time goes in v3:
time: 55.1 us; the launch traced here: 54.9 us
  starting transfers between devices  19.3 us (35%)
  Pallas kernels  18.4 us (33%)
  waiting for transfers between devices  13.9 us (25%)
  local copies, waits for them, and re-layouts  2.41 us (4%)
  between operations  0.81 us (1%)
    ppermute x14, starting transfers between devices, swap(): return lax.ppermute(x, axis, [(s, s ^ mask) for s in range(size)])  19.3 us
    ppermute x14, waiting for transfers between devices, swap(): return lax.ppermute(x, axis, [(s, s ^ mask) for s in range(size)])  13.9 us
    pallas_call x1, Pallas kernels, moments(): pl.pallas_call(functools.partial(moment_kernel, groups), out_shape=[jax.S...  4.97 us
    pallas_call x1, Pallas kernels, inverse_index(): pl.pallas_call(inverse_index_kernel, out_shape=jax.ShapeDtypeStruct((bloc...  4.51 us
    pallas_call x1, Pallas kernels, decode(): pl.pallas_call(functools.partial(decode_kernel, replicas, groups), out_sh...  4.19 us
    pallas_call x1, Pallas kernels, feedback(): pl.pallas_call(feedback_kernel, out_shape=jax.ShapeDtypeStruct((1, rows,...  2.51 us
    unnamed x22, local copies, waits for them, and re-layouts  2.41 us
    pallas_call x1, Pallas kernels, input_gradients(): pl.pallas_call(functools.partial(outer_kernel, groups), out_shape=[jax.Sh...  1.55 us
  transfers between devices with their start and end apart: 14, of which 4 were waited for; matrix products, arithmetic and copies ran while one was open for 0% of the time, Pallas kernels for 26%

profile of v3, /device:TPU:0, one launch (start us, length us, event | category | flops | bytes accessed | tf_op | source)
XLA Modules:
  0.0 54.9 jit_solution(558352098583544506)
XLA Ops:
  0.6 4.0 %collective-permute-start.5 = (bf16[192,512]{1,0:T(8,128)(2,1)}, bf16[192,512]{1,0:T(8,128)(2,1)S(1)}, u32[]{:S(2)}, u32[]{:S(2)}) collective-permute-start(bf16[192,512]{1,0:T(8,128)(2,1)} %refs_4_.3), channel_id=1, source_target_pairs={{0,3},{1,2},{2,1},{3,0},{4,7},{5,6},{6,5},{7,4},{8,11},{9,10},{10,... | collective-permute-start | bytes 589832 | tf_op jit(solution)/shard_map/ppermute | solution.py:346
  4.6 0.5 collective-permute-start.4
  5.1 0.1 collective-permute-start.3
  5.2 0.1 pad_add_fusion.place_ref
  5.3 0.0 copy-start
  5.3 1.4 %copy-done = bf16[192,4096]{1,0:T(8,128)(2,1)S(1)} copy-done((bf16[192,4096]{1,0:T(8,128)(2,1)S(1)}, bf16[192,4096]{1,0:T(8,128)(2,1)}, u32[]{:S(2)}) %copy-start) | copy-done | bytes 1572888
  6.7 0.0 copy-start.7
  6.7 0.0 copy-start.10
  6.7 0.7 %cut.1 = (bf16[192,1024]{1,0:T(8,128)(2,1)S(1)}, bf16[192,1024]{1,0:T(8,128)(2,1)S(1)}, bf16[192,1024]{1,0:T(8,128)(2,1)S(1)}) custom-call(s32[2]{0:T(128)S(1)} %pad_add_fusion.place_ref, bf16[192,4096]{1,0:T(8,128)(2,1)S(1)} %copy-done), custom_call_target="tpu_custom_call" | custom-call | bytes 2359296 | tf_op jit(solution)/shard_map/cut/pallas_call | solution.py:102
  7.4 2.0 %collective-permute-start = (bf16[192,1024]{1,0:T(8,128)(2,1)S(1)}, bf16[192,1024]{1,0:T(8,128)(2,1)S(1)}, u32[]{:S(2)}, u32[]{:S(2)}) collective-permute-start(bf16[192,1024]{1,0:T(8,128)(2,1)S(1)} %get-tuple-element.25), channel_id=1, source_target_pairs={{0,1},{1,0},{2,3},{3,2},{4,5},{5,4},{6,7},{7,6},{8,9},{9,8},{10,11... | collective-permute-start | bytes 1179656 | tf_op jit(solution)/shard_map/ppermute | solution.py:346
  9.4 1.5 %collective-permute-start.1 = (bf16[192,1024]{1,0:T(8,128)(2,1)S(1)}, bf16[192,1024]{1,0:T(8,128)(2,1)S(1)}, u32[]{:S(2)}, u32[]{:S(2)}) collective-permute-start(bf16[192,1024]{1,0:T(8,128)(2,1)S(1)} %get-tuple-element.26), channel_id=1, source_target_pairs={{0,2},{1,3},{2,0},{3,1},{4,6},{5,7},{6,4},{7,5},{8,10},{9,11},{10,... | collective-permute-start | bytes 1179656 | tf_op jit(solution)/shard_map/ppermute | solution.py:346
  10.9 0.0 copy-start.3
  10.9 0.9 %copy-done.3 = s32[4,32,512]{2,1,0:T(8,128)S(1)} copy-done((s32[4,32,512]{2,1,0:T(8,128)S(1)}, s32[4,32,512]{2,1,0:T(8,128)}, u32[]{:S(2)}) %copy-start.3) | copy-done | bytes 262168
  11.8 4.5 %inverse_index.1.refs_10_.inverse_ref = s32[4,256,512]{2,1,0:T(8,128)S(1)} custom-call(s32[4,32,512]{2,1,0:T(8,128)S(1)} %copy-done.3), custom_call_target="tpu_custom_call" | custom-call | flops 33554432 | bytes 2097152 | tf_op jit(solution)/shard_map/inverse_index/pallas_call | solution.py:66
  16.4 0.0 collective-permute-done.5.refs_3_.refs_7_
  16.4 0.0 copy-start.1
  16.4 0.0 copy-start.2
  16.4 0.0 copy-start.4
  16.4 0.0 copy-start.8
  16.4 0.0 copy-start.9
  16.4 0.1 collective-permute-start.2
  16.6 0.0 collective-permute-done.4.refs_2_.refs_6_
  16.6 0.0 collective-permute-done.3.refs_1_.refs_5_
  16.6 0.0 copy-done.7
  16.6 0.0 copy-done.10
  16.6 1.5 %input_gradients.1 = (bf16[192,1024]{1,0:T(8,128)(2,1)S(1)}, bf16[192,1024]{1,0:T(8,128)(2,1)S(1)}, bf16[192,1024]{1,0:T(8,128)(2,1)S(1)}, bf16[192,1024]{1,0:T(8,128)(2,1)S(1)}) custom-call(bf16[192,512]{1,0:T(8,128)(2,1)S(1)} %copy-done.7, bf16[192,512]{1,0:T(8,128)(2,1)S(1)} %collective-permute-done.3.refs_1_.refs_5_, ...), custom_call_target="tpu_custom_call" | custom-call | flops 16106127360 | bytes 3407872 | tf_op jit(solution)/shard_map/input_gradients/pallas_call | solution.py:134
  18.2 2.0 %collective-permute-start.7 = (bf16[192,1024]{1,0:T(8,128)(2,1)S(1)}, bf16[192,1024]{1,0:T(8,128)(2,1)S(1)}, u32[]{:S(2)}, u32[]{:S(2)}) collective-permute-start(bf16[192,1024]{1,0:T(8,128)(2,1)S(1)} %get-tuple-element.29), channel_id=1, source_target_pairs={{0,1},{1,0},{2,3},{3,2},{4,5},{5,4},{6,7},{7,6},{8,9},{9,8},{10,11... | collective-permute-start | bytes 1179656 | tf_op jit(solution)/shard_map/ppermute | solution.py:346
  20.1 1.5 %collective-permute-start.8 = (bf16[192,1024]{1,0:T(8,128)(2,1)S(1)}, bf16[192,1024]{1,0:T(8,128)(2,1)S(1)}, u32[]{:S(2)}, u32[]{:S(2)}) collective-permute-start(bf16[192,1024]{1,0:T(8,128)(2,1)S(1)} %get-tuple-element.30), channel_id=1, source_target_pairs={{0,2},{1,3},{2,0},{3,1},{4,6},{5,7},{6,4},{7,5},{8,10},{9,11},{10,... | collective-permute-start | bytes 1179656 | tf_op jit(solution)/shard_map/ppermute | solution.py:346
  21.6 2.1 %collective-permute-done.refs_1_ = bf16[192,1024]{1,0:T(8,128)(2,1)S(1)} collective-permute-done((bf16[192,1024]{1,0:T(8,128)(2,1)S(1)}, bf16[192,1024]{1,0:T(8,128)(2,1)S(1)}, u32[]{:S(2)}, u32[]{:S(2)}) %collective-permute-start) | collective-permute-done | bytes 393248 | tf_op jit(solution)/shard_map/ppermute | solution.py:346
  23.8 0.0 collective-permute-done.1.refs_2_
  23.8 7.9 %collective-permute-done.2.refs_3_ = bf16[192,1024]{1,0:T(8,128)(2,1)S(1)} collective-permute-done((bf16[192,1024]{1,0:T(8,128)(2,1)S(1)}, bf16[192,1024]{1,0:T(8,128)(2,1)S(1)}, u32[]{:S(2)}, u32[]{:S(2)}) %collective-permute-start.2) | collective-permute-done | bytes 393248 | tf_op jit(solution)/shard_map/ppermute | solution.py:346
  31.7 0.0 copy-done.1
  31.7 0.0 copy-done.2
  31.7 0.0 copy-done.4
  31.7 0.0 copy-done.8
  31.7 0.0 copy-done.9
  31.7 0.0 copy-start.5
  31.7 0.0 copy-start.6
  31.7 5.0 %moment.1 = (f32[1024,512]{1,0:T(8,128)S(1)}, bf16[1024,512]{1,0:T(8,128)(2,1)S(1)}, bf16[4,16,512]{2,1,0:T(8,128)(2,1)S(1)}, bf16[4,16,512]{2,1,0:T(8,128)(2,1)S(1)}) custom-call(s32[2]{0:T(128)S(1)} %pad_add_fusion.place_ref, bf16[192,4096]{1,0:T(8,128)(2,1)S(1)} %copy-done.1, bf16[192,1024]{1,0:T(8,128)(2,1)S(1)} %collective-permute-done.refs_1_, ...), custom_call_target="tpu_custom_call" | custom-call | flops 1610612736 | bytes 8912896 | tf_op jit(solution)/shard_map/moment/pallas_call | solution.py:194
  36.7 0.1 collective-permute-start.6
  36.8 3.0 %collective-permute-start.13 = (bf16[192,1024]{1,0:T(8,128)(2,1)S(1)}, bf16[192,1024]{1,0:T(8,128)(2,1)S(1)}, u32[]{:S(2)}, u32[]{:S(2)}) collective-permute-start(bf16[192,1024]{1,0:T(8,128)(2,1)S(1)} %get-tuple-element.31), channel_id=1, source_target_pairs={{0,3},{1,2},{2,1},{3,0},{4,7},{5,6},{6,5},{7,4},{8,11},{9,10},{10,... | collective-permute-start | bytes 1179656 | tf_op jit(solution)/shard_map/ppermute | solution.py:346
  39.8 0.0 collective-permute-done.6
  39.8 3.7 %collective-permute-start.11 = (bf16[4,16,512]{2,1,0:T(8,128)(2,1)S(1)}, bf16[4,16,512]{2,1,0:T(8,128)(2,1)S(1)}, u32[]{:S(2)}, u32[]{:S(2)}) collective-permute-start(bf16[4,16,512]{2,1,0:T(8,128)(2,1)S(1)} %add_convert_fusion.1), channel_id=1, source_target_pairs={{0,24},{4,28},{8,16},{12,20},{16,8},{20,12},{24,0},{28,4},{1,25},{... | collective-permute-start | bytes 196616 | tf_op jit(solution)/shard_map/ppermute | solution.py:346
  43.5 0.0 collective-permute-done.7.refs_1_
  43.5 0.0 collective-permute-done.8.refs_2_
  43.5 0.0 collective-permute-start.10
  43.5 0.8 %collective-permute-start.9 = (bf16[4,16,512]{2,1,0:T(8,128)(2,1)S(1)}, bf16[4,16,512]{2,1,0:T(8,128)(2,1)S(1)}, u32[]{:S(2)}, u32[]{:S(2)}) collective-permute-start(bf16[4,16,512]{2,1,0:T(8,128)(2,1)S(1)} %add_convert_fusion.1), channel_id=1, source_target_pairs={{0,8},{4,12},{8,0},{12,4},{16,24},{20,28},{24,16},{28,20},{1,9},{5... | collective-permute-start | bytes 196616 | tf_op jit(solution)/shard_map/ppermute | solution.py:346
  44.3 0.0 copy-done.5
  44.3 0.0 copy-done.6
  44.3 2.5 %feedback.1 = f32[1,1024,512]{2,1,0:T(8,128)} custom-call(f32[1024,512]{1,0:T(8,128)S(1)} %get-tuple-element.39.moment_ref, bf16[1024,512]{1,0:T(8,128)(2,1)S(1)} %get-tuple-element.40.masked_ref, bf16[256,256]{1,0:T(8,128)(2,1)S(1)} %copy-done.6, bf16[256,256]{1,0:T(8,128)(2,1)S(1)} %copy-done.5), custom_call_target="tpu_custom_call" | custom-call | flops 536870912 | bytes 5242880 | tf_op jit(solution)/shard_map/feedback/pallas_call | solution.py:241
  46.8 0.0 collective-permute-done.11
  46.8 2.6 %collective-permute-done.10 = bf16[4,16,512]{2,1,0:T(8,128)(2,1)S(1)} collective-permute-done((bf16[4,16,512]{2,1,0:T(8,128)(2,1)S(1)}, bf16[4,16,512]{2,1,0:T(8,128)(2,1)S(1)}, u32[]{:S(2)}, u32[]{:S(2)}) %collective-permute-start.10) | collective-permute-done | bytes 65568 | tf_op jit(solution)/shard_map/ppermute | solution.py:346
  49.4 0.0 collective-permute-done.9
  49.4 0.1 collective-permute-start.12
  49.5 0.0 collective-permute-done.13.refs_3_
  49.5 1.2 %collective-permute-done.12.theirs_ref = bf16[4,16,512]{2,1,0:T(8,128)(2,1)S(1)} collective-permute-done((bf16[4,16,512]{2,1,0:T(8,128)(2,1)S(1)}, bf16[4,16,512]{2,1,0:T(8,128)(2,1)S(1)}, u32[]{:S(2)}, u32[]{:S(2)}) %collective-permute-start.12) | collective-permute-done | bytes 65568 | tf_op jit(solution)/shard_map/ppermute | solution.py:346
  50.7 4.2 %decode.1 = (bf16[1024,512]{1,0:T(8,128)(2,1)}, bf16[192,4096]{1,0:T(8,128)(2,1)}) custom-call(s32[2]{0:T(128)S(1)} %pad_add_fusion.place_ref, bf16[4,16,512]{2,1,0:T(8,128)(2,1)S(1)} %add_convert_fusion.mine_ref, bf16[4,16,512]{2,1,0:T(8,128)(2,1)S(1)} %collective-permute-done.12.theirs_ref, s32[4,256,512]{2,1,0:T(8,128)S(1)} %inverse_index.1.refs_10_.inverse_ref, ...), custom_call_target="tpu_custom_call" | custom-call | flops 805306368 | bytes 6291456 | tf_op jit(solution)/shard_map/decode/pallas_call | solution.py:308
  (2 shorter events, 0.1 us)
Async XLA Ops:
  0.6 15.7 %collective-permute-start.5 = (bf16[192,512]{1,0:T(8,128)(2,1)}, bf16[192,512]{1,0:T(8,128)(2,1)S(1)}, u32[]{:S(2)}, u32[]{:S(2)}) collective-permute-start(bf16[192,512]{1,0:T(8,128)(2,1)} %refs_4_.3), channel_id=1, source_target_pairs={{0,3},{1,2},{2,1},{3,0},{4,7},{5,6},{6,5},{7,4},{8,11},{9,10},{10,... | collective-permute-start | bytes 589832 | tf_op jit(solution)/shard_map/ppermute | solution.py:346
  4.6 12.0 %collective-permute-start.4 = (bf16[192,512]{1,0:T(8,128)(2,1)}, bf16[192,512]{1,0:T(8,128)(2,1)S(1)}, u32[]{:S(2)}, u32[]{:S(2)}) collective-permute-start(bf16[192,512]{1,0:T(8,128)(2,1)} %refs_4_.3), channel_id=1, source_target_pairs={{0,2},{1,3},{2,0},{3,1},{4,6},{5,7},{6,4},{7,5},{8,10},{9,11},{10,... | collective-permute-start | bytes 589832 | tf_op jit(solution)/shard_map/ppermute | solution.py:346
  5.1 11.5 %collective-permute-start.3 = (bf16[192,512]{1,0:T(8,128)(2,1)}, bf16[192,512]{1,0:T(8,128)(2,1)S(1)}, u32[]{:S(2)}, u32[]{:S(2)}) collective-permute-start(bf16[192,512]{1,0:T(8,128)(2,1)} %refs_4_.3), channel_id=1, source_target_pairs={{0,1},{1,0},{2,3},{3,2},{4,5},{5,4},{6,7},{7,6},{8,9},{9,8},{10,11... | collective-permute-start | bytes 589832 | tf_op jit(solution)/shard_map/ppermute | solution.py:346
  5.3 1.4 %copy-start = (bf16[192,4096]{1,0:T(8,128)(2,1)S(1)}, bf16[192,4096]{1,0:T(8,128)(2,1)}, u32[]{:S(2)}) copy-start(bf16[192,4096]{1,0:T(8,128)(2,1)} %refs_0_.3) | copy-start | bytes 4718596
  6.7 9.9 %copy-start.7 = (bf16[192,512]{1,0:T(8,128)(2,1)S(1)}, bf16[192,512]{1,0:T(8,128)(2,1)}, u32[]{:S(2)}) copy-start(bf16[192,512]{1,0:T(8,128)(2,1)} %refs_4_.3) | copy-start | bytes 589828
  6.7 9.9 %copy-start.10 = (bf16[1024,512]{1,0:T(8,128)(2,1)S(1)}, bf16[1024,512]{1,0:T(8,128)(2,1)}, u32[]{:S(2)}) copy-start(bf16[1024,512]{1,0:T(8,128)(2,1)} %refs_4_.2) | copy-start | bytes 3145732
  7.4 16.4 %collective-permute-start = (bf16[192,1024]{1,0:T(8,128)(2,1)S(1)}, bf16[192,1024]{1,0:T(8,128)(2,1)S(1)}, u32[]{:S(2)}, u32[]{:S(2)}) collective-permute-start(bf16[192,1024]{1,0:T(8,128)(2,1)S(1)} %get-tuple-element.25), channel_id=1, source_target_pairs={{0,1},{1,0},{2,3},{3,2},{4,5},{5,4},{6,7},{7,6},{8,9},{9,8},{10,11... | collective-permute-start | bytes 1179656 | tf_op jit(solution)/shard_map/ppermute | solution.py:346
  9.4 14.4 %collective-permute-start.1 = (bf16[192,1024]{1,0:T(8,128)(2,1)S(1)}, bf16[192,1024]{1,0:T(8,128)(2,1)S(1)}, u32[]{:S(2)}, u32[]{:S(2)}) collective-permute-start(bf16[192,1024]{1,0:T(8,128)(2,1)S(1)} %get-tuple-element.26), channel_id=1, source_target_pairs={{0,2},{1,3},{2,0},{3,1},{4,6},{5,7},{6,4},{7,5},{8,10},{9,11},{10,... | collective-permute-start | bytes 1179656 | tf_op jit(solution)/shard_map/ppermute | solution.py:346
  10.9 0.9 %copy-start.3 = (s32[4,32,512]{2,1,0:T(8,128)S(1)}, s32[4,32,512]{2,1,0:T(8,128)}, u32[]{:S(2)}) copy-start(s32[4,32,512]{2,1,0:T(8,128)} %refs_9_.1) | copy-start | bytes 786436
  16.4 15.3 %copy-start.1 = (bf16[192,4096]{1,0:T(8,128)(2,1)S(1)}, bf16[192,4096]{1,0:T(8,128)(2,1)}, u32[]{:S(2)}) copy-start(bf16[192,4096]{1,0:T(8,128)(2,1)} %refs_0_.3) | copy-start | bytes 4718596
  16.4 15.3 %copy-start.2 = (f32[1,1024,512]{2,1,0:T(8,128)S(1)}, f32[1,1024,512]{2,1,0:T(8,128)}, u32[]{:S(2)}) copy-start(f32[1,1024,512]{2,1,0:T(8,128)} %refs_8_.1) | copy-start | bytes 6291460
  16.4 15.3 %copy-start.4 = (s32[4,32,512]{2,1,0:T(8,128)S(1)}, s32[4,32,512]{2,1,0:T(8,128)}, u32[]{:S(2)}) copy-start(s32[4,32,512]{2,1,0:T(8,128)} %refs_9_.1) | copy-start | bytes 786436
  16.4 15.3 %copy-start.8 = (bf16[256,256]{1,0:T(8,128)(2,1)S(1)}, bf16[256,256]{1,0:T(8,128)(2,1)}, u32[]{:S(2)}) copy-start(bf16[256,256]{1,0:T(8,128)(2,1)} %constant.31.clone.refs_12_) | copy-start | bytes 393220
  16.4 15.3 %copy-start.9 = (bf16[256,256]{1,0:T(8,128)(2,1)S(1)}, bf16[256,256]{1,0:T(8,128)(2,1)}, u32[]{:S(2)}) copy-start(bf16[256,256]{1,0:T(8,128)(2,1)} %constant.30.clone.refs_11_) | copy-start | bytes 393220
  16.4 15.3 %collective-permute-start.2 = (bf16[192,1024]{1,0:T(8,128)(2,1)S(1)}, bf16[192,1024]{1,0:T(8,128)(2,1)S(1)}, u32[]{:S(2)}, u32[]{:S(2)}) collective-permute-start(bf16[192,1024]{1,0:T(8,128)(2,1)S(1)} %get-tuple-element.27), channel_id=1, source_target_pairs={{0,3},{1,2},{2,1},{3,0},{4,7},{5,6},{6,5},{7,4},{8,11},{9,10},{10,... | collective-permute-start | bytes 1179656 | tf_op jit(solution)/shard_map/ppermute | solution.py:346
  18.2 25.3 %collective-permute-start.7 = (bf16[192,1024]{1,0:T(8,128)(2,1)S(1)}, bf16[192,1024]{1,0:T(8,128)(2,1)S(1)}, u32[]{:S(2)}, u32[]{:S(2)}) collective-permute-start(bf16[192,1024]{1,0:T(8,128)(2,1)S(1)} %get-tuple-element.29), channel_id=1, source_target_pairs={{0,1},{1,0},{2,3},{3,2},{4,5},{5,4},{6,7},{7,6},{8,9},{9,8},{10,11... | collective-permute-start | bytes 1179656 | tf_op jit(solution)/shard_map/ppermute | solution.py:346
  20.1 23.4 %collective-permute-start.8 = (bf16[192,1024]{1,0:T(8,128)(2,1)S(1)}, bf16[192,1024]{1,0:T(8,128)(2,1)S(1)}, u32[]{:S(2)}, u32[]{:S(2)}) collective-permute-start(bf16[192,1024]{1,0:T(8,128)(2,1)S(1)} %get-tuple-element.30), channel_id=1, source_target_pairs={{0,2},{1,3},{2,0},{3,1},{4,6},{5,7},{6,4},{7,5},{8,10},{9,11},{10,... | collective-permute-start | bytes 1179656 | tf_op jit(solution)/shard_map/ppermute | solution.py:346
  31.7 12.6 %copy-start.5 = (bf16[256,256]{1,0:T(8,128)(2,1)S(1)}, bf16[256,256]{1,0:T(8,128)(2,1)}, u32[]{:S(2)}) copy-start(bf16[256,256]{1,0:T(8,128)(2,1)} %constant.33.clone.low_ref) | copy-start | bytes 393220
  31.7 12.5 %copy-start.6 = (bf16[256,256]{1,0:T(8,128)(2,1)S(1)}, bf16[256,256]{1,0:T(8,128)(2,1)}, u32[]{:S(2)}) copy-start(bf16[256,256]{1,0:T(8,128)(2,1)} %constant.32.clone.high_ref) | copy-start | bytes 393220
  36.7 3.1 %collective-permute-start.6 = (bf16[4,16,512]{2,1,0:T(8,128)(2,1)S(1)}, bf16[4,16,512]{2,1,0:T(8,128)(2,1)S(1)}, u32[]{:S(2)}, u32[]{:S(2)}) collective-permute-start(bf16[4,16,512]{2,1,0:T(8,128)(2,1)S(1)} %get-tuple-element.37), channel_id=1, source_target_pairs={{0,4},{4,0},{8,12},{12,8},{16,20},{20,16},{24,28},{28,24},{1,5},{5... | collective-permute-start | bytes 196616 | tf_op jit(solution)/shard_map/ppermute | solution.py:346
  36.8 12.7 %collective-permute-start.13 = (bf16[192,1024]{1,0:T(8,128)(2,1)S(1)}, bf16[192,1024]{1,0:T(8,128)(2,1)S(1)}, u32[]{:S(2)}, u32[]{:S(2)}) collective-permute-start(bf16[192,1024]{1,0:T(8,128)(2,1)S(1)} %get-tuple-element.31), channel_id=1, source_target_pairs={{0,3},{1,2},{2,1},{3,0},{4,7},{5,6},{6,5},{7,4},{8,11},{9,10},{10,... | collective-permute-start | bytes 1179656 | tf_op jit(solution)/shard_map/ppermute | solution.py:346
  39.8 7.0 %collective-permute-start.11 = (bf16[4,16,512]{2,1,0:T(8,128)(2,1)S(1)}, bf16[4,16,512]{2,1,0:T(8,128)(2,1)S(1)}, u32[]{:S(2)}, u32[]{:S(2)}) collective-permute-start(bf16[4,16,512]{2,1,0:T(8,128)(2,1)S(1)} %add_convert_fusion.1), channel_id=1, source_target_pairs={{0,24},{4,28},{8,16},{12,20},{16,8},{20,12},{24,0},{28,4},{1,25},{... | collective-permute-start | bytes 196616 | tf_op jit(solution)/shard_map/ppermute | solution.py:346
  43.5 5.9 %collective-permute-start.10 = (bf16[4,16,512]{2,1,0:T(8,128)(2,1)S(1)}, bf16[4,16,512]{2,1,0:T(8,128)(2,1)S(1)}, u32[]{:S(2)}, u32[]{:S(2)}) collective-permute-start(bf16[4,16,512]{2,1,0:T(8,128)(2,1)S(1)} %add_convert_fusion.1), channel_id=1, source_target_pairs={{0,16},{4,20},{8,24},{12,28},{16,0},{20,4},{24,8},{28,12},{1,17},{... | collective-permute-start | bytes 196616 | tf_op jit(solution)/shard_map/ppermute | solution.py:346
  43.5 5.9 %collective-permute-start.9 = (bf16[4,16,512]{2,1,0:T(8,128)(2,1)S(1)}, bf16[4,16,512]{2,1,0:T(8,128)(2,1)S(1)}, u32[]{:S(2)}, u32[]{:S(2)}) collective-permute-start(bf16[4,16,512]{2,1,0:T(8,128)(2,1)S(1)} %add_convert_fusion.1), channel_id=1, source_target_pairs={{0,8},{4,12},{8,0},{12,4},{16,24},{20,28},{24,16},{28,20},{1,9},{5... | collective-permute-start | bytes 196616 | tf_op jit(solution)/shard_map/ppermute | solution.py:346
  49.4 1.3 %collective-permute-start.12 = (bf16[4,16,512]{2,1,0:T(8,128)(2,1)S(1)}, bf16[4,16,512]{2,1,0:T(8,128)(2,1)S(1)}, u32[]{:S(2)}, u32[]{:S(2)}) collective-permute-start(bf16[4,16,512]{2,1,0:T(8,128)(2,1)S(1)} %add_convert_fusion.mine_ref), channel_id=1, source_target_pairs={{0,4},{4,0},{8,12},{12,8},{16,20},{20,16},{24,28},{28,24},{1,5},{5... | collective-permute-start | bytes 196616 | tf_op jit(solution)/shard_map/ppermute | solution.py:346

commit v4 on v3

v4 whole, which is shorter than its diff:
```python
import functools

import jax
import jax.numpy as jnp
import numpy as np
from jax import lax
from jax.experimental import pallas as pl
from jax.experimental.pallas import tpu as pltpu
from jax.sharding import PartitionSpec as P

SPAN = 256
MOMENTUM_DECAY = 0.999
LANES = 128
SUBLANES = 8
VMEM_LIMIT = 16 * 1024 * 1024


def transform_table():
    freq = np.arange(SPAN, dtype=np.float64)[:, None]
    place = np.arange(SPAN, dtype=np.float64)[None, :]
    scales = np.where(freq == 0.0, np.sqrt(1.0 / SPAN), np.sqrt(2.0 / SPAN))
    table = scales * np.cos(np.pi * (2.0 * place + 1.0) * freq / (2.0 * SPAN))
    high = table.astype(jnp.bfloat16)
    low = (table - high.astype(np.float64)).astype(jnp.bfloat16)
    return high, low


def two_terms(x):
    high = x.astype(jnp.bfloat16)
    return high, (x - high.astype(jnp.float32)).astype(jnp.bfloat16)


def dot(left, right):
    return jnp.dot(left, right, preferred_element_type=jnp.float32)


def split_dot(table_high, table_low, x):
    high, low = two_terms(x)
    return dot(table_high, high) + (dot(table_high, low) + dot(table_low, high))


def params(**more):
    return pltpu.CompilerParams(vmem_limit_bytes=VMEM_LIMIT, **more)


def inverse_index_kernel(positions_ref, inverse_ref):
    blocks, picks, columns = positions_ref.shape
    chunk = 64
    per_block = SPAN // chunk

    def one_chunk(at, carry):
        b = at // per_block
        start = pl.multiple_of((at % per_block) * chunk, chunk)
        for c in range(0, columns, LANES):
            where = positions_ref[b, :, c : c + LANES]
            level = lax.broadcasted_iota(jnp.int32, (chunk, LANES), 0) + start
            found = jnp.full((chunk, LANES), -1, jnp.int32)
            for i in range(picks):
                found = jnp.where(where[i : i + 1, :] == level, i, found)
            inverse_ref[b, pl.ds(start, chunk), c : c + LANES] = found
        return carry

    lax.fori_loop(0, blocks * per_block, one_chunk, 0)


def inverse_index(positions):
    blocks, picks, columns = positions.shape
    return pl.pallas_call(
        inverse_index_kernel,
        out_shape=jax.ShapeDtypeStruct((blocks, SPAN, columns), jnp.int32),
        compiler_params=params(),
        cost_estimate=pl.CostEstimate(
            flops=2 * blocks * picks * SPAN * columns,
            bytes_accessed=4 * blocks * SPAN * columns,
            transcendentals=0,
        ),
        name="inverse_index",
    )(positions)


def cut_kernel(groups, place_ref, activations_ref, *refs):
    pieces, sems = refs[: groups - 1], refs[groups - 1]
    rows = pieces[0].shape[1]
    copies = []
    for m in range(1, groups):
        at = pl.multiple_of((place_ref[0] ^ m) * rows, rows)
        copies.append(
            pltpu.make_async_copy(
                activations_ref.at[:, pl.ds(at, rows)], pieces[m - 1], sems.at[m - 1]
            )
        )
    for copy in copies:
        copy.start()
    for copy in copies:
        copy.wait()


def cut(place, activations, groups):
    tokens, width = activations.shape
    rows = width // groups
    return pl.pallas_call(
        functools.partial(cut_kernel, groups),
        out_shape=[jax.ShapeDtypeStruct((tokens, rows), jnp.bfloat16)] * (groups - 1),
        in_specs=[
            pl.BlockSpec(memory_space=pltpu.SMEM),
            pl.BlockSpec(memory_space=pltpu.HBM),
        ],
        out_specs=[pl.BlockSpec(memory_space=pltpu.VMEM)] * (groups - 1),
        scratch_shapes=[pltpu.SemaphoreType.DMA((groups - 1,))],
        compiler_params=params(),
        cost_estimate=pl.CostEstimate(
            flops=0, bytes_accessed=4 * (groups - 1) * tokens * rows, transcendentals=0
        ),
        name="cut",
    )(place, activations)


def outer(cotangent, weight):
    return lax.dot_general(
        cotangent, weight, (((1,), (1,)), ((), ())), preferred_element_type=jnp.float32
    ).astype(jnp.bfloat16)


def outer_kernel(groups, *refs):
    weight_ref = refs[groups]
    for s in range(groups):
        refs[groups + 1 + s][...] = outer(refs[s][...], weight_ref[...])


def input_gradients(cotangents, weight):
    tokens, outputs = cotangents[0].shape
    rows = weight.shape[0]
    groups = len(cotangents)
    return pl.pallas_call(
        functools.partial(outer_kernel, groups),
        out_shape=[jax.ShapeDtypeStruct((tokens, rows), jnp.bfloat16)] * groups,
        in_specs=[pl.BlockSpec(memory_space=pltpu.VMEM)] * (groups + 1),
        out_specs=[pl.BlockSpec(memory_space=pltpu.VMEM)] * groups,
        compiler_params=params(),
        cost_estimate=pl.CostEstimate(
            flops=40 * groups * tokens * rows * outputs,
            bytes_accessed=2 * (groups * tokens * (rows + outputs) + rows * outputs),
            transcendentals=0,
        ),
        name="input_gradients",
    )(*cotangents, weight)


def across_tokens(left, right):
    return lax.dot_general(
        left, right, (((0,), (0,)), ((), ())), preferred_element_type=jnp.float32
    )


def early_kernel(groups, place_ref, *refs):
    inputs, cotangents = refs[:groups], refs[groups : 2 * groups]
    momentum_ref, high_ref, low_ref, moment_ref, coeffs_ref = refs[2 * groups :]
    blocks = moment_ref.shape[0] // SPAN
    for b in range(blocks):
        rows = slice(b * SPAN, (b + 1) * SPAN)
        own = pl.ds(pl.multiple_of((place_ref[0] * blocks + b) * SPAN, SPAN), SPAN)
        moment = MOMENTUM_DECAY * momentum_ref[0, rows, :]
        for s in range(groups):
            held = inputs[s][:, own if s == 0 else rows]
            moment = moment + across_tokens(held, cotangents[s][...])
        moment_ref[rows, :] = moment
        coeffs_ref[rows, :] = split_dot(high_ref[...], low_ref[...], moment)


def early_moments(place, activations, inputs, cotangents, momentum, high, low):
    groups = len(cotangents)
    tokens = cotangents[0].shape[0]
    _, rows, columns = momentum.shape
    return pl.pallas_call(
        functools.partial(early_kernel, groups),
        out_shape=[jax.ShapeDtypeStruct((rows, columns), jnp.float32)] * 2,
        in_specs=[pl.BlockSpec(memory_space=pltpu.SMEM)]
        + [pl.BlockSpec(memory_space=pltpu.VMEM)] * (2 * groups + 3),
        out_specs=[pl.BlockSpec(memory_space=pltpu.VMEM)] * 2,
        compiler_params=params(),
        cost_estimate=pl.CostEstimate(
            flops=2 * rows * columns * (groups * tokens + 3 * SPAN),
            bytes_accessed=rows * (groups * tokens * 2 + 12 * columns),
            transcendentals=0,
        ),
        name="early_moment",
    )(place, activations, *inputs, *cotangents, momentum, high, low)


def moment_kernel(groups, place_ref, *refs):
    inputs, cotangents = refs[:groups], refs[groups : 2 * groups - 1]
    (
        lower_ref,
        upper_ref,
        weight_ref,
        early_ref,
        early_coeffs_ref,
        positions_ref,
        high_ref,
        low_ref,
        moment_ref,
        coeffs_ref,
        mine_ref,
        theirs_ref,
        far_part_ref,
        far_ref,
    ) = refs[2 * groups - 1 :]
    token_half = lower_ref.shape[0]
    far_ref[:token_half, :] = lower_ref[...]
    far_ref[token_half:, :] = upper_ref[...]
    cotangents = (*cotangents, far_ref)
    far_part_ref[...] = outer(far_ref[...], weight_ref[...])
    blocks, picks, columns = positions_ref.shape
    half = picks // 2
    second = place_ref[1] == 1
    for b in range(blocks):
        rows = slice(b * SPAN, (b + 1) * SPAN)
        gradient = None
        for s in range(groups):
            term = across_tokens(inputs[s][:, rows], cotangents[s][...])
            gradient = term if gradient is None else gradient + term
        moment_ref[rows, :] = early_ref[rows, :] + gradient
        rounded = gradient.astype(jnp.bfloat16)
        coeffs_ref[rows, :] = early_coeffs_ref[rows, :] + (
            dot(high_ref[...], rounded) + dot(low_ref[...], rounded)
        )
        parts = []
        for c in range(0, columns, LANES):
            found = []
            for p in range(0, picks, SUBLANES):
                where = positions_ref[b, p : p + SUBLANES, c : c + LANES]
                inside, group = where & (SUBLANES - 1), where >> 3
                total = jnp.zeros((SUBLANES, LANES), jnp.float32)
                for g in range(SPAN // SUBLANES):
                    at = b * SPAN + g * SUBLANES
                    tile = coeffs_ref[at : at + SUBLANES, c : c + LANES]
                    total = jnp.where(
                        group == g, jnp.take_along_axis(tile, inside, axis=0), total
                    )
                found.append(total)
            parts.append(jnp.concatenate(found, axis=0).astype(jnp.bfloat16))
        bands = jnp.concatenate(parts, axis=1)
        mine_ref[b] = jnp.where(second, bands[half:], bands[:half])
        theirs_ref[b] = jnp.where(second, bands[:half], bands[half:])


def moments(place, inputs, cotangents, far_halves, weight, early, early_coeffs, positions, high, low):
    groups = len(inputs)
    tokens, rows = inputs[0].shape
    blocks, picks, columns = positions.shape
    half_shape = jax.ShapeDtypeStruct((blocks, picks // 2, columns), jnp.bfloat16)
    return pl.pallas_call(
        functools.partial(moment_kernel, groups),
        out_shape=[jax.ShapeDtypeStruct((rows, columns), jnp.float32)] * 2
        + [half_shape] * 2
        + [jax.ShapeDtypeStruct((tokens, rows), jnp.bfloat16)],
        in_specs=[pl.BlockSpec(memory_space=pltpu.SMEM)]
        + [pl.BlockSpec(memory_space=pltpu.VMEM)] * (2 * groups + 7),
        out_specs=[pl.BlockSpec(memory_space=pltpu.VMEM)] * 5,
        scratch_shapes=[pltpu.VMEM((tokens, columns), jnp.bfloat16)],
        compiler_params=params(),
        cost_estimate=pl.CostEstimate(
            flops=2 * blocks * SPAN * columns * (groups * tokens + 3 * SPAN),
            bytes_accessed=blocks * SPAN * (groups * tokens * 2 + 14 * columns),
            transcendentals=0,
        ),
        name="moment",
    )(
        place, *inputs, *cotangents, *far_halves, weight, early, early_coeffs, positions, high, low
    )


def feedback_kernel(moment_ref, coeffs_ref, inverse_ref, high_ref, low_ref, kept_ref, held_ref, sems):
    blocks = held_ref.shape[0]
    copies = []
    for b in range(blocks):
        rows = slice(b * SPAN, (b + 1) * SPAN)
        sent = jnp.where(inverse_ref[b] >= 0, coeffs_ref[rows, :], 0.0)
        held_ref[b] = moment_ref[rows, :] - split_dot(high_ref[...], low_ref[...], sent)
        copies.append(pltpu.make_async_copy(held_ref.at[b], kept_ref.at[0, rows, :], sems.at[b]))
        copies[-1].start()
    for copy in copies:
        copy.wait()


def feedback(moment, coeffs, inverse, high, low):
    rows, columns = moment.shape
    blocks = rows // SPAN
    return pl.pallas_call(
        feedback_kernel,
        out_shape=jax.ShapeDtypeStruct((1, rows, columns), jnp.float32),
        in_specs=[pl.BlockSpec(memory_space=pltpu.VMEM)] * 5,
        out_specs=pl.BlockSpec(memory_space=pltpu.HBM),
        scratch_shapes=[
            pltpu.VMEM((blocks, SPAN, columns), jnp.float32),
            pltpu.SemaphoreType.DMA((blocks,)),
        ],
        compiler_params=params(),
        cost_estimate=pl.CostEstimate(
            flops=4 * rows * columns * SPAN, bytes_accessed=10 * rows * columns, transcendentals=0
        ),
        name="feedback",
    )(moment, coeffs, inverse, high, low)


def decode_kernel(replicas, groups, place_ref, mine_ref, theirs_ref, inverse_ref, high_ref, low_ref, *refs):
    parts, update_ref, whole_ref, dense_ref, held_ref, sems, part_sems = (
        refs[:groups],
        *refs[groups:],
    )
    width = parts[0].shape[1]
    copies = []
    for m in range(groups):
        at = pl.multiple_of((place_ref[0] ^ m) * width, width)
        copies.append(
            pltpu.make_async_copy(parts[m], whole_ref.at[:, pl.ds(at, width)], part_sems.at[m])
        )
        copies[-1].start()

    blocks, half, columns = mine_ref.shape
    second = place_ref[1] == 1
    for b in range(blocks):
        mine = mine_ref[b].astype(jnp.float32)
        theirs = theirs_ref[b].astype(jnp.float32)
        first_half = jnp.where(second, theirs, mine)
        second_half = jnp.where(second, mine, theirs)
        for c in range(0, columns, LANES):
            source = [
                part[p : p + SUBLANES, c : c + LANES]
                for part in (first_half, second_half)
                for p in range(0, half, SUBLANES)
            ]
            for g in range(0, SPAN, SUBLANES):
                pick = inverse_ref[b, g : g + SUBLANES, c : c + LANES]
                inside, group = pick & (SUBLANES - 1), pick >> 3
                total = jnp.zeros((SUBLANES, LANES), jnp.float32)
                for s, tile in enumerate(source):
                    total = jnp.where(
                        group == s, jnp.take_along_axis(tile, inside, axis=0), total
                    )
                dense_ref[g : g + SUBLANES, c : c + LANES] = total
        dense = dense_ref[...].astype(jnp.bfloat16)
        update = (dot(high_ref[...], dense) + dot(low_ref[...], dense)) * (1.0 / replicas)
        held_ref[b] = update.astype(jnp.bfloat16)
        copies.append(
            pltpu.make_async_copy(
                held_ref.at[b], update_ref.at[b * SPAN : (b + 1) * SPAN, :], sems.at[b]
            )
        )
        copies[-1].start()
    for copy in copies:
        copy.wait()


def decode(place, mine, theirs, inverse, high, low, parts, replicas):
    blocks, half, columns = mine.shape
    groups = len(parts)
    tokens, width = parts[0].shape
    return pl.pallas_call(
        functools.partial(decode_kernel, replicas, groups),
        out_shape=[
            jax.ShapeDtypeStruct((blocks * SPAN, columns), jnp.bfloat16),
            jax.ShapeDtypeStruct((tokens, groups * width), jnp.bfloat16),
        ],
        in_specs=[pl.BlockSpec(memory_space=pltpu.SMEM)]
        + [pl.BlockSpec(memory_space=pltpu.VMEM)] * (5 + groups),
        out_specs=[pl.BlockSpec(memory_space=pltpu.HBM)] * 2,
        scratch_shapes=[
            pltpu.VMEM((SPAN, columns), jnp.float32),
            pltpu.VMEM((blocks, SPAN, columns), jnp.bfloat16),
            pltpu.SemaphoreType.DMA((blocks,)),
            pltpu.SemaphoreType.DMA((groups,)),
        ],
        compiler_params=params(),
        cost_estimate=pl.CostEstimate(
            flops=6 * blocks * SPAN * SPAN * columns,
            bytes_accessed=6 * blocks * SPAN * columns + 4 * groups * tokens * width,
            transcendentals=0,
        ),
        name="decode",
    )(place, mine, theirs, inverse, high, low, *parts)


def swap(x, axis, mask):
    size = lax.axis_size(axis)
    return lax.ppermute(x, axis, [(s, s ^ mask) for s in range(size)])


def sum_over_chips(x, after):
    replicas = lax.axis_size("dp")
    stride = 2
    total = x
    while stride < replicas:
        sent = total.astype(jnp.bfloat16)
        masks = [stride * m for m in (1, 2, 3) if stride * m < replicas]
        late, after = lax.optimization_barrier((sent, after)) if stride == 2 else (sent, after)
        parts = [sent] + [swap(late if m == masks[0] else sent, "dp", m) for m in masks]
        parts = [part.astype(jnp.float32) for part in parts]
        total = parts[0] + parts[1] if len(parts) == 2 else (parts[0] + parts[1]) + (parts[2] + parts[3])
        stride *= 4
    return total.astype(jnp.bfloat16), after


def far_cotangent(cotangents, groups):
    half = cotangents[0].shape[0] // 2
    if groups == 4:
        return swap(cotangents[2][:half], "fsdp", 1), swap(cotangents[1][half:], "fsdp", 2)
    far = swap(cotangents[0], "fsdp", groups - 1)
    return far[:half], far[half:]


def on_device(activations, cotangent, weight, momentum, positions):
    groups, replicas = lax.axis_size("fsdp"), lax.axis_size("dp")
    rows = weight.shape[0]
    index = lax.axis_index("fsdp")
    place = jnp.stack([index, lax.axis_index("dp") % 2]).astype(jnp.int32)
    high, low = transform_table()

    cotangents = [cotangent] + [swap(cotangent, "fsdp", m) for m in range(1, groups - 1)]
    far_halves = far_cotangent(cotangents, groups)
    inverse = inverse_index(positions)
    sent = cut(place, activations, groups)
    inputs = [swap(sent[m - 1], "fsdp", m) for m in range(1, groups)]
    near = input_gradients(cotangents, weight)
    late = groups - 2
    early, early_coeffs = early_moments(
        place, activations, inputs[: late - 1], cotangents[:late], momentum, high, low
    )
    inputs, inverse, early, _ = lax.optimization_barrier((inputs, inverse, early, near))
    parts = [near[0]] + [swap(near[m], "fsdp", m) for m in range(1, groups - 1)]

    moment, coeffs, mine, theirs, far = moments(
        place,
        inputs[late - 1 :],
        cotangents[late:],
        far_halves,
        weight,
        early,
        early_coeffs,
        positions,
        high,
        low,
    )
    parts.append(swap(far, "fsdp", groups - 1))
    chip = mine.astype(jnp.float32) + swap(theirs, "dp", 1).astype(jnp.float32)
    new_momentum = feedback(moment, coeffs, inverse, high.T, low.T)
    summed, parts[1:-1] = sum_over_chips(chip, parts[1:-1])
    summed, new_momentum = lax.optimization_barrier((summed, new_momentum))
    update, grad_input = decode(
        place, summed, swap(summed, "dp", 1), inverse, high.T, low.T, parts, replicas
    )
    return grad_input, new_momentum, update


def solution(mesh):
    placed = (
        P(("dp", "fsdp"), None),
        P(("dp", "fsdp"), None),
        P("fsdp", None),
        P("dp", "fsdp", None),
        P("fsdp", None, None),
    )
    return jax.shard_map(
        on_device,
        mesh=mesh,
        in_specs=placed,
        out_specs=(P(("dp", "fsdp"), None), P("dp", "fsdp", None), P("fsdp", None)),
        check_vma=False,
    )
```

time: 55.1 us -> 49.9 us (0.906)
  waiting for transfers between devices: 13.9 us -> 10.5 us
  starting transfers between devices: 19.3 us -> 17.9 us
    ppermute x14 -> x15, waiting for transfers between devices: 13.9 us -> 10.5 us  [swap(): return lax.ppermute(x, axis, [(s, s ^ mask) for s in range(size)])]
    pallas_call x0 -> x1, Pallas kernels: none -> 2.75 us  [early_moments(): pl.pallas_call(functools.partial(early_kernel, groups), out_shape=[jax.Sh...]
    pallas_call x1, Pallas kernels: 4.97 us -> 3.19 us  [moments(): pl.pallas_call(functools.partial(moment_kernel, groups), out_shape=[jax.S...]
    ppermute x14 -> x15, starting transfers between devices: 19.3 us -> 17.9 us  [swap(): return lax.ppermute(x, axis, [(s, s ^ mask) for s in range(size)])]
    pallas_call x1, Pallas kernels: 4.19 us -> 3.4 us  [decode(): pl.pallas_call(functools.partial(decode_kernel, replicas, groups), out_sh...]
  transfers between devices with their start and end apart: 14 -> 15, of which waited for: 4 -> 5; matrix products, arithmetic and copies ran while one was open for 0% -> 0% of each run, Pallas kernels for 26% -> 29%
where the time goes in v4:
time: 49.9 us; the launch traced here: 49.7 us
  Pallas kernels  18 us (36%)
  starting transfers between devices  17.9 us (36%)
  waiting for transfers between devices  10.5 us (21%)
  local copies, waits for them, and re-layouts  2.42 us (5%)
  between operations  0.8 us (2%)
    ppermute x15, starting transfers between devices, swap(): return lax.ppermute(x, axis, [(s, s ^ mask) for s in range(size)])  17.9 us
    ppermute x15, waiting for transfers between devices, swap(): return lax.ppermute(x, axis, [(s, s ^ mask) for s in range(size)])  10.5 us
    pallas_call x1, Pallas kernels, inverse_index(): pl.pallas_call(inverse_index_kernel, out_shape=jax.ShapeDtypeStruct((bloc...  4.52 us
    pallas_call x1, Pallas kernels, decode(): pl.pallas_call(functools.partial(decode_kernel, replicas, groups), out_sh...  3.4 us
    pallas_call x1, Pallas kernels, moments(): pl.pallas_call(functools.partial(moment_kernel, groups), out_shape=[jax.S...  3.19 us
    pallas_call x1, Pallas kernels, early_moments(): pl.pallas_call(functools.partial(early_kernel, groups), out_shape=[jax.Sh...  2.75 us
    unnamed x22, local copies, waits for them, and re-layouts  2.4 us
    pallas_call x1, Pallas kernels, feedback(): pl.pallas_call(feedback_kernel, out_shape=jax.ShapeDtypeStruct((1, rows,...  2.22 us
  transfers between devices with their start and end apart: 15, of which 5 were waited for; matrix products, arithmetic and copies ran while one was open for 0% of the time, Pallas kernels for 29%

profile of v4, /device:TPU:0, one launch (start us, length us, event | category | flops | bytes accessed | tf_op | source)
XLA Modules:
  0.0 49.7 jit_solution(12533050654257731862)
XLA Ops:
  0.6 3.0 %collective-permute-start.3 = (bf16[192,512]{1,0:T(8,128)(2,1)}, bf16[192,512]{1,0:T(8,128)(2,1)S(1)}, u32[]{:S(2)}, u32[]{:S(2)}) collective-permute-start(bf16[192,512]{1,0:T(8,128)(2,1)} %refs_0_.3), channel_id=1, source_target_pairs={{0,1},{1,0},{2,3},{3,2},{4,5},{5,4},{6,7},{7,6},{8,9},{9,8},{10,11... | collective-permute-start | bytes 589832 | tf_op jit(solution)/shard_map/ppermute | solution.py:386
  3.6 1.5 %collective-permute-start.4 = (bf16[192,512]{1,0:T(8,128)(2,1)}, bf16[192,512]{1,0:T(8,128)(2,1)S(1)}, u32[]{:S(2)}, u32[]{:S(2)}) collective-permute-start(bf16[192,512]{1,0:T(8,128)(2,1)} %refs_0_.3), channel_id=1, source_target_pairs={{0,2},{1,3},{2,0},{3,1},{4,6},{5,7},{6,4},{7,5},{8,10},{9,11},{10,... | collective-permute-start | bytes 589832 | tf_op jit(solution)/shard_map/ppermute | solution.py:386
  5.2 0.1 pad_add_fusion.place_ref
  5.2 0.0 copy-start
  5.2 1.4 %copy-done = bf16[192,4096]{1,0:T(8,128)(2,1)S(1)} copy-done((bf16[192,4096]{1,0:T(8,128)(2,1)S(1)}, bf16[192,4096]{1,0:T(8,128)(2,1)}, u32[]{:S(2)}) %copy-start) | copy-done | bytes 1572888
  6.6 0.0 copy-start.5
  6.6 0.0 copy-start.10
  6.6 0.7 %cut.1 = (bf16[192,1024]{1,0:T(8,128)(2,1)S(1)}, bf16[192,1024]{1,0:T(8,128)(2,1)S(1)}, bf16[192,1024]{1,0:T(8,128)(2,1)S(1)}) custom-call(s32[2]{0:T(128)S(1)} %pad_add_fusion.place_ref, bf16[192,4096]{1,0:T(8,128)(2,1)S(1)} %copy-done), custom_call_target="tpu_custom_call" | custom-call | bytes 2359296 | tf_op jit(solution)/shard_map/cut/pallas_call | solution.py:101
  7.3 0.6 %collective-permute-start = (bf16[192,1024]{1,0:T(8,128)(2,1)S(1)}, bf16[192,1024]{1,0:T(8,128)(2,1)S(1)}, u32[]{:S(2)}, u32[]{:S(2)}) collective-permute-start(bf16[192,1024]{1,0:T(8,128)(2,1)S(1)} %get-tuple-element.27), channel_id=1, source_target_pairs={{0,1},{1,0},{2,3},{3,2},{4,5},{5,4},{6,7},{7,6},{8,9},{9,8},{10,11... | collective-permute-start | bytes 1179656 | tf_op jit(solution)/shard_map/ppermute | solution.py:386
  7.9 0.1 collective-permute-start.1
  8.0 2.9 %collective-permute-start.2 = (bf16[192,1024]{1,0:T(8,128)(2,1)S(1)}, bf16[192,1024]{1,0:T(8,128)(2,1)S(1)}, u32[]{:S(2)}, u32[]{:S(2)}) collective-permute-start(bf16[192,1024]{1,0:T(8,128)(2,1)S(1)} %get-tuple-element.29), channel_id=1, source_target_pairs={{0,3},{1,2},{2,1},{3,0},{4,7},{5,6},{6,5},{7,4},{8,11},{9,10},{10,... | collective-permute-start | bytes 1179656 | tf_op jit(solution)/shard_map/ppermute | solution.py:386
  10.9 0.0 copy-start.3
  10.9 0.9 %copy-done.3 = s32[4,32,512]{2,1,0:T(8,128)S(1)} copy-done((s32[4,32,512]{2,1,0:T(8,128)S(1)}, s32[4,32,512]{2,1,0:T(8,128)}, u32[]{:S(2)}) %copy-start.3) | copy-done | bytes 262168
  11.8 4.5 %inverse_index.1.inverse_ref = s32[4,256,512]{2,1,0:T(8,128)S(1)} custom-call(s32[4,32,512]{2,1,0:T(8,128)S(1)} %copy-done.3), custom_call_target="tpu_custom_call" | custom-call | flops 33554432 | bytes 2097152 | tf_op jit(solution)/shard_map/inverse_index/pallas_call | solution.py:68
  16.4 0.0 collective-permute-done.3.refs_3_.refs_1_
  16.4 0.6 %collective-permute-start.6 = (bf16[96,512]{1,0:T(8,128)(2,1)S(1)}, bf16[96,512]{1,0:T(8,128)(2,1)S(1)}, u32[]{:S(2)}, u32[]{:S(2)}) collective-permute-start(bf16[96,512]{1,0:T(8,128)(2,1)S(1)} %slice.9), channel_id=1, source_target_pairs={{0,2},{1,3},{2,0},{3,1},{4,6},{5,7},{6,4},{7,5},{8,10},{9,11},{10,... | collective-permute-start | bytes 294920 | tf_op jit(solution)/shard_map/ppermute | solution.py:386
  17.0 0.0 collective-permute-done.4.refs_2_
  17.0 0.0 copy-start.1
  17.0 0.0 copy-start.2
  17.0 0.0 copy-start.8
  17.0 0.0 copy-start.9
  17.0 0.1 collective-permute-start.5
  17.2 0.0 copy-done.5
  17.2 0.0 copy-done.10
  17.2 1.2 %input_gradients.1 = (bf16[192,1024]{1,0:T(8,128)(2,1)S(1)}, bf16[192,1024]{1,0:T(8,128)(2,1)S(1)}, bf16[192,1024]{1,0:T(8,128)(2,1)S(1)}) custom-call(bf16[192,512]{1,0:T(8,128)(2,1)S(1)} %copy-done.10, bf16[192,512]{1,0:T(8,128)(2,1)S(1)} %collective-permute-done.3.refs_3_.refs_1_, bf16[192,512]{1,0:T(8,128)(2,1)S(1)} %collective-permute-done.4.refs_2_, ...), custom_call_target="tpu_custom_call" | custom-call | flops 12079595520 | bytes 2818048 | tf_op jit(solution)/shard_map/input_gradients/pallas_call | solution.py:134
  18.4 1.1 %collective-permute-done.refs_1_ = bf16[192,1024]{1,0:T(8,128)(2,1)S(1)} collective-permute-done((bf16[192,1024]{1,0:T(8,128)(2,1)S(1)}, bf16[192,1024]{1,0:T(8,128)(2,1)S(1)}, u32[]{:S(2)}, u32[]{:S(2)}) %collective-permute-start) | collective-permute-done | bytes 393248 | tf_op jit(solution)/shard_map/ppermute | solution.py:386
  19.5 0.0 copy-start.4
  19.5 1.0 %collective-permute-start.8 = (bf16[192,1024]{1,0:T(8,128)(2,1)S(1)}, bf16[192,1024]{1,0:T(8,128)(2,1)S(1)}, u32[]{:S(2)}, u32[]{:S(2)}) collective-permute-start(bf16[192,1024]{1,0:T(8,128)(2,1)S(1)} %get-tuple-element.32), channel_id=1, source_target_pairs={{0,1},{1,0},{2,3},{3,2},{4,5},{5,4},{6,7},{7,6},{8,9},{9,8},{10,11... | collective-permute-start | bytes 1179656 | tf_op jit(solution)/shard_map/ppermute | solution.py:386
  20.4 0.0 copy-done.1
  20.4 0.0 copy-done.2
  20.4 0.0 copy-done.8
  20.4 0.0 copy-done.9
  20.4 2.8 %early_moment.1 = (f32[1024,512]{1,0:T(8,128)S(1)}, f32[1024,512]{1,0:T(8,128)S(1)}) custom-call(s32[2]{0:T(128)S(1)} %pad_add_fusion.place_ref, bf16[192,4096]{1,0:T(8,128)(2,1)S(1)} %copy-done.1, bf16[192,1024]{1,0:T(8,128)(2,1)S(1)} %collective-permute-done.refs_1_, bf16[192,512]{1,0:T(8,128)(2,1)S(1)} %copy-done.10, ...), custom_call_target="tpu_custom_call" | custom-call | flops 1207959552 | bytes 7077888 | tf_op jit(solution)/shard_map/early_moment/pallas_call | solution.py:174
  23.2 5.0 %collective-permute-done.1.refs_0_ = bf16[192,1024]{1,0:T(8,128)(2,1)S(1)} collective-permute-done((bf16[192,1024]{1,0:T(8,128)(2,1)S(1)}, bf16[192,1024]{1,0:T(8,128)(2,1)S(1)}, u32[]{:S(2)}, u32[]{:S(2)}) %collective-permute-start.1) | collective-permute-done | bytes 393248 | tf_op jit(solution)/shard_map/ppermute | solution.py:386
  28.2 1.8 %collective-permute-start.9 = (bf16[192,1024]{1,0:T(8,128)(2,1)S(1)}, bf16[192,1024]{1,0:T(8,128)(2,1)S(1)}, u32[]{:S(2)}, u32[]{:S(2)}) collective-permute-start(bf16[192,1024]{1,0:T(8,128)(2,1)S(1)} %get-tuple-element.33), channel_id=1, source_target_pairs={{0,2},{1,3},{2,0},{3,1},{4,6},{5,7},{6,4},{7,5},{8,10},{9,11},{10,... | collective-permute-start | bytes 1179656 | tf_op jit(solution)/shard_map/ppermute | solution.py:386
  30.0 0.0 collective-permute-done.2.refs_1_
  30.0 0.3 collective-permute-done.6.refs_4_
  30.3 0.0 collective-permute-done.5.refs_3_
  30.3 0.0 copy-done.4
  30.3 0.0 copy-start.6
  30.3 0.0 copy-start.7
  30.3 3.2 %moment.1 = (f32[1024,512]{1,0:T(8,128)S(1)}, f32[1024,512]{1,0:T(8,128)S(1)}, bf16[4,16,512]{2,1,0:T(8,128)(2,1)S(1)}, bf16[4,16,512]{2,1,0:T(8,128)(2,1)S(1)}, bf16[192,1024]{1,0:T(8,128)(2,1)S(1)}) custom-call(s32[2]{0:T(128)S(1)} %pad_add_fusion.place_ref, bf16[192,1024]{1,0:T(8,128)(2,1)S(1)} %collective-permute-done.1.refs_0_, ...), custom_call_target="tpu_custom_call" | custom-call | flops 1207959552 | bytes 8126464 | tf_op jit(solution)/shard_map/moment/pallas_call | solution.py:252
  33.5 0.1 collective-permute-start.7
  33.6 1.7 %collective-permute-start.14 = (bf16[192,1024]{1,0:T(8,128)(2,1)S(1)}, bf16[192,1024]{1,0:T(8,128)(2,1)S(1)}, u32[]{:S(2)}, u32[]{:S(2)}) collective-permute-start(bf16[192,1024]{1,0:T(8,128)(2,1)S(1)} %get-tuple-element.47), channel_id=1, source_target_pairs={{0,3},{1,2},{2,1},{3,0},{4,7},{5,6},{6,5},{7,4},{8,11},{9,10},{10,... | collective-permute-start | bytes 1179656 | tf_op jit(solution)/shard_map/ppermute | solution.py:386
  35.3 0.0 collective-permute-done.7
  35.4 3.7 %collective-permute-start.12 = (bf16[4,16,512]{2,1,0:T(8,128)(2,1)S(1)}, bf16[4,16,512]{2,1,0:T(8,128)(2,1)S(1)}, u32[]{:S(2)}, u32[]{:S(2)}) collective-permute-start(bf16[4,16,512]{2,1,0:T(8,128)(2,1)S(1)} %add_convert_fusion.1), channel_id=1, source_target_pairs={{0,24},{4,28},{8,16},{12,20},{16,8},{20,12},{24,0},{28,4},{1,25},{... | collective-permute-start | bytes 196616 | tf_op jit(solution)/shard_map/ppermute | solution.py:386
  39.0 0.0 collective-permute-start.11
  39.0 0.0 collective-permute-done.8.refs_1_
  39.0 0.0 collective-permute-done.9.refs_2_
  39.0 0.8 %collective-permute-start.10 = (bf16[4,16,512]{2,1,0:T(8,128)(2,1)S(1)}, bf16[4,16,512]{2,1,0:T(8,128)(2,1)S(1)}, u32[]{:S(2)}, u32[]{:S(2)}) collective-permute-start(bf16[4,16,512]{2,1,0:T(8,128)(2,1)S(1)} %add_convert_fusion.1), channel_id=1, source_target_pairs={{0,8},{4,12},{8,0},{12,4},{16,24},{20,28},{24,16},{28,20},{1,9},{5... | collective-permute-start | bytes 196616 | tf_op jit(solution)/shard_map/ppermute | solution.py:386
  39.8 0.0 copy-done.6
  39.8 0.0 copy-done.7
  39.8 2.2 %feedback.1 = f32[1,1024,512]{2,1,0:T(8,128)} custom-call(f32[1024,512]{1,0:T(8,128)S(1)} %get-tuple-element.41.moment_ref, f32[1024,512]{1,0:T(8,128)S(1)} %get-tuple-element.42.coeffs_ref, s32[4,256,512]{2,1,0:T(8,128)S(1)} %inverse_index.1.inverse_ref, bf16[256,256]{1,0:T(8,128)(2,1)S(1)} %copy-done.7, bf16[256,256]{1,0:T(8,128)(2,1)S(1)} %copy-done.6), custom_call_target="tpu_custom_call" | custom-call | flops 536870912 | bytes 5242880 | tf_op jit(solution)/shard_map/feedback/pallas_call | solution.py:289
  42.1 0.0 collective-permute-done.12
  42.1 2.8 %collective-permute-done.11 = bf16[4,16,512]{2,1,0:T(8,128)(2,1)S(1)} collective-permute-done((bf16[4,16,512]{2,1,0:T(8,128)(2,1)S(1)}, bf16[4,16,512]{2,1,0:T(8,128)(2,1)S(1)}, u32[]{:S(2)}, u32[]{:S(2)}) %collective-permute-start.11) | collective-permute-done | bytes 65568 | tf_op jit(solution)/shard_map/ppermute | solution.py:386
  44.9 0.0 collective-permute-done.10
  45.0 0.1 collective-permute-start.13
  45.0 1.2 %collective-permute-done.13.theirs_ref = bf16[4,16,512]{2,1,0:T(8,128)(2,1)S(1)} collective-permute-done((bf16[4,16,512]{2,1,0:T(8,128)(2,1)S(1)}, bf16[4,16,512]{2,1,0:T(8,128)(2,1)S(1)}, u32[]{:S(2)}, u32[]{:S(2)}) %collective-permute-start.13) | collective-permute-done | bytes 65568 | tf_op jit(solution)/shard_map/ppermute | solution.py:386
  46.3 0.0 collective-permute-done.14.refs_3_
  46.3 3.4 %decode.1 = (bf16[1024,512]{1,0:T(8,128)(2,1)}, bf16[192,4096]{1,0:T(8,128)(2,1)}) custom-call(s32[2]{0:T(128)S(1)} %pad_add_fusion.place_ref, bf16[4,16,512]{2,1,0:T(8,128)(2,1)S(1)} %add_convert_fusion.mine_ref, bf16[4,16,512]{2,1,0:T(8,128)(2,1)S(1)} %collective-permute-done.13.theirs_ref, s32[4,256,512]{2,1,0:T(8,128)S(1)} %inverse_index.1.inverse_ref, ...), custom_call_target="tpu_custom_call" | custom-call | flops 805306368 | bytes 6291456 | tf_op jit(solution)/shard_map/decode/pallas_call | solution.py:359
  (4 shorter events, 0.1 us)
Async XLA Ops:
  0.6 15.7 %collective-permute-start.3 = (bf16[192,512]{1,0:T(8,128)(2,1)}, bf16[192,512]{1,0:T(8,128)(2,1)S(1)}, u32[]{:S(2)}, u32[]{:S(2)}) collective-permute-start(bf16[192,512]{1,0:T(8,128)(2,1)} %refs_0_.3), channel_id=1, source_target_pairs={{0,1},{1,0},{2,3},{3,2},{4,5},{5,4},{6,7},{7,6},{8,9},{9,8},{10,11... | collective-permute-start | bytes 589832 | tf_op jit(solution)/shard_map/ppermute | solution.py:386
  3.6 13.3 %collective-permute-start.4 = (bf16[192,512]{1,0:T(8,128)(2,1)}, bf16[192,512]{1,0:T(8,128)(2,1)S(1)}, u32[]{:S(2)}, u32[]{:S(2)}) collective-permute-start(bf16[192,512]{1,0:T(8,128)(2,1)} %refs_0_.3), channel_id=1, source_target_pairs={{0,2},{1,3},{2,0},{3,1},{4,6},{5,7},{6,4},{7,5},{8,10},{9,11},{10,... | collective-permute-start | bytes 589832 | tf_op jit(solution)/shard_map/ppermute | solution.py:386
  5.2 1.4 %copy-start = (bf16[192,4096]{1,0:T(8,128)(2,1)S(1)}, bf16[192,4096]{1,0:T(8,128)(2,1)}, u32[]{:S(2)}) copy-start(bf16[192,4096]{1,0:T(8,128)(2,1)} %refs_0_.2) | copy-start | bytes 4718596
  6.6 10.5 %copy-start.5 = (bf16[1024,512]{1,0:T(8,128)(2,1)S(1)}, bf16[1024,512]{1,0:T(8,128)(2,1)}, u32[]{:S(2)}) copy-start(bf16[1024,512]{1,0:T(8,128)(2,1)} %refs_5_.2) | copy-start | bytes 3145732
  6.6 10.6 %copy-start.10 = (bf16[192,512]{1,0:T(8,128)(2,1)S(1)}, bf16[192,512]{1,0:T(8,128)(2,1)}, u32[]{:S(2)}) copy-start(bf16[192,512]{1,0:T(8,128)(2,1)} %refs_0_.3) | copy-start | bytes 589828
  7.3 12.1 %collective-permute-start = (bf16[192,1024]{1,0:T(8,128)(2,1)S(1)}, bf16[192,1024]{1,0:T(8,128)(2,1)S(1)}, u32[]{:S(2)}, u32[]{:S(2)}) collective-permute-start(bf16[192,1024]{1,0:T(8,128)(2,1)S(1)} %get-tuple-element.27), channel_id=1, source_target_pairs={{0,1},{1,0},{2,3},{3,2},{4,5},{5,4},{6,7},{7,6},{8,9},{9,8},{10,11... | collective-permute-start | bytes 1179656 | tf_op jit(solution)/shard_map/ppermute | solution.py:386
  7.9 20.3 %collective-permute-start.1 = (bf16[192,1024]{1,0:T(8,128)(2,1)S(1)}, bf16[192,1024]{1,0:T(8,128)(2,1)S(1)}, u32[]{:S(2)}, u32[]{:S(2)}) collective-permute-start(bf16[192,1024]{1,0:T(8,128)(2,1)S(1)} %get-tuple-element.28), channel_id=1, source_target_pairs={{0,2},{1,3},{2,0},{3,1},{4,6},{5,7},{6,4},{7,5},{8,10},{9,11},{10,... | collective-permute-start | bytes 1179656 | tf_op jit(solution)/shard_map/ppermute | solution.py:386
  8.0 22.1 %collective-permute-start.2 = (bf16[192,1024]{1,0:T(8,128)(2,1)S(1)}, bf16[192,1024]{1,0:T(8,128)(2,1)S(1)}, u32[]{:S(2)}, u32[]{:S(2)}) collective-permute-start(bf16[192,1024]{1,0:T(8,128)(2,1)S(1)} %get-tuple-element.29), channel_id=1, source_target_pairs={{0,3},{1,2},{2,1},{3,0},{4,7},{5,6},{6,5},{7,4},{8,11},{9,10},{10,... | collective-permute-start | bytes 1179656 | tf_op jit(solution)/shard_map/ppermute | solution.py:386
  10.9 0.9 %copy-start.3 = (s32[4,32,512]{2,1,0:T(8,128)S(1)}, s32[4,32,512]{2,1,0:T(8,128)}, u32[]{:S(2)}) copy-start(s32[4,32,512]{2,1,0:T(8,128)} %refs_8_.1) | copy-start | bytes 786436
  16.4 13.9 %collective-permute-start.6 = (bf16[96,512]{1,0:T(8,128)(2,1)S(1)}, bf16[96,512]{1,0:T(8,128)(2,1)S(1)}, u32[]{:S(2)}, u32[]{:S(2)}) collective-permute-start(bf16[96,512]{1,0:T(8,128)(2,1)S(1)} %slice.9), channel_id=1, source_target_pairs={{0,2},{1,3},{2,0},{3,1},{4,6},{5,7},{6,4},{7,5},{8,10},{9,11},{10,... | collective-permute-start | bytes 294920 | tf_op jit(solution)/shard_map/ppermute | solution.py:386
  17.0 3.4 %copy-start.1 = (bf16[192,4096]{1,0:T(8,128)(2,1)S(1)}, bf16[192,4096]{1,0:T(8,128)(2,1)}, u32[]{:S(2)}) copy-start(bf16[192,4096]{1,0:T(8,128)(2,1)} %refs_0_.2) | copy-start | bytes 4718596
  17.0 3.4 %copy-start.2 = (f32[1,1024,512]{2,1,0:T(8,128)S(1)}, f32[1,1024,512]{2,1,0:T(8,128)}, u32[]{:S(2)}) copy-start(f32[1,1024,512]{2,1,0:T(8,128)} %refs_4_.1) | copy-start | bytes 6291460
  17.0 3.4 %copy-start.8 = (bf16[256,256]{1,0:T(8,128)(2,1)S(1)}, bf16[256,256]{1,0:T(8,128)(2,1)}, u32[]{:S(2)}) copy-start(bf16[256,256]{1,0:T(8,128)(2,1)} %constant.31.clone.refs_6_.refs_10_) | copy-start | bytes 393220
  17.0 3.4 %copy-start.9 = (bf16[256,256]{1,0:T(8,128)(2,1)S(1)}, bf16[256,256]{1,0:T(8,128)(2,1)}, u32[]{:S(2)}) copy-start(bf16[256,256]{1,0:T(8,128)(2,1)} %constant.30.clone.refs_5_.refs_9_) | copy-start | bytes 393220
  17.0 13.3 %collective-permute-start.5 = (bf16[96,512]{1,0:T(8,128)(2,1)S(1)}, bf16[96,512]{1,0:T(8,128)(2,1)S(1)}, u32[]{:S(2)}, u32[]{:S(2)}) collective-permute-start(bf16[96,512]{1,0:T(8,128)(2,1)S(1)} %slice.8), channel_id=1, source_target_pairs={{0,1},{1,0},{2,3},{3,2},{4,5},{5,4},{6,7},{7,6},{8,9},{9,8},{10,11... | collective-permute-start | bytes 294920 | tf_op jit(solution)/shard_map/ppermute | solution.py:386
  19.5 10.9 %copy-start.4 = (s32[4,32,512]{2,1,0:T(8,128)S(1)}, s32[4,32,512]{2,1,0:T(8,128)}, u32[]{:S(2)}) copy-start(s32[4,32,512]{2,1,0:T(8,128)} %refs_8_.1) | copy-start | bytes 786436
  19.5 19.6 %collective-permute-start.8 = (bf16[192,1024]{1,0:T(8,128)(2,1)S(1)}, bf16[192,1024]{1,0:T(8,128)(2,1)S(1)}, u32[]{:S(2)}, u32[]{:S(2)}) collective-permute-start(bf16[192,1024]{1,0:T(8,128)(2,1)S(1)} %get-tuple-element.32), channel_id=1, source_target_pairs={{0,1},{1,0},{2,3},{3,2},{4,5},{5,4},{6,7},{7,6},{8,9},{9,8},{10,11... | collective-permute-start | bytes 1179656 | tf_op jit(solution)/shard_map/ppermute | solution.py:386
  28.2 10.8 %collective-permute-start.9 = (bf16[192,1024]{1,0:T(8,128)(2,1)S(1)}, bf16[192,1024]{1,0:T(8,128)(2,1)S(1)}, u32[]{:S(2)}, u32[]{:S(2)}) collective-permute-start(bf16[192,1024]{1,0:T(8,128)(2,1)S(1)} %get-tuple-element.33), channel_id=1, source_target_pairs={{0,2},{1,3},{2,0},{3,1},{4,6},{5,7},{6,4},{7,5},{8,10},{9,11},{10,... | collective-permute-start | bytes 1179656 | tf_op jit(solution)/shard_map/ppermute | solution.py:386
  30.3 9.5 %copy-start.6 = (bf16[256,256]{1,0:T(8,128)(2,1)S(1)}, bf16[256,256]{1,0:T(8,128)(2,1)}, u32[]{:S(2)}) copy-start(bf16[256,256]{1,0:T(8,128)(2,1)} %constant.33.clone.low_ref) | copy-start | bytes 393220
  30.3 9.5 %copy-start.7 = (bf16[256,256]{1,0:T(8,128)(2,1)S(1)}, bf16[256,256]{1,0:T(8,128)(2,1)}, u32[]{:S(2)}) copy-start(bf16[256,256]{1,0:T(8,128)(2,1)} %constant.32.clone.high_ref) | copy-start | bytes 393220
  33.5 1.8 %collective-permute-start.7 = (bf16[4,16,512]{2,1,0:T(8,128)(2,1)S(1)}, bf16[4,16,512]{2,1,0:T(8,128)(2,1)S(1)}, u32[]{:S(2)}, u32[]{:S(2)}) collective-permute-start(bf16[4,16,512]{2,1,0:T(8,128)(2,1)S(1)} %get-tuple-element.39), channel_id=1, source_target_pairs={{0,4},{4,0},{8,12},{12,8},{16,20},{20,16},{24,28},{28,24},{1,5},{5... | collective-permute-start | bytes 196616 | tf_op jit(solution)/shard_map/ppermute | solution.py:386
  33.6 12.7 %collective-permute-start.14 = (bf16[192,1024]{1,0:T(8,128)(2,1)S(1)}, bf16[192,1024]{1,0:T(8,128)(2,1)S(1)}, u32[]{:S(2)}, u32[]{:S(2)}) collective-permute-start(bf16[192,1024]{1,0:T(8,128)(2,1)S(1)} %get-tuple-element.47), channel_id=1, source_target_pairs={{0,3},{1,2},{2,1},{3,0},{4,7},{5,6},{6,5},{7,4},{8,11},{9,10},{10,... | collective-permute-start | bytes 1179656 | tf_op jit(solution)/shard_map/ppermute | solution.py:386
  35.4 6.7 %collective-permute-start.12 = (bf16[4,16,512]{2,1,0:T(8,128)(2,1)S(1)}, bf16[4,16,512]{2,1,0:T(8,128)(2,1)S(1)}, u32[]{:S(2)}, u32[]{:S(2)}) collective-permute-start(bf16[4,16,512]{2,1,0:T(8,128)(2,1)S(1)} %add_convert_fusion.1), channel_id=1, source_target_pairs={{0,24},{4,28},{8,16},{12,20},{16,8},{20,12},{24,0},{28,4},{1,25},{... | collective-permute-start | bytes 196616 | tf_op jit(solution)/shard_map/ppermute | solution.py:386
  39.0 5.9 %collective-permute-start.11 = (bf16[4,16,512]{2,1,0:T(8,128)(2,1)S(1)}, bf16[4,16,512]{2,1,0:T(8,128)(2,1)S(1)}, u32[]{:S(2)}, u32[]{:S(2)}) collective-permute-start(bf16[4,16,512]{2,1,0:T(8,128)(2,1)S(1)} %add_convert_fusion.1), channel_id=1, source_target_pairs={{0,16},{4,20},{8,24},{12,28},{16,0},{20,4},{24,8},{28,12},{1,17},{... | collective-permute-start | bytes 196616 | tf_op jit(solution)/shard_map/ppermute | solution.py:386
  39.0 5.9 %collective-permute-start.10 = (bf16[4,16,512]{2,1,0:T(8,128)(2,1)S(1)}, bf16[4,16,512]{2,1,0:T(8,128)(2,1)S(1)}, u32[]{:S(2)}, u32[]{:S(2)}) collective-permute-start(bf16[4,16,512]{2,1,0:T(8,128)(2,1)S(1)} %add_convert_fusion.1), channel_id=1, source_target_pairs={{0,8},{4,12},{8,0},{12,4},{16,24},{20,28},{24,16},{28,20},{1,9},{5... | collective-permute-start | bytes 196616 | tf_op jit(solution)/shard_map/ppermute | solution.py:386
  45.0 1.3 %collective-permute-start.13 = (bf16[4,16,512]{2,1,0:T(8,128)(2,1)S(1)}, bf16[4,16,512]{2,1,0:T(8,128)(2,1)S(1)}, u32[]{:S(2)}, u32[]{:S(2)}) collective-permute-start(bf16[4,16,512]{2,1,0:T(8,128)(2,1)S(1)} %add_convert_fusion.mine_ref), channel_id=1, source_target_pairs={{0,4},{4,0},{8,12},{12,8},{16,20},{20,16},{24,28},{28,24},{1,5},{5... | collective-permute-start | bytes 196616 | tf_op jit(solution)/shard_map/ppermute | solution.py:386

commit v5 on v4

--- a/solution.py
+++ b/solution.py
@@ -270,10 +270,20 @@
     )
 
 
-def feedback_kernel(moment_ref, coeffs_ref, inverse_ref, high_ref, low_ref, kept_ref, held_ref, sems):
-    blocks = held_ref.shape[0]
+def start_copies(first, place_ref, parts, whole_ref, sems):
+    width = parts[0].shape[1]
     copies = []
-    for b in range(blocks):
+    for m, part in enumerate(parts):
+        at = pl.multiple_of((place_ref[0] ^ (first + m)) * width, width)
+        copies.append(pltpu.make_async_copy(part, whole_ref.at[:, pl.ds(at, width)], sems.at[m]))
+        copies[-1].start()
+    return copies
+
+
+def feedback_kernel(groups, place_ref, moment_ref, coeffs_ref, inverse_ref, high_ref, low_ref, *refs):
+    parts, kept_ref, whole_ref, held_ref, sems, part_sems = refs[:groups], *refs[groups:]
+    copies = start_copies(0, place_ref, parts, whole_ref, part_sems)
+    for b in range(held_ref.shape[0]):
         rows = slice(b * SPAN, (b + 1) * SPAN)
         sent = jnp.where(inverse_ref[b] >= 0, coeffs_ref[rows, :], 0.0)
         held_ref[b] = moment_ref[rows, :] - split_dot(high_ref[...], low_ref[...], sent)
@@ -283,63 +293,100 @@
         copy.wait()
 
 
-def feedback(moment, coeffs, inverse, high, low):
+def feedback(place, moment, coeffs, inverse, high, low, parts):
     rows, columns = moment.shape
     blocks = rows // SPAN
-    return pl.pallas_call(
-        feedback_kernel,
-        out_shape=jax.ShapeDtypeStruct((1, rows, columns), jnp.float32),
-        in_specs=[pl.BlockSpec(memory_space=pltpu.VMEM)] * 5,
-        out_specs=pl.BlockSpec(memory_space=pltpu.HBM),
+    groups = len(parts)
+    tokens, width = parts[0].shape
+    return pl.pallas_call(
+        functools.partial(feedback_kernel, groups),
+        out_shape=[
+            jax.ShapeDtypeStruct((1, rows, columns), jnp.float32),
+            jax.ShapeDtypeStruct((tokens, (groups + 1) * width), jnp.bfloat16),
+        ],
+        in_specs=[pl.BlockSpec(memory_space=pltpu.SMEM)]
+        + [pl.BlockSpec(memory_space=pltpu.VMEM)] * (5 + groups),
+        out_specs=[pl.BlockSpec(memory_space=pltpu.HBM)] * 2,
         scratch_shapes=[
             pltpu.VMEM((blocks, SPAN, columns), jnp.float32),
             pltpu.SemaphoreType.DMA((blocks,)),
+            pltpu.SemaphoreType.DMA((groups,)),
         ],
         compiler_params=params(),
         cost_estimate=pl.CostEstimate(
-            flops=4 * rows * columns * SPAN, bytes_accessed=10 * rows * columns, transcendentals=0
+            flops=6 * rows * columns * SPAN,
+            bytes_accessed=16 * rows * columns + 4 * groups * tokens * width,
+            transcendentals=0,
         ),
         name="feedback",
-    )(moment, coeffs, inverse, high, low)
-
-
-def decode_kernel(replicas, groups, place_ref, mine_ref, theirs_ref, inverse_ref, high_ref, low_ref, *refs):
-    parts, update_ref, whole_ref, dense_ref, held_ref, sems, part_sems = (
-        refs[:groups],
-        *refs[groups:],
-    )
-    width = parts[0].shape[1]
-    copies = []
-    for m in range(groups):
-        at = pl.multiple_of((place_ref[0] ^ m) * width, width)
-        copies.append(
-            pltpu.make_async_copy(parts[m], whole_ref.at[:, pl.ds(at, width)], part_sems.at[m])
-        )
-        copies[-1].start()
-
-    blocks, half, columns = mine_ref.shape
-    second = place_ref[1] == 1
+    )(place, moment, coeffs, inverse, high, low, *parts)
+
+
+def put_in_place(bands_ref, inverse_ref, b, first, before):
+    _, half, columns = bands_ref.shape
+    bands = bands_ref[b].astype(jnp.float32)
+    for c in range(0, columns, LANES):
+        source = [bands[p : p + SUBLANES, c : c + LANES] for p in range(0, half, SUBLANES)]
+        for g in range(0, SPAN, SUBLANES):
+            at = (slice(g, g + SUBLANES), slice(c, c + LANES))
+            pick = inverse_ref[b, *at]
+            inside, group = pick & (SUBLANES - 1), (pick >> 3) - first
+            total = before(at)
+            for s, tile in enumerate(source):
+                total = jnp.where(group == s, jnp.take_along_axis(tile, inside, axis=0), total)
+            yield at, total
+
+
+def place_kernel(place_ref, bands_ref, inverse_ref, dense_ref):
+    blocks, half, _ = bands_ref.shape
+    first = place_ref[1] * (half // SUBLANES)
+    nothing = lambda at: jnp.zeros((SUBLANES, LANES), jnp.float32)
     for b in range(blocks):
-        mine = mine_ref[b].astype(jnp.float32)
-        theirs = theirs_ref[b].astype(jnp.float32)
-        first_half = jnp.where(second, theirs, mine)
-        second_half = jnp.where(second, mine, theirs)
-        for c in range(0, columns, LANES):
-            source = [
-                part[p : p + SUBLANES, c : c + LANES]
-                for part in (first_half, second_half)
-                for p in range(0, half, SUBLANES)
-            ]
-            for g in range(0, SPAN, SUBLANES):
-                pick = inverse_ref[b, g : g + SUBLANES, c : c + LANES]
-                inside, group = pick & (SUBLANES - 1), pick >> 3
-                total = jnp.zeros((SUBLANES, LANES), jnp.float32)
-                for s, tile in enumerate(source):
-                    total = jnp.where(
-                        group == s, jnp.take_along_axis(tile, inside, axis=0), total
-                    )
-                dense_ref[g : g + SUBLANES, c : c + LANES] = total
-        dense = dense_ref[...].astype(jnp.bfloat16)
+        for at, tile in put_in_place(bands_ref, inverse_ref, b, first, nothing):
+            dense_ref[b, *at] = tile
+
+
+def place_own(place, bands, inverse):
+    return pl.pallas_call(
+        place_kernel,
+        out_shape=jax.ShapeDtypeStruct(inverse.shape, jnp.float32),
+        in_specs=[pl.BlockSpec(memory_space=pltpu.SMEM)]
+        + [pl.BlockSpec(memory_space=pltpu.VMEM)] * 2,
+        out_specs=pl.BlockSpec(memory_space=pltpu.VMEM),
+        compiler_params=params(),
+        cost_estimate=pl.CostEstimate(
+            flops=8 * inverse.size, bytes_accessed=8 * inverse.size, transcendentals=0
+        ),
+        name="place_own",
+    )(place, bands, inverse)
+
+
+def decode_kernel(
+    replicas,
+    groups,
+    place_ref,
+    own_ref,
+    theirs_ref,
+    inverse_ref,
+    high_ref,
+    low_ref,
+    part_ref,
+    filled_ref,
+    update_ref,
+    whole_ref,
+    dense_ref,
+    held_ref,
+    sems,
+    part_sems,
+):
+    copies = start_copies(groups - 1, place_ref, [part_ref], whole_ref, part_sems)
+    blocks, half, _ = theirs_ref.shape
+    first = (1 - place_ref[1]) * (half // SUBLANES)
+    for b in range(blocks):
+        placed = lambda at: own_ref[b, *at]
+        for at, tile in put_in_place(theirs_ref, inverse_ref, b, first, placed):
+            dense_ref[b, *at] = tile
+        dense = dense_ref[b].astype(jnp.bfloat16)
         update = (dot(high_ref[...], dense) + dot(low_ref[...], dense)) * (1.0 / replicas)
         held_ref[b] = update.astype(jnp.bfloat16)
         copies.append(
@@ -352,33 +399,35 @@
         copy.wait()
 
 
-def decode(place, mine, theirs, inverse, high, low, parts, replicas):
-    blocks, half, columns = mine.shape
-    groups = len(parts)
-    tokens, width = parts[0].shape
+def decode(place, own, theirs, inverse, high, low, part, filled, replicas):
+    blocks, _, columns = theirs.shape
+    tokens, width = part.shape
+    groups = filled.shape[1] // width
     return pl.pallas_call(
         functools.partial(decode_kernel, replicas, groups),
         out_shape=[
             jax.ShapeDtypeStruct((blocks * SPAN, columns), jnp.bfloat16),
-            jax.ShapeDtypeStruct((tokens, groups * width), jnp.bfloat16),
+            jax.ShapeDtypeStruct(filled.shape, jnp.bfloat16),
         ],
         in_specs=[pl.BlockSpec(memory_space=pltpu.SMEM)]
-        + [pl.BlockSpec(memory_space=pltpu.VMEM)] * (5 + groups),
+        + [pl.BlockSpec(memory_space=pltpu.VMEM)] * 6
+        + [pl.BlockSpec(memory_space=pltpu.HBM)],
         out_specs=[pl.BlockSpec(memory_space=pltpu.HBM)] * 2,
         scratch_shapes=[
-            pltpu.VMEM((SPAN, columns), jnp.float32),
+            pltpu.VMEM((blocks, SPAN, columns), jnp.float32),
             pltpu.VMEM((blocks, SPAN, columns), jnp.bfloat16),
             pltpu.SemaphoreType.DMA((blocks,)),
-            pltpu.SemaphoreType.DMA((groups,)),
+            pltpu.SemaphoreType.DMA((1,)),
         ],
+        input_output_aliases={7: 1},
         compiler_params=params(),
         cost_estimate=pl.CostEstimate(
             flops=6 * blocks * SPAN * SPAN * columns,
-            bytes_accessed=6 * blocks * SPAN * columns + 4 * groups * tokens * width,
+            bytes_accessed=6 * blocks * SPAN * columns + 4 * tokens * width,
             transcendentals=0,
         ),
         name="decode",
-    )(place, mine, theirs, inverse, high, low, *parts)
+    )(place, own, theirs, inverse, high, low, part, filled)
 
 
 def swap(x, axis, mask):
@@ -443,11 +492,13 @@
     )
     parts.append(swap(far, "fsdp", groups - 1))
     chip = mine.astype(jnp.float32) + swap(theirs, "dp", 1).astype(jnp.float32)
-    new_momentum = feedback(moment, coeffs, inverse, high.T, low.T)
+    new_momentum, filled = feedback(place, moment, coeffs, inverse, high.T, low.T, parts[:-1])
     summed, parts[1:-1] = sum_over_chips(chip, parts[1:-1])
     summed, new_momentum = lax.optimization_barrier((summed, new_momentum))
+    theirs = swap(summed, "dp", 1)
+    own = place_own(place, summed, inverse)
     update, grad_input = decode(
-        place, summed, swap(summed, "dp", 1), inverse, high.T, low.T, parts, replicas
+        place, own, theirs, inverse, high.T, low.T, parts[-1], filled, replicas
     )
     return grad_input, new_momentum, update
 

time: 49.9 us -> 49.3 us (0.988)
  waiting for transfers between devices: 10.5 us -> 8.29 us
  Pallas kernels: 18 us -> 19.6 us
    pallas_call x1 -> x2, Pallas kernels: 2.22 us -> 4.58 us  [the longest x1 3.15 us: feedback(): pl.pallas_call(functools.partial(feedback_kernel, groups), out_shape=[jax...]
    ppermute x15, waiting for transfers between devices: 10.5 us -> 8.29 us  [swap(): return lax.ppermute(x, axis, [(s, s ^ mask) for s in range(size)])]
    pallas_call x1, Pallas kernels: 3.4 us -> 2.65 us  [decode(): pl.pallas_call(functools.partial(decode_kernel, replicas, groups), out_sh...]
  transfers between devices with their start and end apart: 15 -> 15, of which waited for: 5 -> 4; matrix products, arithmetic and copies ran while one was open for 0% -> 0% of each run, Pallas kernels for 29% -> 34%
where the time goes in v5:
time: 49.3 us; the launch traced here: 49.1 us
  Pallas kernels  19.6 us (40%)
  starting transfers between devices  17.9 us (36%)
  waiting for transfers between devices  8.29 us (17%)
  local copies, waits for them, and re-layouts  2.42 us (5%)
  between operations  0.82 us (2%)
    ppermute x15, starting transfers between devices, swap(): return lax.ppermute(x, axis, [(s, s ^ mask) for s in range(size)])  17.9 us
    ppermute x15, waiting for transfers between devices, swap(): return lax.ppermute(x, axis, [(s, s ^ mask) for s in range(size)])  8.29 us
    pallas_call x1, Pallas kernels, inverse_index(): pl.pallas_call(inverse_index_kernel, out_shape=jax.ShapeDtypeStruct((bloc...  4.52 us
    pallas_call x1, Pallas kernels, moments(): pl.pallas_call(functools.partial(moment_kernel, groups), out_shape=[jax.S...  3.19 us
    pallas_call x1, Pallas kernels, feedback(): pl.pallas_call(functools.partial(feedback_kernel, groups), out_shape=[jax...  3.15 us
    pallas_call x1, Pallas kernels, early_moments(): pl.pallas_call(functools.partial(early_kernel, groups), out_shape=[jax.Sh...  2.75 us
    pallas_call x1, Pallas kernels, decode(): pl.pallas_call(functools.partial(decode_kernel, replicas, groups), out_sh...  2.65 us
    unnamed x22, local copies, waits for them, and re-layouts  2.4 us
  transfers between devices with their start and end apart: 15, of which 4 were waited for; matrix products, arithmetic and copies ran while one was open for 0% of the time, Pallas kernels for 34%

profile of v5, /device:TPU:0, one launch (start us, length us, event | category | flops | bytes accessed | tf_op | source)
XLA Modules:
  0.0 49.1 jit_solution(14692823862982964125)
XLA Ops:
  0.6 3.0 %collective-permute-start.3 = (bf16[192,512]{1,0:T(8,128)(2,1)}, bf16[192,512]{1,0:T(8,128)(2,1)S(1)}, u32[]{:S(2)}, u32[]{:S(2)}) collective-permute-start(bf16[192,512]{1,0:T(8,128)(2,1)} %refs_0_.3), channel_id=1, source_target_pairs={{0,1},{1,0},{2,3},{3,2},{4,5},{5,4},{6,7},{7,6},{8,9},{9,8},{10,11... | collective-permute-start | bytes 589832 | tf_op jit(solution)/shard_map/ppermute | solution.py:435
  3.6 1.5 %collective-permute-start.4 = (bf16[192,512]{1,0:T(8,128)(2,1)}, bf16[192,512]{1,0:T(8,128)(2,1)S(1)}, u32[]{:S(2)}, u32[]{:S(2)}) collective-permute-start(bf16[192,512]{1,0:T(8,128)(2,1)} %refs_0_.3), channel_id=1, source_target_pairs={{0,2},{1,3},{2,0},{3,1},{4,6},{5,7},{6,4},{7,5},{8,10},{9,11},{10,... | collective-permute-start | bytes 589832 | tf_op jit(solution)/shard_map/ppermute | solution.py:435
  5.2 0.1 pad_add_fusion.place_ref
  5.2 0.0 copy-start
  5.2 1.4 %copy-done = bf16[192,4096]{1,0:T(8,128)(2,1)S(1)} copy-done((bf16[192,4096]{1,0:T(8,128)(2,1)S(1)}, bf16[192,4096]{1,0:T(8,128)(2,1)}, u32[]{:S(2)}) %copy-start) | copy-done | bytes 1572888
  6.6 0.0 copy-start.5
  6.6 0.0 copy-start.10
  6.6 0.7 %cut.1 = (bf16[192,1024]{1,0:T(8,128)(2,1)S(1)}, bf16[192,1024]{1,0:T(8,128)(2,1)S(1)}, bf16[192,1024]{1,0:T(8,128)(2,1)S(1)}) custom-call(s32[2]{0:T(128)S(1)} %pad_add_fusion.place_ref, bf16[192,4096]{1,0:T(8,128)(2,1)S(1)} %copy-done), custom_call_target="tpu_custom_call" | custom-call | bytes 2359296 | tf_op jit(solution)/shard_map/cut/pallas_call | solution.py:101
  7.3 0.6 %collective-permute-start = (bf16[192,1024]{1,0:T(8,128)(2,1)S(1)}, bf16[192,1024]{1,0:T(8,128)(2,1)S(1)}, u32[]{:S(2)}, u32[]{:S(2)}) collective-permute-start(bf16[192,1024]{1,0:T(8,128)(2,1)S(1)} %get-tuple-element.27), channel_id=1, source_target_pairs={{0,1},{1,0},{2,3},{3,2},{4,5},{5,4},{6,7},{7,6},{8,9},{9,8},{10,11... | collective-permute-start | bytes 1179656 | tf_op jit(solution)/shard_map/ppermute | solution.py:435
  7.9 0.1 collective-permute-start.1
  8.0 2.9 %collective-permute-start.2 = (bf16[192,1024]{1,0:T(8,128)(2,1)S(1)}, bf16[192,1024]{1,0:T(8,128)(2,1)S(1)}, u32[]{:S(2)}, u32[]{:S(2)}) collective-permute-start(bf16[192,1024]{1,0:T(8,128)(2,1)S(1)} %get-tuple-element.29), channel_id=1, source_target_pairs={{0,3},{1,2},{2,1},{3,0},{4,7},{5,6},{6,5},{7,4},{8,11},{9,10},{10,... | collective-permute-start | bytes 1179656 | tf_op jit(solution)/shard_map/ppermute | solution.py:435
  10.9 0.0 copy-start.3
  10.9 0.9 %copy-done.3 = s32[4,32,512]{2,1,0:T(8,128)S(1)} copy-done((s32[4,32,512]{2,1,0:T(8,128)S(1)}, s32[4,32,512]{2,1,0:T(8,128)}, u32[]{:S(2)}) %copy-start.3) | copy-done | bytes 262168
  11.8 4.5 %inverse_index.1.inverse_ref = s32[4,256,512]{2,1,0:T(8,128)S(1)} custom-call(s32[4,32,512]{2,1,0:T(8,128)S(1)} %copy-done.3), custom_call_target="tpu_custom_call" | custom-call | flops 33554432 | bytes 2097152 | tf_op jit(solution)/shard_map/inverse_index/pallas_call | solution.py:68
  16.4 0.0 collective-permute-done.3.refs_3_.refs_1_
  16.4 0.6 %collective-permute-start.6 = (bf16[96,512]{1,0:T(8,128)(2,1)S(1)}, bf16[96,512]{1,0:T(8,128)(2,1)S(1)}, u32[]{:S(2)}, u32[]{:S(2)}) collective-permute-start(bf16[96,512]{1,0:T(8,128)(2,1)S(1)} %slice.9), channel_id=1, source_target_pairs={{0,2},{1,3},{2,0},{3,1},{4,6},{5,7},{6,4},{7,5},{8,10},{9,11},{10,... | collective-permute-start | bytes 294920 | tf_op jit(solution)/shard_map/ppermute | solution.py:435
  17.0 0.0 collective-permute-done.4.refs_2_
  17.0 0.0 copy-start.1
  17.0 0.0 copy-start.2
  17.0 0.0 copy-start.8
  17.0 0.0 copy-start.9
  17.0 0.1 collective-permute-start.5
  17.2 0.0 copy-done.5
  17.2 0.0 copy-done.10
  17.2 1.2 %input_gradients.1 = (bf16[192,1024]{1,0:T(8,128)(2,1)S(1)}, bf16[192,1024]{1,0:T(8,128)(2,1)S(1)}, bf16[192,1024]{1,0:T(8,128)(2,1)S(1)}) custom-call(bf16[192,512]{1,0:T(8,128)(2,1)S(1)} %copy-done.10, bf16[192,512]{1,0:T(8,128)(2,1)S(1)} %collective-permute-done.3.refs_3_.refs_1_, bf16[192,512]{1,0:T(8,128)(2,1)S(1)} %collective-permute-done.4.refs_2_, ...), custom_call_target="tpu_custom_call" | custom-call | flops 12079595520 | bytes 2818048 | tf_op jit(solution)/shard_map/input_gradients/pallas_call | solution.py:134
  18.4 1.1 %collective-permute-done.refs_1_ = bf16[192,1024]{1,0:T(8,128)(2,1)S(1)} collective-permute-done((bf16[192,1024]{1,0:T(8,128)(2,1)S(1)}, bf16[192,1024]{1,0:T(8,128)(2,1)S(1)}, u32[]{:S(2)}, u32[]{:S(2)}) %collective-permute-start) | collective-permute-done | bytes 393248 | tf_op jit(solution)/shard_map/ppermute | solution.py:435
  19.5 0.0 copy-start.4
  19.5 1.0 %collective-permute-start.8 = (bf16[192,1024]{1,0:T(8,128)(2,1)S(1)}, bf16[192,1024]{1,0:T(8,128)(2,1)S(1)}, u32[]{:S(2)}, u32[]{:S(2)}) collective-permute-start(bf16[192,1024]{1,0:T(8,128)(2,1)S(1)} %get-tuple-element.32), channel_id=1, source_target_pairs={{0,1},{1,0},{2,3},{3,2},{4,5},{5,4},{6,7},{7,6},{8,9},{9,8},{10,11... | collective-permute-start | bytes 1179656 | tf_op jit(solution)/shard_map/ppermute | solution.py:435
  20.4 0.0 copy-done.1
  20.4 0.0 copy-done.2
  20.4 0.0 copy-done.8
  20.4 0.0 copy-done.9
  20.4 2.8 %early_moment.1 = (f32[1024,512]{1,0:T(8,128)S(1)}, f32[1024,512]{1,0:T(8,128)S(1)}) custom-call(s32[2]{0:T(128)S(1)} %pad_add_fusion.place_ref, bf16[192,4096]{1,0:T(8,128)(2,1)S(1)} %copy-done.1, bf16[192,1024]{1,0:T(8,128)(2,1)S(1)} %collective-permute-done.refs_1_, bf16[192,512]{1,0:T(8,128)(2,1)S(1)} %copy-done.10, ...), custom_call_target="tpu_custom_call" | custom-call | flops 1207959552 | bytes 7077888 | tf_op jit(solution)/shard_map/early_moment/pallas_call | solution.py:174
  23.2 5.0 %collective-permute-done.1.refs_0_ = bf16[192,1024]{1,0:T(8,128)(2,1)S(1)} collective-permute-done((bf16[192,1024]{1,0:T(8,128)(2,1)S(1)}, bf16[192,1024]{1,0:T(8,128)(2,1)S(1)}, u32[]{:S(2)}, u32[]{:S(2)}) %collective-permute-start.1) | collective-permute-done | bytes 393248 | tf_op jit(solution)/shard_map/ppermute | solution.py:435
  28.2 1.8 %collective-permute-start.9 = (bf16[192,1024]{1,0:T(8,128)(2,1)S(1)}, bf16[192,1024]{1,0:T(8,128)(2,1)S(1)}, u32[]{:S(2)}, u32[]{:S(2)}) collective-permute-start(bf16[192,1024]{1,0:T(8,128)(2,1)S(1)} %get-tuple-element.33), channel_id=1, source_target_pairs={{0,2},{1,3},{2,0},{3,1},{4,6},{5,7},{6,4},{7,5},{8,10},{9,11},{10,... | collective-permute-start | bytes 1179656 | tf_op jit(solution)/shard_map/ppermute | solution.py:435
  30.0 0.0 collective-permute-done.2.refs_1_
  30.0 0.3 collective-permute-done.6.refs_4_
  30.3 0.0 collective-permute-done.5.refs_3_
  30.3 0.0 copy-done.4
  30.3 0.0 copy-start.6
  30.3 0.0 copy-start.7
  30.3 3.2 %moment.1 = (f32[1024,512]{1,0:T(8,128)S(1)}, f32[1024,512]{1,0:T(8,128)S(1)}, bf16[4,16,512]{2,1,0:T(8,128)(2,1)S(1)}, bf16[4,16,512]{2,1,0:T(8,128)(2,1)S(1)}, bf16[192,1024]{1,0:T(8,128)(2,1)S(1)}) custom-call(s32[2]{0:T(128)S(1)} %pad_add_fusion.place_ref, bf16[192,1024]{1,0:T(8,128)(2,1)S(1)} %collective-permute-done.1.refs_0_, ...), custom_call_target="tpu_custom_call" | custom-call | flops 1207959552 | bytes 8126464 | tf_op jit(solution)/shard_map/moment/pallas_call | solution.py:252
  33.5 0.1 collective-permute-start.7
  33.6 1.7 %collective-permute-start.14 = (bf16[192,1024]{1,0:T(8,128)(2,1)S(1)}, bf16[192,1024]{1,0:T(8,128)(2,1)S(1)}, u32[]{:S(2)}, u32[]{:S(2)}) collective-permute-start(bf16[192,1024]{1,0:T(8,128)(2,1)S(1)} %get-tuple-element.46), channel_id=1, source_target_pairs={{0,3},{1,2},{2,1},{3,0},{4,7},{5,6},{6,5},{7,4},{8,11},{9,10},{10,... | collective-permute-start | bytes 1179656 | tf_op jit(solution)/shard_map/ppermute | solution.py:435
  35.3 0.0 collective-permute-done.7
  35.4 3.7 %collective-permute-start.12 = (bf16[4,16,512]{2,1,0:T(8,128)(2,1)S(1)}, bf16[4,16,512]{2,1,0:T(8,128)(2,1)S(1)}, u32[]{:S(2)}, u32[]{:S(2)}) collective-permute-start(bf16[4,16,512]{2,1,0:T(8,128)(2,1)S(1)} %add_convert_fusion.1), channel_id=1, source_target_pairs={{0,24},{4,28},{8,16},{12,20},{16,8},{20,12},{24,0},{28,4},{1,25},{... | collective-permute-start | bytes 196616 | tf_op jit(solution)/shard_map/ppermute | solution.py:435
  39.0 0.0 collective-permute-start.11
  39.0 0.0 collective-permute-done.8.refs_1_
  39.0 0.0 collective-permute-done.9.refs_2_
  39.0 0.8 %collective-permute-start.10 = (bf16[4,16,512]{2,1,0:T(8,128)(2,1)S(1)}, bf16[4,16,512]{2,1,0:T(8,128)(2,1)S(1)}, u32[]{:S(2)}, u32[]{:S(2)}) collective-permute-start(bf16[4,16,512]{2,1,0:T(8,128)(2,1)S(1)} %add_convert_fusion.1), channel_id=1, source_target_pairs={{0,8},{4,12},{8,0},{12,4},{16,24},{20,28},{24,16},{28,20},{1,9},{5... | collective-permute-start | bytes 196616 | tf_op jit(solution)/shard_map/ppermute | solution.py:435
  39.8 0.0 copy-done.6
  39.8 0.0 copy-done.7
  39.8 3.2 %feedback.1 = (f32[1,1024,512]{2,1,0:T(8,128)}, bf16[192,4096]{1,0:T(8,128)(2,1)}) custom-call(s32[2]{0:T(128)S(1)} %pad_add_fusion.place_ref, f32[1024,512]{1,0:T(8,128)S(1)} %get-tuple-element.41.moment_ref, f32[1024,512]{1,0:T(8,128)S(1)} %get-tuple-element.42.coeffs_ref, s32[4,256,512]{2,1,0:T(8,128)S(1)} %inverse_index.1.inverse_ref, ...), custom_call_target="tpu_custom_call" | custom-call | flops 805306368 | bytes 10747904 | tf_op jit(solution)/shard_map/feedback/pallas_call | solution.py:301
  43.0 0.0 collective-permute-done.12
  43.0 1.9 %collective-permute-done.11 = bf16[4,16,512]{2,1,0:T(8,128)(2,1)S(1)} collective-permute-done((bf16[4,16,512]{2,1,0:T(8,128)(2,1)S(1)}, bf16[4,16,512]{2,1,0:T(8,128)(2,1)S(1)}, u32[]{:S(2)}, u32[]{:S(2)}) %collective-permute-start.11) | collective-permute-done | bytes 65568 | tf_op jit(solution)/shard_map/ppermute | solution.py:435
  44.9 0.0 collective-permute-done.10
  45.0 0.1 collective-permute-start.13
  45.0 1.4 %place_own.1.own_ref = f32[4,256,512]{2,1,0:T(8,128)S(1)} custom-call(s32[2]{0:T(128)S(1)} %pad_add_fusion.place_ref, bf16[4,16,512]{2,1,0:T(8,128)(2,1)S(1)} %add_convert_fusion.bands_ref, s32[4,256,512]{2,1,0:T(8,128)S(1)} %inverse_index.1.inverse_ref), custom_call_target="tpu_custom_call" | custom-call | flops 4194304 | bytes 4194304 | tf_op jit(solution)/shard_map/place_own/pallas_call | solution.py:350
  46.5 0.0 collective-permute-done.13.theirs_ref
  46.5 0.0 collective-permute-done.14.part_ref
  46.5 2.6 %decode.1 = (bf16[1024,512]{1,0:T(8,128)(2,1)}, bf16[192,4096]{1,0:T(8,128)(2,1)}) custom-call(s32[2]{0:T(128)S(1)} %pad_add_fusion.place_ref, f32[4,256,512]{2,1,0:T(8,128)S(1)} %place_own.1.own_ref, bf16[4,16,512]{2,1,0:T(8,128)(2,1)S(1)} %collective-permute-done.13.theirs_ref, ...), custom_call_target="tpu_custom_call", output_to_operand_aliasing={{1}: (7, {})} | custom-call | flops 805306368 | bytes 3932160 | tf_op jit(solution)/shard_map/decode/pallas_call | solution.py:406
  (4 shorter events, 0.1 us)
Async XLA Ops:
  0.6 15.7 %collective-permute-start.3 = (bf16[192,512]{1,0:T(8,128)(2,1)}, bf16[192,512]{1,0:T(8,128)(2,1)S(1)}, u32[]{:S(2)}, u32[]{:S(2)}) collective-permute-start(bf16[192,512]{1,0:T(8,128)(2,1)} %refs_0_.3), channel_id=1, source_target_pairs={{0,1},{1,0},{2,3},{3,2},{4,5},{5,4},{6,7},{7,6},{8,9},{9,8},{10,11... | collective-permute-start | bytes 589832 | tf_op jit(solution)/shard_map/ppermute | solution.py:435
  3.6 13.3 %collective-permute-start.4 = (bf16[192,512]{1,0:T(8,128)(2,1)}, bf16[192,512]{1,0:T(8,128)(2,1)S(1)}, u32[]{:S(2)}, u32[]{:S(2)}) collective-permute-start(bf16[192,512]{1,0:T(8,128)(2,1)} %refs_0_.3), channel_id=1, source_target_pairs={{0,2},{1,3},{2,0},{3,1},{4,6},{5,7},{6,4},{7,5},{8,10},{9,11},{10,... | collective-permute-start | bytes 589832 | tf_op jit(solution)/shard_map/ppermute | solution.py:435
  5.2 1.4 %copy-start = (bf16[192,4096]{1,0:T(8,128)(2,1)S(1)}, bf16[192,4096]{1,0:T(8,128)(2,1)}, u32[]{:S(2)}) copy-start(bf16[192,4096]{1,0:T(8,128)(2,1)} %refs_0_.2) | copy-start | bytes 4718596
  6.6 10.5 %copy-start.5 = (bf16[1024,512]{1,0:T(8,128)(2,1)S(1)}, bf16[1024,512]{1,0:T(8,128)(2,1)}, u32[]{:S(2)}) copy-start(bf16[1024,512]{1,0:T(8,128)(2,1)} %refs_5_.2) | copy-start | bytes 3145732
  6.6 10.6 %copy-start.10 = (bf16[192,512]{1,0:T(8,128)(2,1)S(1)}, bf16[192,512]{1,0:T(8,128)(2,1)}, u32[]{:S(2)}) copy-start(bf16[192,512]{1,0:T(8,128)(2,1)} %refs_0_.3) | copy-start | bytes 589828
  7.3 12.1 %collective-permute-start = (bf16[192,1024]{1,0:T(8,128)(2,1)S(1)}, bf16[192,1024]{1,0:T(8,128)(2,1)S(1)}, u32[]{:S(2)}, u32[]{:S(2)}) collective-permute-start(bf16[192,1024]{1,0:T(8,128)(2,1)S(1)} %get-tuple-element.27), channel_id=1, source_target_pairs={{0,1},{1,0},{2,3},{3,2},{4,5},{5,4},{6,7},{7,6},{8,9},{9,8},{10,11... | collective-permute-start | bytes 1179656 | tf_op jit(solution)/shard_map/ppermute | solution.py:435
  7.9 20.3 %collective-permute-start.1 = (bf16[192,1024]{1,0:T(8,128)(2,1)S(1)}, bf16[192,1024]{1,0:T(8,128)(2,1)S(1)}, u32[]{:S(2)}, u32[]{:S(2)}) collective-permute-start(bf16[192,1024]{1,0:T(8,128)(2,1)S(1)} %get-tuple-element.28), channel_id=1, source_target_pairs={{0,2},{1,3},{2,0},{3,1},{4,6},{5,7},{6,4},{7,5},{8,10},{9,11},{10,... | collective-permute-start | bytes 1179656 | tf_op jit(solution)/shard_map/ppermute | solution.py:435
  8.0 22.1 %collective-permute-start.2 = (bf16[192,1024]{1,0:T(8,128)(2,1)S(1)}, bf16[192,1024]{1,0:T(8,128)(2,1)S(1)}, u32[]{:S(2)}, u32[]{:S(2)}) collective-permute-start(bf16[192,1024]{1,0:T(8,128)(2,1)S(1)} %get-tuple-element.29), channel_id=1, source_target_pairs={{0,3},{1,2},{2,1},{3,0},{4,7},{5,6},{6,5},{7,4},{8,11},{9,10},{10,... | collective-permute-start | bytes 1179656 | tf_op jit(solution)/shard_map/ppermute | solution.py:435
  10.9 0.9 %copy-start.3 = (s32[4,32,512]{2,1,0:T(8,128)S(1)}, s32[4,32,512]{2,1,0:T(8,128)}, u32[]{:S(2)}) copy-start(s32[4,32,512]{2,1,0:T(8,128)} %refs_8_.1) | copy-start | bytes 786436
  16.4 13.9 %collective-permute-start.6 = (bf16[96,512]{1,0:T(8,128)(2,1)S(1)}, bf16[96,512]{1,0:T(8,128)(2,1)S(1)}, u32[]{:S(2)}, u32[]{:S(2)}) collective-permute-start(bf16[96,512]{1,0:T(8,128)(2,1)S(1)} %slice.9), channel_id=1, source_target_pairs={{0,2},{1,3},{2,0},{3,1},{4,6},{5,7},{6,4},{7,5},{8,10},{9,11},{10,... | collective-permute-start | bytes 294920 | tf_op jit(solution)/shard_map/ppermute | solution.py:435
  17.0 3.4 %copy-start.1 = (bf16[192,4096]{1,0:T(8,128)(2,1)S(1)}, bf16[192,4096]{1,0:T(8,128)(2,1)}, u32[]{:S(2)}) copy-start(bf16[192,4096]{1,0:T(8,128)(2,1)} %refs_0_.2) | copy-start | bytes 4718596
  17.0 3.4 %copy-start.2 = (f32[1,1024,512]{2,1,0:T(8,128)S(1)}, f32[1,1024,512]{2,1,0:T(8,128)}, u32[]{:S(2)}) copy-start(f32[1,1024,512]{2,1,0:T(8,128)} %refs_4_.1) | copy-start | bytes 6291460
  17.0 3.4 %copy-start.8 = (bf16[256,256]{1,0:T(8,128)(2,1)S(1)}, bf16[256,256]{1,0:T(8,128)(2,1)}, u32[]{:S(2)}) copy-start(bf16[256,256]{1,0:T(8,128)(2,1)} %constant.31.clone.refs_6_.refs_10_) | copy-start | bytes 393220
  17.0 3.4 %copy-start.9 = (bf16[256,256]{1,0:T(8,128)(2,1)S(1)}, bf16[256,256]{1,0:T(8,128)(2,1)}, u32[]{:S(2)}) copy-start(bf16[256,256]{1,0:T(8,128)(2,1)} %constant.30.clone.refs_5_.refs_9_) | copy-start | bytes 393220
  17.0 13.3 %collective-permute-start.5 = (bf16[96,512]{1,0:T(8,128)(2,1)S(1)}, bf16[96,512]{1,0:T(8,128)(2,1)S(1)}, u32[]{:S(2)}, u32[]{:S(2)}) collective-permute-start(bf16[96,512]{1,0:T(8,128)(2,1)S(1)} %slice.8), channel_id=1, source_target_pairs={{0,1},{1,0},{2,3},{3,2},{4,5},{5,4},{6,7},{7,6},{8,9},{9,8},{10,11... | collective-permute-start | bytes 294920 | tf_op jit(solution)/shard_map/ppermute | solution.py:435
  19.5 10.9 %copy-start.4 = (s32[4,32,512]{2,1,0:T(8,128)S(1)}, s32[4,32,512]{2,1,0:T(8,128)}, u32[]{:S(2)}) copy-start(s32[4,32,512]{2,1,0:T(8,128)} %refs_8_.1) | copy-start | bytes 786436
  19.5 19.6 %collective-permute-start.8 = (bf16[192,1024]{1,0:T(8,128)(2,1)S(1)}, bf16[192,1024]{1,0:T(8,128)(2,1)S(1)}, u32[]{:S(2)}, u32[]{:S(2)}) collective-permute-start(bf16[192,1024]{1,0:T(8,128)(2,1)S(1)} %get-tuple-element.32), channel_id=1, source_target_pairs={{0,1},{1,0},{2,3},{3,2},{4,5},{5,4},{6,7},{7,6},{8,9},{9,8},{10,11... | collective-permute-start | bytes 1179656 | tf_op jit(solution)/shard_map/ppermute | solution.py:435
  28.2 10.8 %collective-permute-start.9 = (bf16[192,1024]{1,0:T(8,128)(2,1)S(1)}, bf16[192,1024]{1,0:T(8,128)(2,1)S(1)}, u32[]{:S(2)}, u32[]{:S(2)}) collective-permute-start(bf16[192,1024]{1,0:T(8,128)(2,1)S(1)} %get-tuple-element.33), channel_id=1, source_target_pairs={{0,2},{1,3},{2,0},{3,1},{4,6},{5,7},{6,4},{7,5},{8,10},{9,11},{10,... | collective-permute-start | bytes 1179656 | tf_op jit(solution)/shard_map/ppermute | solution.py:435
  30.3 9.5 %copy-start.6 = (bf16[256,256]{1,0:T(8,128)(2,1)S(1)}, bf16[256,256]{1,0:T(8,128)(2,1)}, u32[]{:S(2)}) copy-start(bf16[256,256]{1,0:T(8,128)(2,1)} %constant.33.clone.low_ref) | copy-start | bytes 393220
  30.3 9.5 %copy-start.7 = (bf16[256,256]{1,0:T(8,128)(2,1)S(1)}, bf16[256,256]{1,0:T(8,128)(2,1)}, u32[]{:S(2)}) copy-start(bf16[256,256]{1,0:T(8,128)(2,1)} %constant.32.clone.high_ref) | copy-start | bytes 393220
  33.5 1.8 %collective-permute-start.7 = (bf16[4,16,512]{2,1,0:T(8,128)(2,1)S(1)}, bf16[4,16,512]{2,1,0:T(8,128)(2,1)S(1)}, u32[]{:S(2)}, u32[]{:S(2)}) collective-permute-start(bf16[4,16,512]{2,1,0:T(8,128)(2,1)S(1)} %get-tuple-element.39), channel_id=1, source_target_pairs={{0,4},{4,0},{8,12},{12,8},{16,20},{20,16},{24,28},{28,24},{1,5},{5... | collective-permute-start | bytes 196616 | tf_op jit(solution)/shard_map/ppermute | solution.py:435
  33.6 12.9 %collective-permute-start.14 = (bf16[192,1024]{1,0:T(8,128)(2,1)S(1)}, bf16[192,1024]{1,0:T(8,128)(2,1)S(1)}, u32[]{:S(2)}, u32[]{:S(2)}) collective-permute-start(bf16[192,1024]{1,0:T(8,128)(2,1)S(1)} %get-tuple-element.46), channel_id=1, source_target_pairs={{0,3},{1,2},{2,1},{3,0},{4,7},{5,6},{6,5},{7,4},{8,11},{9,10},{10,... | collective-permute-start | bytes 1179656 | tf_op jit(solution)/shard_map/ppermute | solution.py:435
  35.4 7.6 %collective-permute-start.12 = (bf16[4,16,512]{2,1,0:T(8,128)(2,1)S(1)}, bf16[4,16,512]{2,1,0:T(8,128)(2,1)S(1)}, u32[]{:S(2)}, u32[]{:S(2)}) collective-permute-start(bf16[4,16,512]{2,1,0:T(8,128)(2,1)S(1)} %add_convert_fusion.1), channel_id=1, source_target_pairs={{0,24},{4,28},{8,16},{12,20},{16,8},{20,12},{24,0},{28,4},{1,25},{... | collective-permute-start | bytes 196616 | tf_op jit(solution)/shard_map/ppermute | solution.py:435
  39.0 5.9 %collective-permute-start.11 = (bf16[4,16,512]{2,1,0:T(8,128)(2,1)S(1)}, bf16[4,16,512]{2,1,0:T(8,128)(2,1)S(1)}, u32[]{:S(2)}, u32[]{:S(2)}) collective-permute-start(bf16[4,16,512]{2,1,0:T(8,128)(2,1)S(1)} %add_convert_fusion.1), channel_id=1, source_target_pairs={{0,16},{4,20},{8,24},{12,28},{16,0},{20,4},{24,8},{28,12},{1,17},{... | collective-permute-start | bytes 196616 | tf_op jit(solution)/shard_map/ppermute | solution.py:435
  39.0 5.9 %collective-permute-start.10 = (bf16[4,16,512]{2,1,0:T(8,128)(2,1)S(1)}, bf16[4,16,512]{2,1,0:T(8,128)(2,1)S(1)}, u32[]{:S(2)}, u32[]{:S(2)}) collective-permute-start(bf16[4,16,512]{2,1,0:T(8,128)(2,1)S(1)} %add_convert_fusion.1), channel_id=1, source_target_pairs={{0,8},{4,12},{8,0},{12,4},{16,24},{20,28},{24,16},{28,20},{1,9},{5... | collective-permute-start | bytes 196616 | tf_op jit(solution)/shard_map/ppermute | solution.py:435
  45.0 1.5 %collective-permute-start.13 = (bf16[4,16,512]{2,1,0:T(8,128)(2,1)S(1)}, bf16[4,16,512]{2,1,0:T(8,128)(2,1)S(1)}, u32[]{:S(2)}, u32[]{:S(2)}) collective-permute-start(bf16[4,16,512]{2,1,0:T(8,128)(2,1)S(1)} %add_convert_fusion.bands_ref), channel_id=1, source_target_pairs={{0,4},{4,0},{8,12},{12,8},{16,20},{20,16},{24,28},{28,24},{1,5},{5... | collective-permute-start | bytes 196616 | tf_op jit(solution)/shard_map/ppermute | solution.py:435

commit v6 on v5

--- a/solution.py
+++ b/solution.py
@@ -333,7 +333,8 @@
             inside, group = pick & (SUBLANES - 1), (pick >> 3) - first
             total = before(at)
             for s, tile in enumerate(source):
-                total = jnp.where(group == s, jnp.take_along_axis(tile, inside, axis=0), total)
+                found = jnp.take_along_axis(tile, inside, axis=0, mode="promise_in_bounds")
+                total = jnp.where(group == s, found, total)
             yield at, total
 
 
@@ -382,13 +383,19 @@
     copies = start_copies(groups - 1, place_ref, [part_ref], whole_ref, part_sems)
     blocks, half, _ = theirs_ref.shape
     first = (1 - place_ref[1]) * (half // SUBLANES)
-    for b in range(blocks):
+
+    def put(b):
         placed = lambda at: own_ref[b, *at]
         for at, tile in put_in_place(theirs_ref, inverse_ref, b, first, placed):
             dense_ref[b, *at] = tile
+
+    put(0)
+    for b in range(blocks):
         dense = dense_ref[b].astype(jnp.bfloat16)
-        update = (dot(high_ref[...], dense) + dot(low_ref[...], dense)) * (1.0 / replicas)
-        held_ref[b] = update.astype(jnp.bfloat16)
+        update = dot(high_ref[...], dense) + dot(low_ref[...], dense)
+        if b + 1 < blocks:
+            put(b + 1)
+        held_ref[b] = (update * (1.0 / replicas)).astype(jnp.bfloat16)
         copies.append(
             pltpu.make_async_copy(
                 held_ref.at[b], update_ref.at[b * SPAN : (b + 1) * SPAN, :], sems.at[b]

time: 49.3 us -> 49.3 us (level)
  no operation moved by 1% of the time
where the time goes in v6:
time: 49.3 us; the launch traced here: 49.1 us
  Pallas kernels  19.6 us (40%)
  starting transfers between devices  17.9 us (36%)
  waiting for transfers between devices  8.29 us (17%)
  local copies, waits for them, and re-layouts  2.42 us (5%)
  between operations  0.82 us (2%)
    ppermute x15, starting transfers between devices, swap(): return lax.ppermute(x, axis, [(s, s ^ mask) for s in range(size)])  17.9 us
    ppermute x15, waiting for transfers between devices, swap(): return lax.ppermute(x, axis, [(s, s ^ mask) for s in range(size)])  8.29 us
    pallas_call x1, Pallas kernels, inverse_index(): pl.pallas_call(inverse_index_kernel, out_shape=jax.ShapeDtypeStruct((bloc...  4.52 us
    pallas_call x1, Pallas kernels, moments(): pl.pallas_call(functools.partial(moment_kernel, groups), out_shape=[jax.S...  3.19 us
    pallas_call x1, Pallas kernels, feedback(): pl.pallas_call(functools.partial(feedback_kernel, groups), out_shape=[jax...  3.15 us
    pallas_call x1, Pallas kernels, early_moments(): pl.pallas_call(functools.partial(early_kernel, groups), out_shape=[jax.Sh...  2.75 us
    pallas_call x1, Pallas kernels, decode(): pl.pallas_call(functools.partial(decode_kernel, replicas, groups), out_sh...  2.64 us
    unnamed x22, local copies, waits for them, and re-layouts  2.4 us
  transfers between devices with their start and end apart: 15, of which 4 were waited for; matrix products, arithmetic and copies ran while one was open for 0% of the time, Pallas kernels for 34%

profile of v6, /device:TPU:0, one launch (start us, length us, event | category | flops | bytes accessed | tf_op | source)
XLA Modules:
  0.0 49.1 jit_solution(1951129376090618672)
XLA Ops:
  0.6 3.0 %collective-permute-start.3 = (bf16[192,512]{1,0:T(8,128)(2,1)}, bf16[192,512]{1,0:T(8,128)(2,1)S(1)}, u32[]{:S(2)}, u32[]{:S(2)}) collective-permute-start(bf16[192,512]{1,0:T(8,128)(2,1)} %refs_0_.3), channel_id=1, source_target_pairs={{0,1},{1,0},{2,3},{3,2},{4,5},{5,4},{6,7},{7,6},{8,9},{9,8},{10,11... | collective-permute-start | bytes 589832 | tf_op jit(solution)/shard_map/ppermute | solution.py:442
  3.6 1.5 %collective-permute-start.4 = (bf16[192,512]{1,0:T(8,128)(2,1)}, bf16[192,512]{1,0:T(8,128)(2,1)S(1)}, u32[]{:S(2)}, u32[]{:S(2)}) collective-permute-start(bf16[192,512]{1,0:T(8,128)(2,1)} %refs_0_.3), channel_id=1, source_target_pairs={{0,2},{1,3},{2,0},{3,1},{4,6},{5,7},{6,4},{7,5},{8,10},{9,11},{10,... | collective-permute-start | bytes 589832 | tf_op jit(solution)/shard_map/ppermute | solution.py:442
  5.2 0.1 pad_add_fusion.place_ref
  5.2 0.0 copy-start
  5.2 1.4 %copy-done = bf16[192,4096]{1,0:T(8,128)(2,1)S(1)} copy-done((bf16[192,4096]{1,0:T(8,128)(2,1)S(1)}, bf16[192,4096]{1,0:T(8,128)(2,1)}, u32[]{:S(2)}) %copy-start) | copy-done | bytes 1572888
  6.6 0.0 copy-start.5
  6.6 0.0 copy-start.10
  6.6 0.7 %cut.1 = (bf16[192,1024]{1,0:T(8,128)(2,1)S(1)}, bf16[192,1024]{1,0:T(8,128)(2,1)S(1)}, bf16[192,1024]{1,0:T(8,128)(2,1)S(1)}) custom-call(s32[2]{0:T(128)S(1)} %pad_add_fusion.place_ref, bf16[192,4096]{1,0:T(8,128)(2,1)S(1)} %copy-done), custom_call_target="tpu_custom_call" | custom-call | bytes 2359296 | tf_op jit(solution)/shard_map/cut/pallas_call | solution.py:101
  7.3 0.6 %collective-permute-start = (bf16[192,1024]{1,0:T(8,128)(2,1)S(1)}, bf16[192,1024]{1,0:T(8,128)(2,1)S(1)}, u32[]{:S(2)}, u32[]{:S(2)}) collective-permute-start(bf16[192,1024]{1,0:T(8,128)(2,1)S(1)} %get-tuple-element.27), channel_id=1, source_target_pairs={{0,1},{1,0},{2,3},{3,2},{4,5},{5,4},{6,7},{7,6},{8,9},{9,8},{10,11... | collective-permute-start | bytes 1179656 | tf_op jit(solution)/shard_map/ppermute | solution.py:442
  7.9 0.1 collective-permute-start.1
  8.0 2.9 %collective-permute-start.2 = (bf16[192,1024]{1,0:T(8,128)(2,1)S(1)}, bf16[192,1024]{1,0:T(8,128)(2,1)S(1)}, u32[]{:S(2)}, u32[]{:S(2)}) collective-permute-start(bf16[192,1024]{1,0:T(8,128)(2,1)S(1)} %get-tuple-element.29), channel_id=1, source_target_pairs={{0,3},{1,2},{2,1},{3,0},{4,7},{5,6},{6,5},{7,4},{8,11},{9,10},{10,... | collective-permute-start | bytes 1179656 | tf_op jit(solution)/shard_map/ppermute | solution.py:442
  10.9 0.0 copy-start.3
  10.9 0.9 %copy-done.3 = s32[4,32,512]{2,1,0:T(8,128)S(1)} copy-done((s32[4,32,512]{2,1,0:T(8,128)S(1)}, s32[4,32,512]{2,1,0:T(8,128)}, u32[]{:S(2)}) %copy-start.3) | copy-done | bytes 262168
  11.8 4.5 %inverse_index.1.inverse_ref = s32[4,256,512]{2,1,0:T(8,128)S(1)} custom-call(s32[4,32,512]{2,1,0:T(8,128)S(1)} %copy-done.3), custom_call_target="tpu_custom_call" | custom-call | flops 33554432 | bytes 2097152 | tf_op jit(solution)/shard_map/inverse_index/pallas_call | solution.py:68
  16.4 0.0 collective-permute-done.3.refs_3_.refs_1_
  16.4 0.6 %collective-permute-start.6 = (bf16[96,512]{1,0:T(8,128)(2,1)S(1)}, bf16[96,512]{1,0:T(8,128)(2,1)S(1)}, u32[]{:S(2)}, u32[]{:S(2)}) collective-permute-start(bf16[96,512]{1,0:T(8,128)(2,1)S(1)} %slice.9), channel_id=1, source_target_pairs={{0,2},{1,3},{2,0},{3,1},{4,6},{5,7},{6,4},{7,5},{8,10},{9,11},{10,... | collective-permute-start | bytes 294920 | tf_op jit(solution)/shard_map/ppermute | solution.py:442
  17.0 0.0 collective-permute-done.4.refs_2_
  17.0 0.0 copy-start.1
  17.0 0.0 copy-start.2
  17.0 0.0 copy-start.8
  17.0 0.0 copy-start.9
  17.0 0.1 collective-permute-start.5
  17.2 0.0 copy-done.5
  17.2 0.0 copy-done.10
  17.2 1.2 %input_gradients.1 = (bf16[192,1024]{1,0:T(8,128)(2,1)S(1)}, bf16[192,1024]{1,0:T(8,128)(2,1)S(1)}, bf16[192,1024]{1,0:T(8,128)(2,1)S(1)}) custom-call(bf16[192,512]{1,0:T(8,128)(2,1)S(1)} %copy-done.10, bf16[192,512]{1,0:T(8,128)(2,1)S(1)} %collective-permute-done.3.refs_3_.refs_1_, bf16[192,512]{1,0:T(8,128)(2,1)S(1)} %collective-permute-done.4.refs_2_, ...), custom_call_target="tpu_custom_call" | custom-call | flops 12079595520 | bytes 2818048 | tf_op jit(solution)/shard_map/input_gradients/pallas_call | solution.py:134
  18.4 1.1 %collective-permute-done.refs_1_ = bf16[192,1024]{1,0:T(8,128)(2,1)S(1)} collective-permute-done((bf16[192,1024]{1,0:T(8,128)(2,1)S(1)}, bf16[192,1024]{1,0:T(8,128)(2,1)S(1)}, u32[]{:S(2)}, u32[]{:S(2)}) %collective-permute-start) | collective-permute-done | bytes 393248 | tf_op jit(solution)/shard_map/ppermute | solution.py:442
  19.5 0.0 copy-start.4
  19.5 1.0 %collective-permute-start.8 = (bf16[192,1024]{1,0:T(8,128)(2,1)S(1)}, bf16[192,1024]{1,0:T(8,128)(2,1)S(1)}, u32[]{:S(2)}, u32[]{:S(2)}) collective-permute-start(bf16[192,1024]{1,0:T(8,128)(2,1)S(1)} %get-tuple-element.32), channel_id=1, source_target_pairs={{0,1},{1,0},{2,3},{3,2},{4,5},{5,4},{6,7},{7,6},{8,9},{9,8},{10,11... | collective-permute-start | bytes 1179656 | tf_op jit(solution)/shard_map/ppermute | solution.py:442
  20.4 0.0 copy-done.1
  20.4 0.0 copy-done.2
  20.4 0.0 copy-done.8
  20.4 0.0 copy-done.9
  20.4 2.8 %early_moment.1 = (f32[1024,512]{1,0:T(8,128)S(1)}, f32[1024,512]{1,0:T(8,128)S(1)}) custom-call(s32[2]{0:T(128)S(1)} %pad_add_fusion.place_ref, bf16[192,4096]{1,0:T(8,128)(2,1)S(1)} %copy-done.1, bf16[192,1024]{1,0:T(8,128)(2,1)S(1)} %collective-permute-done.refs_1_, bf16[192,512]{1,0:T(8,128)(2,1)S(1)} %copy-done.10, ...), custom_call_target="tpu_custom_call" | custom-call | flops 1207959552 | bytes 7077888 | tf_op jit(solution)/shard_map/early_moment/pallas_call | solution.py:174
  23.2 5.0 %collective-permute-done.1.refs_0_ = bf16[192,1024]{1,0:T(8,128)(2,1)S(1)} collective-permute-done((bf16[192,1024]{1,0:T(8,128)(2,1)S(1)}, bf16[192,1024]{1,0:T(8,128)(2,1)S(1)}, u32[]{:S(2)}, u32[]{:S(2)}) %collective-permute-start.1) | collective-permute-done | bytes 393248 | tf_op jit(solution)/shard_map/ppermute | solution.py:442
  28.2 1.8 %collective-permute-start.9 = (bf16[192,1024]{1,0:T(8,128)(2,1)S(1)}, bf16[192,1024]{1,0:T(8,128)(2,1)S(1)}, u32[]{:S(2)}, u32[]{:S(2)}) collective-permute-start(bf16[192,1024]{1,0:T(8,128)(2,1)S(1)} %get-tuple-element.33), channel_id=1, source_target_pairs={{0,2},{1,3},{2,0},{3,1},{4,6},{5,7},{6,4},{7,5},{8,10},{9,11},{10,... | collective-permute-start | bytes 1179656 | tf_op jit(solution)/shard_map/ppermute | solution.py:442
  30.0 0.0 collective-permute-done.2.refs_1_
  30.0 0.3 collective-permute-done.6.refs_4_
  30.3 0.0 collective-permute-done.5.refs_3_
  30.3 0.0 copy-done.4
  30.3 0.0 copy-start.6
  30.3 0.0 copy-start.7
  30.3 3.2 %moment.1 = (f32[1024,512]{1,0:T(8,128)S(1)}, f32[1024,512]{1,0:T(8,128)S(1)}, bf16[4,16,512]{2,1,0:T(8,128)(2,1)S(1)}, bf16[4,16,512]{2,1,0:T(8,128)(2,1)S(1)}, bf16[192,1024]{1,0:T(8,128)(2,1)S(1)}) custom-call(s32[2]{0:T(128)S(1)} %pad_add_fusion.place_ref, bf16[192,1024]{1,0:T(8,128)(2,1)S(1)} %collective-permute-done.1.refs_0_, ...), custom_call_target="tpu_custom_call" | custom-call | flops 1207959552 | bytes 8126464 | tf_op jit(solution)/shard_map/moment/pallas_call | solution.py:252
  33.5 0.1 collective-permute-start.7
  33.6 1.7 %collective-permute-start.14 = (bf16[192,1024]{1,0:T(8,128)(2,1)S(1)}, bf16[192,1024]{1,0:T(8,128)(2,1)S(1)}, u32[]{:S(2)}, u32[]{:S(2)}) collective-permute-start(bf16[192,1024]{1,0:T(8,128)(2,1)S(1)} %get-tuple-element.46), channel_id=1, source_target_pairs={{0,3},{1,2},{2,1},{3,0},{4,7},{5,6},{6,5},{7,4},{8,11},{9,10},{10,... | collective-permute-start | bytes 1179656 | tf_op jit(solution)/shard_map/ppermute | solution.py:442
  35.3 0.0 collective-permute-done.7
  35.4 3.7 %collective-permute-start.12 = (bf16[4,16,512]{2,1,0:T(8,128)(2,1)S(1)}, bf16[4,16,512]{2,1,0:T(8,128)(2,1)S(1)}, u32[]{:S(2)}, u32[]{:S(2)}) collective-permute-start(bf16[4,16,512]{2,1,0:T(8,128)(2,1)S(1)} %add_convert_fusion.1), channel_id=1, source_target_pairs={{0,24},{4,28},{8,16},{12,20},{16,8},{20,12},{24,0},{28,4},{1,25},{... | collective-permute-start | bytes 196616 | tf_op jit(solution)/shard_map/ppermute | solution.py:442
  39.0 0.0 collective-permute-start.11
  39.0 0.0 collective-permute-done.8.refs_1_
  39.0 0.0 collective-permute-done.9.refs_2_
  39.0 0.8 %collective-permute-start.10 = (bf16[4,16,512]{2,1,0:T(8,128)(2,1)S(1)}, bf16[4,16,512]{2,1,0:T(8,128)(2,1)S(1)}, u32[]{:S(2)}, u32[]{:S(2)}) collective-permute-start(bf16[4,16,512]{2,1,0:T(8,128)(2,1)S(1)} %add_convert_fusion.1), channel_id=1, source_target_pairs={{0,8},{4,12},{8,0},{12,4},{16,24},{20,28},{24,16},{28,20},{1,9},{5... | collective-permute-start | bytes 196616 | tf_op jit(solution)/shard_map/ppermute | solution.py:442
  39.8 0.0 copy-done.6
  39.8 0.0 copy-done.7
  39.8 3.2 %feedback.1 = (f32[1,1024,512]{2,1,0:T(8,128)}, bf16[192,4096]{1,0:T(8,128)(2,1)}) custom-call(s32[2]{0:T(128)S(1)} %pad_add_fusion.place_ref, f32[1024,512]{1,0:T(8,128)S(1)} %get-tuple-element.41.moment_ref, f32[1024,512]{1,0:T(8,128)S(1)} %get-tuple-element.42.coeffs_ref, s32[4,256,512]{2,1,0:T(8,128)S(1)} %inverse_index.1.inverse_ref, ...), custom_call_target="tpu_custom_call" | custom-call | flops 805306368 | bytes 10747904 | tf_op jit(solution)/shard_map/feedback/pallas_call | solution.py:301
  43.0 0.0 collective-permute-done.12
  43.0 1.9 %collective-permute-done.11 = bf16[4,16,512]{2,1,0:T(8,128)(2,1)S(1)} collective-permute-done((bf16[4,16,512]{2,1,0:T(8,128)(2,1)S(1)}, bf16[4,16,512]{2,1,0:T(8,128)(2,1)S(1)}, u32[]{:S(2)}, u32[]{:S(2)}) %collective-permute-start.11) | collective-permute-done | bytes 65568 | tf_op jit(solution)/shard_map/ppermute | solution.py:442
  44.9 0.0 collective-permute-done.10
  45.0 0.1 collective-permute-start.13
  45.0 1.4 %place_own.1.own_ref = f32[4,256,512]{2,1,0:T(8,128)S(1)} custom-call(s32[2]{0:T(128)S(1)} %pad_add_fusion.place_ref, bf16[4,16,512]{2,1,0:T(8,128)(2,1)S(1)} %add_convert_fusion.bands_ref, s32[4,256,512]{2,1,0:T(8,128)S(1)} %inverse_index.1.inverse_ref), custom_call_target="tpu_custom_call" | custom-call | flops 4194304 | bytes 4194304 | tf_op jit(solution)/shard_map/place_own/pallas_call | solution.py:351
  46.5 0.0 collective-permute-done.13.theirs_ref
  46.5 0.0 collective-permute-done.14.part_ref
  46.5 2.6 %decode.1 = (bf16[1024,512]{1,0:T(8,128)(2,1)}, bf16[192,4096]{1,0:T(8,128)(2,1)}) custom-call(s32[2]{0:T(128)S(1)} %pad_add_fusion.place_ref, f32[4,256,512]{2,1,0:T(8,128)S(1)} %place_own.1.own_ref, bf16[4,16,512]{2,1,0:T(8,128)(2,1)S(1)} %collective-permute-done.13.theirs_ref, ...), custom_call_target="tpu_custom_call", output_to_operand_aliasing={{1}: (7, {})} | custom-call | flops 805306368 | bytes 3932160 | tf_op jit(solution)/shard_map/decode/pallas_call | solution.py:413
  (4 shorter events, 0.1 us)
Async XLA Ops:
  0.6 15.7 %collective-permute-start.3 = (bf16[192,512]{1,0:T(8,128)(2,1)}, bf16[192,512]{1,0:T(8,128)(2,1)S(1)}, u32[]{:S(2)}, u32[]{:S(2)}) collective-permute-start(bf16[192,512]{1,0:T(8,128)(2,1)} %refs_0_.3), channel_id=1, source_target_pairs={{0,1},{1,0},{2,3},{3,2},{4,5},{5,4},{6,7},{7,6},{8,9},{9,8},{10,11... | collective-permute-start | bytes 589832 | tf_op jit(solution)/shard_map/ppermute | solution.py:442
  3.6 13.3 %collective-permute-start.4 = (bf16[192,512]{1,0:T(8,128)(2,1)}, bf16[192,512]{1,0:T(8,128)(2,1)S(1)}, u32[]{:S(2)}, u32[]{:S(2)}) collective-permute-start(bf16[192,512]{1,0:T(8,128)(2,1)} %refs_0_.3), channel_id=1, source_target_pairs={{0,2},{1,3},{2,0},{3,1},{4,6},{5,7},{6,4},{7,5},{8,10},{9,11},{10,... | collective-permute-start | bytes 589832 | tf_op jit(solution)/shard_map/ppermute | solution.py:442
  5.2 1.4 %copy-start = (bf16[192,4096]{1,0:T(8,128)(2,1)S(1)}, bf16[192,4096]{1,0:T(8,128)(2,1)}, u32[]{:S(2)}) copy-start(bf16[192,4096]{1,0:T(8,128)(2,1)} %refs_0_.2) | copy-start | bytes 4718596
  6.6 10.5 %copy-start.5 = (bf16[1024,512]{1,0:T(8,128)(2,1)S(1)}, bf16[1024,512]{1,0:T(8,128)(2,1)}, u32[]{:S(2)}) copy-start(bf16[1024,512]{1,0:T(8,128)(2,1)} %refs_5_.2) | copy-start | bytes 3145732
  6.6 10.6 %copy-start.10 = (bf16[192,512]{1,0:T(8,128)(2,1)S(1)}, bf16[192,512]{1,0:T(8,128)(2,1)}, u32[]{:S(2)}) copy-start(bf16[192,512]{1,0:T(8,128)(2,1)} %refs_0_.3) | copy-start | bytes 589828
  7.3 12.1 %collective-permute-start = (bf16[192,1024]{1,0:T(8,128)(2,1)S(1)}, bf16[192,1024]{1,0:T(8,128)(2,1)S(1)}, u32[]{:S(2)}, u32[]{:S(2)}) collective-permute-start(bf16[192,1024]{1,0:T(8,128)(2,1)S(1)} %get-tuple-element.27), channel_id=1, source_target_pairs={{0,1},{1,0},{2,3},{3,2},{4,5},{5,4},{6,7},{7,6},{8,9},{9,8},{10,11... | collective-permute-start | bytes 1179656 | tf_op jit(solution)/shard_map/ppermute | solution.py:442
  7.9 20.3 %collective-permute-start.1 = (bf16[192,1024]{1,0:T(8,128)(2,1)S(1)}, bf16[192,1024]{1,0:T(8,128)(2,1)S(1)}, u32[]{:S(2)}, u32[]{:S(2)}) collective-permute-start(bf16[192,1024]{1,0:T(8,128)(2,1)S(1)} %get-tuple-element.28), channel_id=1, source_target_pairs={{0,2},{1,3},{2,0},{3,1},{4,6},{5,7},{6,4},{7,5},{8,10},{9,11},{10,... | collective-permute-start | bytes 1179656 | tf_op jit(solution)/shard_map/ppermute | solution.py:442
  8.0 22.1 %collective-permute-start.2 = (bf16[192,1024]{1,0:T(8,128)(2,1)S(1)}, bf16[192,1024]{1,0:T(8,128)(2,1)S(1)}, u32[]{:S(2)}, u32[]{:S(2)}) collective-permute-start(bf16[192,1024]{1,0:T(8,128)(2,1)S(1)} %get-tuple-element.29), channel_id=1, source_target_pairs={{0,3},{1,2},{2,1},{3,0},{4,7},{5,6},{6,5},{7,4},{8,11},{9,10},{10,... | collective-permute-start | bytes 1179656 | tf_op jit(solution)/shard_map/ppermute | solution.py:442
  10.9 0.9 %copy-start.3 = (s32[4,32,512]{2,1,0:T(8,128)S(1)}, s32[4,32,512]{2,1,0:T(8,128)}, u32[]{:S(2)}) copy-start(s32[4,32,512]{2,1,0:T(8,128)} %refs_8_.1) | copy-start | bytes 786436
  16.4 13.9 %collective-permute-start.6 = (bf16[96,512]{1,0:T(8,128)(2,1)S(1)}, bf16[96,512]{1,0:T(8,128)(2,1)S(1)}, u32[]{:S(2)}, u32[]{:S(2)}) collective-permute-start(bf16[96,512]{1,0:T(8,128)(2,1)S(1)} %slice.9), channel_id=1, source_target_pairs={{0,2},{1,3},{2,0},{3,1},{4,6},{5,7},{6,4},{7,5},{8,10},{9,11},{10,... | collective-permute-start | bytes 294920 | tf_op jit(solution)/shard_map/ppermute | solution.py:442
  17.0 3.4 %copy-start.1 = (bf16[192,4096]{1,0:T(8,128)(2,1)S(1)}, bf16[192,4096]{1,0:T(8,128)(2,1)}, u32[]{:S(2)}) copy-start(bf16[192,4096]{1,0:T(8,128)(2,1)} %refs_0_.2) | copy-start | bytes 4718596
  17.0 3.4 %copy-start.2 = (f32[1,1024,512]{2,1,0:T(8,128)S(1)}, f32[1,1024,512]{2,1,0:T(8,128)}, u32[]{:S(2)}) copy-start(f32[1,1024,512]{2,1,0:T(8,128)} %refs_4_.1) | copy-start | bytes 6291460
  17.0 3.4 %copy-start.8 = (bf16[256,256]{1,0:T(8,128)(2,1)S(1)}, bf16[256,256]{1,0:T(8,128)(2,1)}, u32[]{:S(2)}) copy-start(bf16[256,256]{1,0:T(8,128)(2,1)} %constant.31.clone.refs_6_.refs_10_) | copy-start | bytes 393220
  17.0 3.4 %copy-start.9 = (bf16[256,256]{1,0:T(8,128)(2,1)S(1)}, bf16[256,256]{1,0:T(8,128)(2,1)}, u32[]{:S(2)}) copy-start(bf16[256,256]{1,0:T(8,128)(2,1)} %constant.30.clone.refs_5_.refs_9_) | copy-start | bytes 393220
  17.0 13.3 %collective-permute-start.5 = (bf16[96,512]{1,0:T(8,128)(2,1)S(1)}, bf16[96,512]{1,0:T(8,128)(2,1)S(1)}, u32[]{:S(2)}, u32[]{:S(2)}) collective-permute-start(bf16[96,512]{1,0:T(8,128)(2,1)S(1)} %slice.8), channel_id=1, source_target_pairs={{0,1},{1,0},{2,3},{3,2},{4,5},{5,4},{6,7},{7,6},{8,9},{9,8},{10,11... | collective-permute-start | bytes 294920 | tf_op jit(solution)/shard_map/ppermute | solution.py:442
  19.5 10.9 %copy-start.4 = (s32[4,32,512]{2,1,0:T(8,128)S(1)}, s32[4,32,512]{2,1,0:T(8,128)}, u32[]{:S(2)}) copy-start(s32[4,32,512]{2,1,0:T(8,128)} %refs_8_.1) | copy-start | bytes 786436
  19.5 19.6 %collective-permute-start.8 = (bf16[192,1024]{1,0:T(8,128)(2,1)S(1)}, bf16[192,1024]{1,0:T(8,128)(2,1)S(1)}, u32[]{:S(2)}, u32[]{:S(2)}) collective-permute-start(bf16[192,1024]{1,0:T(8,128)(2,1)S(1)} %get-tuple-element.32), channel_id=1, source_target_pairs={{0,1},{1,0},{2,3},{3,2},{4,5},{5,4},{6,7},{7,6},{8,9},{9,8},{10,11... | collective-permute-start | bytes 1179656 | tf_op jit(solution)/shard_map/ppermute | solution.py:442
  28.2 10.8 %collective-permute-start.9 = (bf16[192,1024]{1,0:T(8,128)(2,1)S(1)}, bf16[192,1024]{1,0:T(8,128)(2,1)S(1)}, u32[]{:S(2)}, u32[]{:S(2)}) collective-permute-start(bf16[192,1024]{1,0:T(8,128)(2,1)S(1)} %get-tuple-element.33), channel_id=1, source_target_pairs={{0,2},{1,3},{2,0},{3,1},{4,6},{5,7},{6,4},{7,5},{8,10},{9,11},{10,... | collective-permute-start | bytes 1179656 | tf_op jit(solution)/shard_map/ppermute | solution.py:442
  30.3 9.5 %copy-start.6 = (bf16[256,256]{1,0:T(8,128)(2,1)S(1)}, bf16[256,256]{1,0:T(8,128)(2,1)}, u32[]{:S(2)}) copy-start(bf16[256,256]{1,0:T(8,128)(2,1)} %constant.33.clone.low_ref) | copy-start | bytes 393220
  30.3 9.5 %copy-start.7 = (bf16[256,256]{1,0:T(8,128)(2,1)S(1)}, bf16[256,256]{1,0:T(8,128)(2,1)}, u32[]{:S(2)}) copy-start(bf16[256,256]{1,0:T(8,128)(2,1)} %constant.32.clone.high_ref) | copy-start | bytes 393220
  33.5 1.8 %collective-permute-start.7 = (bf16[4,16,512]{2,1,0:T(8,128)(2,1)S(1)}, bf16[4,16,512]{2,1,0:T(8,128)(2,1)S(1)}, u32[]{:S(2)}, u32[]{:S(2)}) collective-permute-start(bf16[4,16,512]{2,1,0:T(8,128)(2,1)S(1)} %get-tuple-element.39), channel_id=1, source_target_pairs={{0,4},{4,0},{8,12},{12,8},{16,20},{20,16},{24,28},{28,24},{1,5},{5... | collective-permute-start | bytes 196616 | tf_op jit(solution)/shard_map/ppermute | solution.py:442
  33.6 12.9 %collective-permute-start.14 = (bf16[192,1024]{1,0:T(8,128)(2,1)S(1)}, bf16[192,1024]{1,0:T(8,128)(2,1)S(1)}, u32[]{:S(2)}, u32[]{:S(2)}) collective-permute-start(bf16[192,1024]{1,0:T(8,128)(2,1)S(1)} %get-tuple-element.46), channel_id=1, source_target_pairs={{0,3},{1,2},{2,1},{3,0},{4,7},{5,6},{6,5},{7,4},{8,11},{9,10},{10,... | collective-permute-start | bytes 1179656 | tf_op jit(solution)/shard_map/ppermute | solution.py:442
  35.4 7.6 %collective-permute-start.12 = (bf16[4,16,512]{2,1,0:T(8,128)(2,1)S(1)}, bf16[4,16,512]{2,1,0:T(8,128)(2,1)S(1)}, u32[]{:S(2)}, u32[]{:S(2)}) collective-permute-start(bf16[4,16,512]{2,1,0:T(8,128)(2,1)S(1)} %add_convert_fusion.1), channel_id=1, source_target_pairs={{0,24},{4,28},{8,16},{12,20},{16,8},{20,12},{24,0},{28,4},{1,25},{... | collective-permute-start | bytes 196616 | tf_op jit(solution)/shard_map/ppermute | solution.py:442
  39.0 5.9 %collective-permute-start.11 = (bf16[4,16,512]{2,1,0:T(8,128)(2,1)S(1)}, bf16[4,16,512]{2,1,0:T(8,128)(2,1)S(1)}, u32[]{:S(2)}, u32[]{:S(2)}) collective-permute-start(bf16[4,16,512]{2,1,0:T(8,128)(2,1)S(1)} %add_convert_fusion.1), channel_id=1, source_target_pairs={{0,16},{4,20},{8,24},{12,28},{16,0},{20,4},{24,8},{28,12},{1,17},{... | collective-permute-start | bytes 196616 | tf_op jit(solution)/shard_map/ppermute | solution.py:442
  39.0 5.9 %collective-permute-start.10 = (bf16[4,16,512]{2,1,0:T(8,128)(2,1)S(1)}, bf16[4,16,512]{2,1,0:T(8,128)(2,1)S(1)}, u32[]{:S(2)}, u32[]{:S(2)}) collective-permute-start(bf16[4,16,512]{2,1,0:T(8,128)(2,1)S(1)} %add_convert_fusion.1), channel_id=1, source_target_pairs={{0,8},{4,12},{8,0},{12,4},{16,24},{20,28},{24,16},{28,20},{1,9},{5... | collective-permute-start | bytes 196616 | tf_op jit(solution)/shard_map/ppermute | solution.py:442
  45.0 1.5 %collective-permute-start.13 = (bf16[4,16,512]{2,1,0:T(8,128)(2,1)S(1)}, bf16[4,16,512]{2,1,0:T(8,128)(2,1)S(1)}, u32[]{:S(2)}, u32[]{:S(2)}) collective-permute-start(bf16[4,16,512]{2,1,0:T(8,128)(2,1)S(1)} %add_convert_fusion.bands_ref), channel_id=1, source_target_pairs={{0,4},{4,0},{8,12},{12,8},{16,20},{20,16},{24,28},{28,24},{1,5},{5... | collective-permute-start | bytes 196616 | tf_op jit(solution)/shard_map/ppermute | solution.py:442

commit v7 on v5

--- a/solution.py
+++ b/solution.py
@@ -476,6 +476,8 @@
         place, activations, inputs[: late - 1], cotangents[:late], momentum, high, low
     )
     inputs, inverse, early, _ = lax.optimization_barrier((inputs, inverse, early, near))
+    near = list(near)
+    near[1], early = lax.optimization_barrier((near[1], early))
     parts = [near[0]] + [swap(near[m], "fsdp", m) for m in range(1, groups - 1)]
 
     moment, coeffs, mine, theirs, far = moments(

time: 49.3 us -> 49.3 us (level)
  waiting for transfers between devices: 8.29 us -> 8.91 us
  starting transfers between devices: 17.9 us -> 17.3 us
    ppermute x15, waiting for transfers between devices: 8.29 us -> 8.91 us  [swap(): return lax.ppermute(x, axis, [(s, s ^ mask) for s in range(size)])]
    ppermute x15, starting transfers between devices: 17.9 us -> 17.3 us  [swap(): return lax.ppermute(x, axis, [(s, s ^ mask) for s in range(size)])]
where the time goes in v7:
time: 49.3 us; the launch traced here: 49.1 us
  Pallas kernels  19.6 us (40%)
  starting transfers between devices  17.3 us (35%)
  waiting for transfers between devices  8.91 us (18%)
  local copies, waits for them, and re-layouts  2.42 us (5%)
  between operations  0.82 us (2%)
    ppermute x15, starting transfers between devices, swap(): return lax.ppermute(x, axis, [(s, s ^ mask) for s in range(size)])  17.3 us
    ppermute x15, waiting for transfers between devices, swap(): return lax.ppermute(x, axis, [(s, s ^ mask) for s in range(size)])  8.91 us
    pallas_call x1, Pallas kernels, inverse_index(): pl.pallas_call(inverse_index_kernel, out_shape=jax.ShapeDtypeStruct((bloc...  4.52 us
    pallas_call x1, Pallas kernels, moments(): pl.pallas_call(functools.partial(moment_kernel, groups), out_shape=[jax.S...  3.19 us
    pallas_call x1, Pallas kernels, feedback(): pl.pallas_call(functools.partial(feedback_kernel, groups), out_shape=[jax...  3.15 us
    pallas_call x1, Pallas kernels, early_moments(): pl.pallas_call(functools.partial(early_kernel, groups), out_shape=[jax.Sh...  2.75 us
    pallas_call x1, Pallas kernels, decode(): pl.pallas_call(functools.partial(decode_kernel, replicas, groups), out_sh...  2.65 us
    unnamed x22, local copies, waits for them, and re-layouts  2.4 us
  transfers between devices with their start and end apart: 15, of which 4 were waited for; matrix products, arithmetic and copies ran while one was open for 0% of the time, Pallas kernels for 34%

profile of v7, /device:TPU:0, one launch (start us, length us, event | category | flops | bytes accessed | tf_op | source)
XLA Modules:
  0.0 49.1 jit_solution(6874539817350841911)
XLA Ops:
  0.6 3.0 %collective-permute-start.3 = (bf16[192,512]{1,0:T(8,128)(2,1)}, bf16[192,512]{1,0:T(8,128)(2,1)S(1)}, u32[]{:S(2)}, u32[]{:S(2)}) collective-permute-start(bf16[192,512]{1,0:T(8,128)(2,1)} %refs_0_.3), channel_id=1, source_target_pairs={{0,1},{1,0},{2,3},{3,2},{4,5},{5,4},{6,7},{7,6},{8,9},{9,8},{10,11... | collective-permute-start | bytes 589832 | tf_op jit(solution)/shard_map/ppermute | solution.py:435
  3.6 1.5 %collective-permute-start.4 = (bf16[192,512]{1,0:T(8,128)(2,1)}, bf16[192,512]{1,0:T(8,128)(2,1)S(1)}, u32[]{:S(2)}, u32[]{:S(2)}) collective-permute-start(bf16[192,512]{1,0:T(8,128)(2,1)} %refs_0_.3), channel_id=1, source_target_pairs={{0,2},{1,3},{2,0},{3,1},{4,6},{5,7},{6,4},{7,5},{8,10},{9,11},{10,... | collective-permute-start | bytes 589832 | tf_op jit(solution)/shard_map/ppermute | solution.py:435
  5.2 0.1 pad_add_fusion.place_ref
  5.2 0.0 copy-start
  5.2 1.4 %copy-done = bf16[192,4096]{1,0:T(8,128)(2,1)S(1)} copy-done((bf16[192,4096]{1,0:T(8,128)(2,1)S(1)}, bf16[192,4096]{1,0:T(8,128)(2,1)}, u32[]{:S(2)}) %copy-start) | copy-done | bytes 1572888
  6.6 0.0 copy-start.5
  6.6 0.0 copy-start.10
  6.6 0.7 %cut.1 = (bf16[192,1024]{1,0:T(8,128)(2,1)S(1)}, bf16[192,1024]{1,0:T(8,128)(2,1)S(1)}, bf16[192,1024]{1,0:T(8,128)(2,1)S(1)}) custom-call(s32[2]{0:T(128)S(1)} %pad_add_fusion.place_ref, bf16[192,4096]{1,0:T(8,128)(2,1)S(1)} %copy-done), custom_call_target="tpu_custom_call" | custom-call | bytes 2359296 | tf_op jit(solution)/shard_map/cut/pallas_call | solution.py:101
  7.3 0.6 %collective-permute-start = (bf16[192,1024]{1,0:T(8,128)(2,1)S(1)}, bf16[192,1024]{1,0:T(8,128)(2,1)S(1)}, u32[]{:S(2)}, u32[]{:S(2)}) collective-permute-start(bf16[192,1024]{1,0:T(8,128)(2,1)S(1)} %get-tuple-element.29), channel_id=1, source_target_pairs={{0,1},{1,0},{2,3},{3,2},{4,5},{5,4},{6,7},{7,6},{8,9},{9,8},{10,11... | collective-permute-start | bytes 1179656 | tf_op jit(solution)/shard_map/ppermute | solution.py:435
  7.9 0.1 collective-permute-start.1
  8.0 2.9 %collective-permute-start.2 = (bf16[192,1024]{1,0:T(8,128)(2,1)S(1)}, bf16[192,1024]{1,0:T(8,128)(2,1)S(1)}, u32[]{:S(2)}, u32[]{:S(2)}) collective-permute-start(bf16[192,1024]{1,0:T(8,128)(2,1)S(1)} %get-tuple-element.31), channel_id=1, source_target_pairs={{0,3},{1,2},{2,1},{3,0},{4,7},{5,6},{6,5},{7,4},{8,11},{9,10},{10,... | collective-permute-start | bytes 1179656 | tf_op jit(solution)/shard_map/ppermute | solution.py:435
  10.9 0.0 copy-start.3
  10.9 0.9 %copy-done.3 = s32[4,32,512]{2,1,0:T(8,128)S(1)} copy-done((s32[4,32,512]{2,1,0:T(8,128)S(1)}, s32[4,32,512]{2,1,0:T(8,128)}, u32[]{:S(2)}) %copy-start.3) | copy-done | bytes 262168
  11.8 4.5 %inverse_index.1.inverse_ref = s32[4,256,512]{2,1,0:T(8,128)S(1)} custom-call(s32[4,32,512]{2,1,0:T(8,128)S(1)} %copy-done.3), custom_call_target="tpu_custom_call" | custom-call | flops 33554432 | bytes 2097152 | tf_op jit(solution)/shard_map/inverse_index/pallas_call | solution.py:68
  16.4 0.0 collective-permute-done.3.refs_3_.refs_1_
  16.4 0.6 %collective-permute-start.6 = (bf16[96,512]{1,0:T(8,128)(2,1)S(1)}, bf16[96,512]{1,0:T(8,128)(2,1)S(1)}, u32[]{:S(2)}, u32[]{:S(2)}) collective-permute-start(bf16[96,512]{1,0:T(8,128)(2,1)S(1)} %slice.9), channel_id=1, source_target_pairs={{0,2},{1,3},{2,0},{3,1},{4,6},{5,7},{6,4},{7,5},{8,10},{9,11},{10,... | collective-permute-start | bytes 294920 | tf_op jit(solution)/shard_map/ppermute | solution.py:435
  17.0 0.0 collective-permute-done.4.refs_2_
  17.0 0.0 copy-start.1
  17.0 0.0 copy-start.2
  17.0 0.0 copy-start.8
  17.0 0.0 copy-start.9
  17.0 0.1 collective-permute-start.5
  17.2 0.0 copy-done.5
  17.2 0.0 copy-done.10
  17.2 1.2 %input_gradients.1 = (bf16[192,1024]{1,0:T(8,128)(2,1)S(1)}, bf16[192,1024]{1,0:T(8,128)(2,1)S(1)}, bf16[192,1024]{1,0:T(8,128)(2,1)S(1)}) custom-call(bf16[192,512]{1,0:T(8,128)(2,1)S(1)} %copy-done.10, bf16[192,512]{1,0:T(8,128)(2,1)S(1)} %collective-permute-done.3.refs_3_.refs_1_, bf16[192,512]{1,0:T(8,128)(2,1)S(1)} %collective-permute-done.4.refs_2_, ...), custom_call_target="tpu_custom_call" | custom-call | flops 12079595520 | bytes 2818048 | tf_op jit(solution)/shard_map/input_gradients/pallas_call | solution.py:134
  18.4 1.1 %collective-permute-done.refs_1_ = bf16[192,1024]{1,0:T(8,128)(2,1)S(1)} collective-permute-done((bf16[192,1024]{1,0:T(8,128)(2,1)S(1)}, bf16[192,1024]{1,0:T(8,128)(2,1)S(1)}, u32[]{:S(2)}, u32[]{:S(2)}) %collective-permute-start) | collective-permute-done | bytes 393248 | tf_op jit(solution)/shard_map/ppermute | solution.py:435
  19.5 0.0 copy-start.4
  19.5 1.0 %collective-permute-start.9 = (bf16[192,1024]{1,0:T(8,128)(2,1)S(1)}, bf16[192,1024]{1,0:T(8,128)(2,1)S(1)}, u32[]{:S(2)}, u32[]{:S(2)}) collective-permute-start(bf16[192,1024]{1,0:T(8,128)(2,1)S(1)} %get-tuple-element.35), channel_id=1, source_target_pairs={{0,2},{1,3},{2,0},{3,1},{4,6},{5,7},{6,4},{7,5},{8,10},{9,11},{10,... | collective-permute-start | bytes 1179656 | tf_op jit(solution)/shard_map/ppermute | solution.py:435
  20.5 0.0 copy-done.1
  20.5 0.0 copy-done.2
  20.5 0.0 copy-done.8
  20.5 0.0 copy-done.9
  20.5 2.7 %early_moment.1 = (f32[1024,512]{1,0:T(8,128)S(1)}, f32[1024,512]{1,0:T(8,128)S(1)}) custom-call(s32[2]{0:T(128)S(1)} %pad_add_fusion.place_ref, bf16[192,4096]{1,0:T(8,128)(2,1)S(1)} %copy-done.1, bf16[192,1024]{1,0:T(8,128)(2,1)S(1)} %collective-permute-done.refs_1_, bf16[192,512]{1,0:T(8,128)(2,1)S(1)} %copy-done.10, ...), custom_call_target="tpu_custom_call" | custom-call | flops 1207959552 | bytes 7077888 | tf_op jit(solution)/shard_map/early_moment/pallas_call | solution.py:174
  23.2 5.0 %collective-permute-done.1.refs_0_ = bf16[192,1024]{1,0:T(8,128)(2,1)S(1)} collective-permute-done((bf16[192,1024]{1,0:T(8,128)(2,1)S(1)}, bf16[192,1024]{1,0:T(8,128)(2,1)S(1)}, u32[]{:S(2)}, u32[]{:S(2)}) %collective-permute-start.1) | collective-permute-done | bytes 393248 | tf_op jit(solution)/shard_map/ppermute | solution.py:435
  28.2 0.0 collective-permute-done.2.refs_1_
  28.2 1.2 %collective-permute-start.8 = (bf16[192,1024]{1,0:T(8,128)(2,1)S(1)}, bf16[192,1024]{1,0:T(8,128)(2,1)S(1)}, u32[]{:S(2)}, u32[]{:S(2)}) collective-permute-start(bf16[192,1024]{1,0:T(8,128)(2,1)S(1)} %get-tuple-element.43), channel_id=1, source_target_pairs={{0,1},{1,0},{2,3},{3,2},{4,5},{5,4},{6,7},{7,6},{8,9},{9,8},{10,11... | collective-permute-start | bytes 1179656 | tf_op jit(solution)/shard_map/ppermute | solution.py:435
  29.4 0.9 %collective-permute-done.6.refs_4_ = bf16[96,512]{1,0:T(8,128)(2,1)S(1)} collective-permute-done((bf16[96,512]{1,0:T(8,128)(2,1)S(1)}, bf16[96,512]{1,0:T(8,128)(2,1)S(1)}, u32[]{:S(2)}, u32[]{:S(2)}) %collective-permute-start.6) | collective-permute-done | bytes 98336 | tf_op jit(solution)/shard_map/ppermute | solution.py:435
  30.3 0.0 collective-permute-done.5.refs_3_
  30.3 0.0 copy-done.4
  30.3 0.0 copy-start.6
  30.3 0.0 copy-start.7
  30.3 3.2 %moment.1 = (f32[1024,512]{1,0:T(8,128)S(1)}, f32[1024,512]{1,0:T(8,128)S(1)}, bf16[4,16,512]{2,1,0:T(8,128)(2,1)S(1)}, bf16[4,16,512]{2,1,0:T(8,128)(2,1)S(1)}, bf16[192,1024]{1,0:T(8,128)(2,1)S(1)}) custom-call(s32[2]{0:T(128)S(1)} %pad_add_fusion.place_ref, bf16[192,1024]{1,0:T(8,128)(2,1)S(1)} %collective-permute-done.1.refs_0_, ...), custom_call_target="tpu_custom_call" | custom-call | flops 1207959552 | bytes 8126464 | tf_op jit(solution)/shard_map/moment/pallas_call | solution.py:252
  33.5 0.1 collective-permute-start.7
  33.6 1.7 %collective-permute-start.14 = (bf16[192,1024]{1,0:T(8,128)(2,1)S(1)}, bf16[192,1024]{1,0:T(8,128)(2,1)S(1)}, u32[]{:S(2)}, u32[]{:S(2)}) collective-permute-start(bf16[192,1024]{1,0:T(8,128)(2,1)S(1)} %get-tuple-element.50), channel_id=1, source_target_pairs={{0,3},{1,2},{2,1},{3,0},{4,7},{5,6},{6,5},{7,4},{8,11},{9,10},{10,... | collective-permute-start | bytes 1179656 | tf_op jit(solution)/shard_map/ppermute | solution.py:435
  35.3 0.0 collective-permute-done.7
  35.4 3.7 %collective-permute-start.12 = (bf16[4,16,512]{2,1,0:T(8,128)(2,1)S(1)}, bf16[4,16,512]{2,1,0:T(8,128)(2,1)S(1)}, u32[]{:S(2)}, u32[]{:S(2)}) collective-permute-start(bf16[4,16,512]{2,1,0:T(8,128)(2,1)S(1)} %add_convert_fusion.1), channel_id=1, source_target_pairs={{0,24},{4,28},{8,16},{12,20},{16,8},{20,12},{24,0},{28,4},{1,25},{... | collective-permute-start | bytes 196616 | tf_op jit(solution)/shard_map/ppermute | solution.py:435
  39.0 0.0 collective-permute-start.11
  39.0 0.0 collective-permute-done.9.refs_2_
  39.0 0.0 collective-permute-done.8.refs_1_
  39.0 0.8 %collective-permute-start.10 = (bf16[4,16,512]{2,1,0:T(8,128)(2,1)S(1)}, bf16[4,16,512]{2,1,0:T(8,128)(2,1)S(1)}, u32[]{:S(2)}, u32[]{:S(2)}) collective-permute-start(bf16[4,16,512]{2,1,0:T(8,128)(2,1)S(1)} %add_convert_fusion.1), channel_id=1, source_target_pairs={{0,8},{4,12},{8,0},{12,4},{16,24},{20,28},{24,16},{28,20},{1,9},{5... | collective-permute-start | bytes 196616 | tf_op jit(solution)/shard_map/ppermute | solution.py:435
  39.8 0.0 copy-done.6
  39.8 0.0 copy-done.7
  39.8 3.2 %feedback.1 = (f32[1,1024,512]{2,1,0:T(8,128)}, bf16[192,4096]{1,0:T(8,128)(2,1)}) custom-call(s32[2]{0:T(128)S(1)} %pad_add_fusion.place_ref, f32[1024,512]{1,0:T(8,128)S(1)} %get-tuple-element.45.moment_ref, f32[1024,512]{1,0:T(8,128)S(1)} %get-tuple-element.46.coeffs_ref, s32[4,256,512]{2,1,0:T(8,128)S(1)} %inverse_index.1.inverse_ref, ...), custom_call_target="tpu_custom_call" | custom-call | flops 805306368 | bytes 10747904 | tf_op jit(solution)/shard_map/feedback/pallas_call | solution.py:301
  43.0 0.0 collective-permute-done.12
  43.0 1.9 %collective-permute-done.11 = bf16[4,16,512]{2,1,0:T(8,128)(2,1)S(1)} collective-permute-done((bf16[4,16,512]{2,1,0:T(8,128)(2,1)S(1)}, bf16[4,16,512]{2,1,0:T(8,128)(2,1)S(1)}, u32[]{:S(2)}, u32[]{:S(2)}) %collective-permute-start.11) | collective-permute-done | bytes 65568 | tf_op jit(solution)/shard_map/ppermute | solution.py:435
  44.9 0.0 collective-permute-done.10
  45.0 0.1 collective-permute-start.13
  45.0 1.4 %place_own.1.own_ref = f32[4,256,512]{2,1,0:T(8,128)S(1)} custom-call(s32[2]{0:T(128)S(1)} %pad_add_fusion.place_ref, bf16[4,16,512]{2,1,0:T(8,128)(2,1)S(1)} %add_convert_fusion.bands_ref, s32[4,256,512]{2,1,0:T(8,128)S(1)} %inverse_index.1.inverse_ref), custom_call_target="tpu_custom_call" | custom-call | flops 4194304 | bytes 4194304 | tf_op jit(solution)/shard_map/place_own/pallas_call | solution.py:350
  46.5 0.0 collective-permute-done.14.part_ref
  46.5 0.0 collective-permute-done.13.theirs_ref
  46.5 2.6 %decode.1 = (bf16[1024,512]{1,0:T(8,128)(2,1)}, bf16[192,4096]{1,0:T(8,128)(2,1)}) custom-call(s32[2]{0:T(128)S(1)} %pad_add_fusion.place_ref, f32[4,256,512]{2,1,0:T(8,128)S(1)} %place_own.1.own_ref, bf16[4,16,512]{2,1,0:T(8,128)(2,1)S(1)} %collective-permute-done.13.theirs_ref, ...), custom_call_target="tpu_custom_call", output_to_operand_aliasing={{1}: (7, {})} | custom-call | flops 805306368 | bytes 3932160 | tf_op jit(solution)/shard_map/decode/pallas_call | solution.py:406
  (4 shorter events, 0.1 us)
Async XLA Ops:
  0.6 15.7 %collective-permute-start.3 = (bf16[192,512]{1,0:T(8,128)(2,1)}, bf16[192,512]{1,0:T(8,128)(2,1)S(1)}, u32[]{:S(2)}, u32[]{:S(2)}) collective-permute-start(bf16[192,512]{1,0:T(8,128)(2,1)} %refs_0_.3), channel_id=1, source_target_pairs={{0,1},{1,0},{2,3},{3,2},{4,5},{5,4},{6,7},{7,6},{8,9},{9,8},{10,11... | collective-permute-start | bytes 589832 | tf_op jit(solution)/shard_map/ppermute | solution.py:435
  3.6 13.3 %collective-permute-start.4 = (bf16[192,512]{1,0:T(8,128)(2,1)}, bf16[192,512]{1,0:T(8,128)(2,1)S(1)}, u32[]{:S(2)}, u32[]{:S(2)}) collective-permute-start(bf16[192,512]{1,0:T(8,128)(2,1)} %refs_0_.3), channel_id=1, source_target_pairs={{0,2},{1,3},{2,0},{3,1},{4,6},{5,7},{6,4},{7,5},{8,10},{9,11},{10,... | collective-permute-start | bytes 589832 | tf_op jit(solution)/shard_map/ppermute | solution.py:435
  5.2 1.4 %copy-start = (bf16[192,4096]{1,0:T(8,128)(2,1)S(1)}, bf16[192,4096]{1,0:T(8,128)(2,1)}, u32[]{:S(2)}) copy-start(bf16[192,4096]{1,0:T(8,128)(2,1)} %refs_0_.2) | copy-start | bytes 4718596
  6.6 10.5 %copy-start.5 = (bf16[1024,512]{1,0:T(8,128)(2,1)S(1)}, bf16[1024,512]{1,0:T(8,128)(2,1)}, u32[]{:S(2)}) copy-start(bf16[1024,512]{1,0:T(8,128)(2,1)} %refs_5_.2) | copy-start | bytes 3145732
  6.6 10.6 %copy-start.10 = (bf16[192,512]{1,0:T(8,128)(2,1)S(1)}, bf16[192,512]{1,0:T(8,128)(2,1)}, u32[]{:S(2)}) copy-start(bf16[192,512]{1,0:T(8,128)(2,1)} %refs_0_.3) | copy-start | bytes 589828
  7.3 12.1 %collective-permute-start = (bf16[192,1024]{1,0:T(8,128)(2,1)S(1)}, bf16[192,1024]{1,0:T(8,128)(2,1)S(1)}, u32[]{:S(2)}, u32[]{:S(2)}) collective-permute-start(bf16[192,1024]{1,0:T(8,128)(2,1)S(1)} %get-tuple-element.29), channel_id=1, source_target_pairs={{0,1},{1,0},{2,3},{3,2},{4,5},{5,4},{6,7},{7,6},{8,9},{9,8},{10,11... | collective-permute-start | bytes 1179656 | tf_op jit(solution)/shard_map/ppermute | solution.py:435
  7.9 20.3 %collective-permute-start.1 = (bf16[192,1024]{1,0:T(8,128)(2,1)S(1)}, bf16[192,1024]{1,0:T(8,128)(2,1)S(1)}, u32[]{:S(2)}, u32[]{:S(2)}) collective-permute-start(bf16[192,1024]{1,0:T(8,128)(2,1)S(1)} %get-tuple-element.30), channel_id=1, source_target_pairs={{0,2},{1,3},{2,0},{3,1},{4,6},{5,7},{6,4},{7,5},{8,10},{9,11},{10,... | collective-permute-start | bytes 1179656 | tf_op jit(solution)/shard_map/ppermute | solution.py:435
  8.0 20.2 %collective-permute-start.2 = (bf16[192,1024]{1,0:T(8,128)(2,1)S(1)}, bf16[192,1024]{1,0:T(8,128)(2,1)S(1)}, u32[]{:S(2)}, u32[]{:S(2)}) collective-permute-start(bf16[192,1024]{1,0:T(8,128)(2,1)S(1)} %get-tuple-element.31), channel_id=1, source_target_pairs={{0,3},{1,2},{2,1},{3,0},{4,7},{5,6},{6,5},{7,4},{8,11},{9,10},{10,... | collective-permute-start | bytes 1179656 | tf_op jit(solution)/shard_map/ppermute | solution.py:435
  10.9 0.9 %copy-start.3 = (s32[4,32,512]{2,1,0:T(8,128)S(1)}, s32[4,32,512]{2,1,0:T(8,128)}, u32[]{:S(2)}) copy-start(s32[4,32,512]{2,1,0:T(8,128)} %refs_8_.1) | copy-start | bytes 786436
  16.4 13.9 %collective-permute-start.6 = (bf16[96,512]{1,0:T(8,128)(2,1)S(1)}, bf16[96,512]{1,0:T(8,128)(2,1)S(1)}, u32[]{:S(2)}, u32[]{:S(2)}) collective-permute-start(bf16[96,512]{1,0:T(8,128)(2,1)S(1)} %slice.9), channel_id=1, source_target_pairs={{0,2},{1,3},{2,0},{3,1},{4,6},{5,7},{6,4},{7,5},{8,10},{9,11},{10,... | collective-permute-start | bytes 294920 | tf_op jit(solution)/shard_map/ppermute | solution.py:435
  17.0 3.5 %copy-start.1 = (bf16[192,4096]{1,0:T(8,128)(2,1)S(1)}, bf16[192,4096]{1,0:T(8,128)(2,1)}, u32[]{:S(2)}) copy-start(bf16[192,4096]{1,0:T(8,128)(2,1)} %refs_0_.2) | copy-start | bytes 4718596
  17.0 3.5 %copy-start.2 = (f32[1,1024,512]{2,1,0:T(8,128)S(1)}, f32[1,1024,512]{2,1,0:T(8,128)}, u32[]{:S(2)}) copy-start(f32[1,1024,512]{2,1,0:T(8,128)} %refs_4_.1) | copy-start | bytes 6291460
  17.0 3.4 %copy-start.8 = (bf16[256,256]{1,0:T(8,128)(2,1)S(1)}, bf16[256,256]{1,0:T(8,128)(2,1)}, u32[]{:S(2)}) copy-start(bf16[256,256]{1,0:T(8,128)(2,1)} %constant.31.clone.refs_6_.refs_10_) | copy-start | bytes 393220
  17.0 3.4 %copy-start.9 = (bf16[256,256]{1,0:T(8,128)(2,1)S(1)}, bf16[256,256]{1,0:T(8,128)(2,1)}, u32[]{:S(2)}) copy-start(bf16[256,256]{1,0:T(8,128)(2,1)} %constant.30.clone.refs_5_.refs_9_) | copy-start | bytes 393220
  17.0 13.3 %collective-permute-start.5 = (bf16[96,512]{1,0:T(8,128)(2,1)S(1)}, bf16[96,512]{1,0:T(8,128)(2,1)S(1)}, u32[]{:S(2)}, u32[]{:S(2)}) collective-permute-start(bf16[96,512]{1,0:T(8,128)(2,1)S(1)} %slice.8), channel_id=1, source_target_pairs={{0,1},{1,0},{2,3},{3,2},{4,5},{5,4},{6,7},{7,6},{8,9},{9,8},{10,11... | collective-permute-start | bytes 294920 | tf_op jit(solution)/shard_map/ppermute | solution.py:435
  19.5 10.9 %copy-start.4 = (s32[4,32,512]{2,1,0:T(8,128)S(1)}, s32[4,32,512]{2,1,0:T(8,128)}, u32[]{:S(2)}) copy-start(s32[4,32,512]{2,1,0:T(8,128)} %refs_8_.1) | copy-start | bytes 786436
  19.5 19.6 %collective-permute-start.9 = (bf16[192,1024]{1,0:T(8,128)(2,1)S(1)}, bf16[192,1024]{1,0:T(8,128)(2,1)S(1)}, u32[]{:S(2)}, u32[]{:S(2)}) collective-permute-start(bf16[192,1024]{1,0:T(8,128)(2,1)S(1)} %get-tuple-element.35), channel_id=1, source_target_pairs={{0,2},{1,3},{2,0},{3,1},{4,6},{5,7},{6,4},{7,5},{8,10},{9,11},{10,... | collective-permute-start | bytes 1179656 | tf_op jit(solution)/shard_map/ppermute | solution.py:435
  28.2 10.8 %collective-permute-start.8 = (bf16[192,1024]{1,0:T(8,128)(2,1)S(1)}, bf16[192,1024]{1,0:T(8,128)(2,1)S(1)}, u32[]{:S(2)}, u32[]{:S(2)}) collective-permute-start(bf16[192,1024]{1,0:T(8,128)(2,1)S(1)} %get-tuple-element.43), channel_id=1, source_target_pairs={{0,1},{1,0},{2,3},{3,2},{4,5},{5,4},{6,7},{7,6},{8,9},{9,8},{10,11... | collective-permute-start | bytes 1179656 | tf_op jit(solution)/shard_map/ppermute | solution.py:435
  30.3 9.5 %copy-start.6 = (bf16[256,256]{1,0:T(8,128)(2,1)S(1)}, bf16[256,256]{1,0:T(8,128)(2,1)}, u32[]{:S(2)}) copy-start(bf16[256,256]{1,0:T(8,128)(2,1)} %constant.33.clone.low_ref) | copy-start | bytes 393220
  30.3 9.5 %copy-start.7 = (bf16[256,256]{1,0:T(8,128)(2,1)S(1)}, bf16[256,256]{1,0:T(8,128)(2,1)}, u32[]{:S(2)}) copy-start(bf16[256,256]{1,0:T(8,128)(2,1)} %constant.32.clone.high_ref) | copy-start | bytes 393220
  33.5 1.8 %collective-permute-start.7 = (bf16[4,16,512]{2,1,0:T(8,128)(2,1)S(1)}, bf16[4,16,512]{2,1,0:T(8,128)(2,1)S(1)}, u32[]{:S(2)}, u32[]{:S(2)}) collective-permute-start(bf16[4,16,512]{2,1,0:T(8,128)(2,1)S(1)} %get-tuple-element.42), channel_id=1, source_target_pairs={{0,4},{4,0},{8,12},{12,8},{16,20},{20,16},{24,28},{28,24},{1,5},{5... | collective-permute-start | bytes 196616 | tf_op jit(solution)/shard_map/ppermute | solution.py:435
  33.6 12.9 %collective-permute-start.14 = (bf16[192,1024]{1,0:T(8,128)(2,1)S(1)}, bf16[192,1024]{1,0:T(8,128)(2,1)S(1)}, u32[]{:S(2)}, u32[]{:S(2)}) collective-permute-start(bf16[192,1024]{1,0:T(8,128)(2,1)S(1)} %get-tuple-element.50), channel_id=1, source_target_pairs={{0,3},{1,2},{2,1},{3,0},{4,7},{5,6},{6,5},{7,4},{8,11},{9,10},{10,... | collective-permute-start | bytes 1179656 | tf_op jit(solution)/shard_map/ppermute | solution.py:435
  35.4 7.6 %collective-permute-start.12 = (bf16[4,16,512]{2,1,0:T(8,128)(2,1)S(1)}, bf16[4,16,512]{2,1,0:T(8,128)(2,1)S(1)}, u32[]{:S(2)}, u32[]{:S(2)}) collective-permute-start(bf16[4,16,512]{2,1,0:T(8,128)(2,1)S(1)} %add_convert_fusion.1), channel_id=1, source_target_pairs={{0,24},{4,28},{8,16},{12,20},{16,8},{20,12},{24,0},{28,4},{1,25},{... | collective-permute-start | bytes 196616 | tf_op jit(solution)/shard_map/ppermute | solution.py:435
  39.0 5.9 %collective-permute-start.11 = (bf16[4,16,512]{2,1,0:T(8,128)(2,1)S(1)}, bf16[4,16,512]{2,1,0:T(8,128)(2,1)S(1)}, u32[]{:S(2)}, u32[]{:S(2)}) collective-permute-start(bf16[4,16,512]{2,1,0:T(8,128)(2,1)S(1)} %add_convert_fusion.1), channel_id=1, source_target_pairs={{0,16},{4,20},{8,24},{12,28},{16,0},{20,4},{24,8},{28,12},{1,17},{... | collective-permute-start | bytes 196616 | tf_op jit(solution)/shard_map/ppermute | solution.py:435
  39.0 5.9 %collective-permute-start.10 = (bf16[4,16,512]{2,1,0:T(8,128)(2,1)S(1)}, bf16[4,16,512]{2,1,0:T(8,128)(2,1)S(1)}, u32[]{:S(2)}, u32[]{:S(2)}) collective-permute-start(bf16[4,16,512]{2,1,0:T(8,128)(2,1)S(1)} %add_convert_fusion.1), channel_id=1, source_target_pairs={{0,8},{4,12},{8,0},{12,4},{16,24},{20,28},{24,16},{28,20},{1,9},{5... | collective-permute-start | bytes 196616 | tf_op jit(solution)/shard_map/ppermute | solution.py:435
  45.0 1.5 %collective-permute-start.13 = (bf16[4,16,512]{2,1,0:T(8,128)(2,1)S(1)}, bf16[4,16,512]{2,1,0:T(8,128)(2,1)S(1)}, u32[]{:S(2)}, u32[]{:S(2)}) collective-permute-start(bf16[4,16,512]{2,1,0:T(8,128)(2,1)S(1)} %add_convert_fusion.bands_ref), channel_id=1, source_target_pairs={{0,4},{4,0},{8,12},{12,8},{16,20},{20,16},{24,28},{28,24},{1,5},{5... | collective-permute-start | bytes 196616 | tf_op jit(solution)/shard_map/ppermute | solution.py:435
